TPU v7x, 32 devices: a whole 2x2x4 slice. The times are simulated.
32 devices in a mesh: dp: 16 (over z, y, x), tensor: 2 (over core).
Axes of the slice: x: 2, y: 2, z: 4, core: 2. Of those that a mesh axis runs over, the one named last changes fastest.
Arguments:
- tokens: bfloat16 [3152, 768], P('dp')
- grad_out: bfloat16 [3152, 768], P('dp'), may hold values from -6 to 6
- valid_mask: int32 [3152], P('dp'), may hold values from 0 to 1, as said below
- routes: int32 [3152, 2], P('dp'), may hold values from 0 to 15, as said below
- slot_index: int32 [3152, 2], P('dp'), may hold values from 0 to 36, as said below
- ln1_gain: float32 [768], replicated, may hold values from 0.5 to 1.5
- ln1_bias: float32 [768], replicated, may hold values from -1 to 1
- w_qkv: bfloat16 [768, 3, 768], P(None, None, 'tensor'), may hold values from -0.21875 to 0.21875
- bias_qv: float32 [2, 768], P(None, 'tensor'), may hold values from -1 to 1
- w_attn_out: bfloat16 [768, 768], P('tensor'), may hold values from -1.75 to 1.75
- b_attn_out: float32 [768], replicated, may hold values from -1 to 1
- ln2_gain: float32 [768], replicated, may hold values from 0.5 to 1.5
- ln2_bias: float32 [768], replicated, may hold values from -1 to 1
- router: bfloat16 [768, 16], replicated, may hold values from -0.15625 to 0.15625
- w_expert_in: bfloat16 [16, 768, 3072], P('dp', None, 'tensor'), may hold values from -0.21875 to 0.21875
- b_expert_in: float32 [16, 3072], P('dp', 'tensor'), may hold values from -1 to 1
- w_expert_out: bfloat16 [16, 3072, 768], P('dp', 'tensor'), may hold values from -0.15625 to 0.15625
- b_expert_out: float32 [16, 768], P('dp'), may hold values from -1 to 1
Outputs:
- out_tokens: bfloat16 [3152, 768], P('dp')
- grad_tokens: float32 [3152, 768], P('dp')
- grad_ln1_gain: float32 [768], replicated
- grad_ln1_bias: float32 [768], replicated
- grad_w_qkv: float32 [768, 3, 768], P(None, None, 'tensor')
- grad_bias_qv: float32 [2, 768], P(None, 'tensor')
- grad_w_attn_out: float32 [768, 768], P('tensor')
- grad_b_attn_out: float32 [768], replicated
- grad_ln2_gain: float32 [768], replicated
- grad_ln2_bias: float32 [768], replicated
- grad_router: float32 [768, 16], replicated
- grad_w_expert_in: float32 [16, 768, 3072], P('dp', None, 'tensor')
- grad_b_expert_in: float32 [16, 3072], P('dp', 'tensor')
- grad_w_expert_out: float32 [16, 3072, 768], P('dp', 'tensor')
- grad_b_expert_out: float32 [16, 768], P('dp')
- rms_values: float32 [4], replicated
Inputs may be any that keep to these rules, and one draw needn't show every extreme that they name: `routes`: each token names two different experts. `slot_index`: 36 means that the route is not sent. Among the tokens of one index of dp, the sent routes of one expert take distinct slots, given in token order until 36 is reached; routes of tokens with valid_mask 0 are never sent; on every index of dp some expert has all 36 slots taken. `valid_mask`: the first token of every image is valid.
All inputs are finite; a program needn't handle non-finite values.
Results may differ from a plain program's by a relative error of at most 0.013.
Values may be sent and summed in bfloat16 or wider, within the bound.
A program may use at most 128 MiB of HBM per device.

v0:
```python
import math

import jax
import jax.numpy as jnp
from jax import lax
from jax.sharding import PartitionSpec as P

HEAD = 64
SEQ = 197


HIGHEST = lax.Precision.HIGHEST


def norm_forward(values, gain_vec, shift_vec):
    center = values - jnp.mean(values, axis=-1, keepdims=True)
    inverse = lax.rsqrt(jnp.mean(center * center, axis=-1, keepdims=True) + 1e-06)
    normal = center * inverse
    return (normal * gain_vec + shift_vec, normal, inverse)


def norm_backward(incoming, normal, inverse, gain_vec):
    scaled = incoming * gain_vec
    back_grad = inverse * (
        scaled
        - jnp.mean(scaled, axis=-1, keepdims=True)
        - normal * jnp.mean(scaled * normal, axis=-1, keepdims=True)
    )
    return (back_grad, jnp.sum(incoming * normal, axis=0), jnp.sum(incoming, axis=0))


def masked_scores(queries, keys_img, key_keep, score_scale):
    scores = (
        jnp.einsum("iqhd,ikhd->ihqk", queries, keys_img, preferred_element_type=jnp.float32)
        * score_scale
    )
    return jnp.where(key_keep, scores, -1000000000.0)


def to_experts(buffer):
    result = lax.all_to_all(buffer, "dp", split_axis=0, concat_axis=0, tiled=True)
    return result


def from_experts(partial_rows, shift_vec):
    summed = lax.psum(partial_rows, "tensor")
    result = lax.all_to_all(
        (summed + shift_vec).astype(jnp.bfloat16), "dp", split_axis=0, concat_axis=0, tiled=True
    )
    return result


def per_device(
    tokens,
    grad_out,
    valid_mask,
    routes,
    slot_index,
    ln1_gain,
    ln1_bias,
    w_qkv,
    bias_qv,
    w_attn_out,
    b_attn_out,
    ln2_gain,
    ln2_bias,
    router,
    w_expert_in,
    b_expert_in,
    w_expert_out,
    b_expert_out,
):
    tok_rows, model_width = tokens.shape
    images = tok_rows // SEQ
    local_width = w_qkv.shape[2]
    local_heads = local_width // HEAD
    experts = router.shape[1]
    capacity = 2 * (3 * tok_rows // (2 * lax.axis_size("dp")))
    score_scale = 1.0 / math.sqrt(HEAD)
    keep_flags = valid_mask.astype(jnp.float32)
    stream = tokens.astype(jnp.float32)
    normed_one, normal_one, inverse_one = norm_forward(stream, ln1_gain, ln1_bias)
    normed_one_low = normed_one.astype(jnp.bfloat16)
    bias_full = jnp.stack([bias_qv[0], jnp.zeros_like(bias_qv[0]), bias_qv[1]], axis=0)
    projected = (
        jnp.einsum("td,dcf->tcf", normed_one_low, w_qkv, preferred_element_type=jnp.float32)
        + bias_full
    )
    projected_low = projected.astype(jnp.bfloat16).reshape(images, SEQ, 3, local_heads, HEAD)
    queries = projected_low[:, :, 0]
    keys_img = projected_low[:, :, 1]
    values_img = projected_low[:, :, 2]
    key_keep = valid_mask.reshape(images, 1, 1, SEQ) > 0
    scores = masked_scores(queries, keys_img, key_keep, score_scale)
    top_score = jnp.max(scores, axis=-1, keepdims=True)
    weights = jnp.exp(scores - top_score)
    row_total = jnp.sum(weights, axis=-1, keepdims=True)
    attn_probs = weights / row_total
    mixed_heads = jnp.einsum(
        "ihqk,ikhd->iqhd",
        attn_probs.astype(jnp.bfloat16),
        values_img,
        preferred_element_type=jnp.float32,
    )
    mixed_low = mixed_heads.astype(jnp.bfloat16).reshape(tok_rows, local_width)
    attn_part = jnp.dot(mixed_low, w_attn_out, preferred_element_type=jnp.float32)
    attention = lax.psum(attn_part, "tensor") + b_attn_out
    middle = stream + attention
    normed_two, normal_two, inverse_two = norm_forward(middle, ln2_gain, ln2_bias)
    normed_two_low = normed_two.astype(jnp.bfloat16)
    logits = jnp.dot(normed_two_low, router, preferred_element_type=jnp.float32)
    picked = routes[:, :, None] == jnp.arange(experts, dtype=jnp.int32)[None, None, :]
    chosen = jnp.sum(jnp.where(picked, logits[:, None, :], 0.0), axis=-1)
    gate_values = jax.nn.softmax(chosen, axis=-1)
    target = jnp.where(
        slot_index < capacity, routes * capacity + slot_index, experts * capacity
    ).reshape(-1)

    def place_rows(slot_rows):
        buffer = (
            jnp.zeros((experts * capacity + 1, model_width), jnp.bfloat16).at[target].set(slot_rows)
        )
        return buffer[:-1].reshape(experts, capacity, model_width)

    def take_rows(buffer):
        flat_rows = jnp.concatenate(
            [
                buffer.reshape(experts * capacity, model_width),
                jnp.zeros((1, model_width), buffer.dtype),
            ],
            axis=0,
        )
        return flat_rows[target].reshape(tok_rows, 2, model_width)

    slot_input = to_experts(place_rows(jnp.repeat(normed_two_low, 2, axis=0))).reshape(
        -1, model_width
    )
    pre_act = (
        jnp.dot(slot_input, w_expert_in[0], preferred_element_type=jnp.float32) + b_expert_in[0]
    )
    hidden_low = jax.nn.gelu(pre_act).astype(jnp.bfloat16)
    expert_part = jnp.dot(hidden_low, w_expert_out[0], preferred_element_type=jnp.float32).reshape(
        -1, capacity, model_width
    )
    returned = from_experts(expert_part, b_expert_out[0])
    arrived_rows = take_rows(returned).astype(jnp.float32)
    branch = jnp.sum(gate_values[:, :, None] * arrived_rows, axis=1)
    output = middle + branch
    keep_col = keep_flags[:, None]
    stat_local = jnp.stack(
        [
            jnp.sum(keep_col * stream * stream),
            jnp.sum(keep_col * attention * attention),
            jnp.sum(keep_col * branch * branch),
            jnp.sum(keep_col * output * output),
            jnp.sum(keep_flags),
        ]
    )
    stat_total = lax.psum(stat_local, "dp")
    upstream = grad_out.astype(jnp.float32)
    grad_gates = jnp.sum(upstream[:, None, :] * arrived_rows, axis=-1)
    slot_grad = (gate_values[:, :, None] * upstream[:, None, :]).astype(jnp.bfloat16)
    result_grad = to_experts(place_rows(slot_grad.reshape(-1, model_width))).reshape(
        -1, model_width
    )
    grad_b_expert_out = jnp.sum(result_grad.astype(jnp.float32), axis=0)[None]
    grad_w_expert_out = jnp.einsum(
        "rf,rd->fd", hidden_low, result_grad, preferred_element_type=jnp.float32
    )[None]
    grad_hidden = jnp.einsum(
        "rd,fd->rf", result_grad, w_expert_out[0], preferred_element_type=jnp.float32
    )
    unused_value, gelu_back = jax.vjp(jax.nn.gelu, pre_act)
    grad_pre_low = gelu_back(grad_hidden)[0].astype(jnp.bfloat16)
    grad_b_expert_in = jnp.sum(grad_pre_low.astype(jnp.float32), axis=0)[None]
    grad_w_expert_in = jnp.einsum(
        "rd,rf->df", slot_input, grad_pre_low, preferred_element_type=jnp.float32
    )[None]
    input_part = jnp.einsum(
        "rf,df->rd", grad_pre_low, w_expert_in[0], preferred_element_type=jnp.float32
    ).reshape(-1, capacity, model_width)
    input_grad = from_experts(input_part, jnp.zeros((model_width,), jnp.float32))
    grad_normed_two = jnp.sum(take_rows(input_grad).astype(jnp.float32), axis=1)
    grad_chosen = gate_values * (
        grad_gates - jnp.sum(gate_values * grad_gates, axis=-1, keepdims=True)
    )
    grad_logits = jnp.sum(jnp.where(picked, grad_chosen[:, :, None], 0.0), axis=1)
    router_wide = router.astype(jnp.float32)
    grad_normed_two = grad_normed_two + jnp.einsum(
        "te,de->td", grad_logits, router_wide, precision=HIGHEST
    )
    grad_router = jnp.einsum(
        "td,te->de", normed_two_low.astype(jnp.float32), grad_logits, precision=HIGHEST
    )
    back_two, grad_ln2_gain, grad_ln2_bias = norm_backward(
        grad_normed_two, normal_two, inverse_two, ln2_gain
    )
    grad_middle = upstream + back_two
    attn_grad_low = grad_middle.astype(jnp.bfloat16)
    grad_b_attn_out = jnp.sum(attn_grad_low.astype(jnp.float32), axis=0)
    grad_w_attn_out = jnp.einsum(
        "th,td->hd", mixed_low, attn_grad_low, preferred_element_type=jnp.float32
    )
    grad_mixed_low = (
        jnp.einsum("td,hd->th", attn_grad_low, w_attn_out, preferred_element_type=jnp.float32)
        .astype(jnp.bfloat16)
        .reshape(images, SEQ, local_heads, HEAD)
    )
    scores_again = masked_scores(queries, keys_img, key_keep, score_scale)
    probs_again = jnp.exp(scores_again - top_score) / row_total
    grad_probs = jnp.einsum(
        "iqhd,ikhd->ihqk", grad_mixed_low, values_img, preferred_element_type=jnp.float32
    )
    row_dot = jnp.sum(probs_again * grad_probs, axis=-1, keepdims=True)
    grad_scores_low = (probs_again * (grad_probs - row_dot)).astype(jnp.bfloat16)
    grad_queries = (
        jnp.einsum("ihqk,ikhd->iqhd", grad_scores_low, keys_img, preferred_element_type=jnp.float32)
        * score_scale
    )
    grad_keys = (
        jnp.einsum("ihqk,iqhd->ikhd", grad_scores_low, queries, preferred_element_type=jnp.float32)
        * score_scale
    )
    grad_values = jnp.einsum(
        "ihqk,iqhd->ikhd",
        probs_again.astype(jnp.bfloat16),
        grad_mixed_low,
        preferred_element_type=jnp.float32,
    )
    grad_proj_low = (
        jnp.stack([grad_queries, grad_keys, grad_values], axis=2)
        .astype(jnp.bfloat16)
        .reshape(tok_rows, 3, local_width)
    )
    grad_bias_qv = jnp.stack(
        [
            jnp.sum(grad_proj_low[:, 0].astype(jnp.float32), axis=0),
            jnp.sum(grad_proj_low[:, 2].astype(jnp.float32), axis=0),
        ],
        axis=0,
    )
    grad_w_qkv = jnp.einsum(
        "td,tcf->dcf", normed_one_low, grad_proj_low, preferred_element_type=jnp.float32
    )
    head_part = jnp.einsum("tcf,dcf->td", grad_proj_low, w_qkv, preferred_element_type=jnp.float32)
    grad_normed_one = lax.psum(head_part.astype(jnp.bfloat16), "tensor").astype(jnp.float32)
    back_one, grad_ln1_gain, grad_ln1_bias = norm_backward(
        grad_normed_one, normal_one, inverse_one, ln1_gain
    )
    grad_tokens = grad_middle + back_one
    (
        grad_ln1_gain,
        grad_ln1_bias,
        grad_w_qkv,
        grad_bias_qv,
        grad_w_attn_out,
        grad_b_attn_out,
        grad_ln2_gain,
        grad_ln2_bias,
        grad_router,
    ) = lax.psum(
        (
            grad_ln1_gain,
            grad_ln1_bias,
            grad_w_qkv,
            grad_bias_qv,
            grad_w_attn_out,
            grad_b_attn_out,
            grad_ln2_gain,
            grad_ln2_bias,
            grad_router,
        ),
        "dp",
    )
    rms_values = jnp.sqrt(stat_total[:4] / (stat_total[4] * model_width))
    return (
        output.astype(jnp.bfloat16),
        grad_tokens,
        grad_ln1_gain,
        grad_ln1_bias,
        grad_w_qkv,
        grad_bias_qv,
        grad_w_attn_out,
        grad_b_attn_out,
        grad_ln2_gain,
        grad_ln2_bias,
        grad_router,
        grad_w_expert_in,
        grad_b_expert_in,
        grad_w_expert_out,
        grad_b_expert_out,
        rms_values,
    )


def solution(mesh):
    return jax.shard_map(
        per_device,
        mesh=mesh,
        in_specs=(
            P("dp", None),
            P("dp", None),
            P("dp"),
            P("dp", None),
            P("dp", None),
            P(),
            P(),
            P(None, None, "tensor"),
            P(None, "tensor"),
            P("tensor", None),
            P(),
            P(),
            P(),
            P(),
            P("dp", None, "tensor"),
            P("dp", "tensor"),
            P("dp", "tensor", None),
            P("dp", None),
        ),
        out_specs=(
            P("dp", None),
            P("dp", None),
            P(),
            P(),
            P(None, None, "tensor"),
            P(None, "tensor"),
            P("tensor", None),
            P(),
            P(),
            P(),
            P(),
            P("dp", None, "tensor"),
            P("dp", "tensor"),
            P("dp", "tensor", None),
            P("dp", None),
            P(),
        ),
        check_vma=False,
    )
```

profile of v0, /device:TPU:0, one launch (start us, length us, event | category | flops | bytes accessed | tf_op | source)
XLA Modules:
  0.0 562.6 jit_solution(7411658297101545101)
XLA Ops:
  20.4 21.4 %all-reduce.11.cloned.1.call-done = f32[197,768]{1,0:T(8,128)} async-done(((f32[197,768]{1,0:T(8,128)}), f32[197,768]{1,0:T(8,128)}) %all-reduce.11.cloned.1.call-update) | async-done | bytes 605200 | tf_op jit(solution)/shard_map/psum | solution.py:107
  48.0 3.7 scatter_custom_fusion
  55.9 6.9 %all-to-all-start = ((bf16[16,36,768]{2,1,0:T(8,128)(2,1)}), bf16[16,36,768]{2,1,0:T(8,128)(2,1)}, u32[]{:S(2)}, u32[]{:S(2)}) async-start(bf16[16,36,768]{2,1,0:T(8,128)(2,1)} %reshape.368), calls=%async_computation | async-start | bytes 1966080 | tf_op jit(solution)/shard_map/all_to_all | solution.py:41
  69.6 4.0 scatter_custom_fusion.1
  77.9 8.4 %all-to-all-done = bf16[16,36,768]{2,1,0:T(8,128)(2,1)} async-done(((bf16[16,36,768]{2,1,0:T(8,128)(2,1)}), bf16[16,36,768]{2,1,0:T(8,128)(2,1)}, u32[]{:S(2)}, u32[]{:S(2)}) %all-to-all-start) | async-done | bytes 884768 | tf_op jit(solution)/shard_map/all_to_all | solution.py:41
  86.3 6.1 %all-to-all-start.2 = ((bf16[16,36,768]{2,1,0:T(8,128)(2,1)}), bf16[16,36,768]{2,1,0:T(8,128)(2,1)}, u32[]{:S(2)}, u32[]{:S(2)}) async-start(bf16[16,36,768]{2,1,0:T(8,128)(2,1)} %reshape.371), calls=%async_computation.2 | async-start | bytes 1966080 | tf_op jit(solution)/shard_map/all_to_all | solution.py:41
  94.8 5.7 %multiply_convert_fusion = (bf16[576,1536]{1,0:T(8,128)(2,1)}, f32[576,1536]{1,0:T(8,128)}) fusion(f32[1536]{0:T(1024)S(1)} %reduce.13, bf16[576,768]{1,0:T(8,128)(2,1)} %reshape.369, bf16[1,768,1536]{2,1,0:T(8,128)(2,1)S(1)} %copy-done), kind=kOutput, calls=%fused_computation.17 | convolution fusion | flops 1367801856 | bytes 8558592 | tf_op jit(solution)/shard_map/dot_general | solution.py:139
  104.0 5.2 fusion.10
  109.3 5.4 all-to-all-done.2
  116.9 7.9 %convert_reduce_fusion = (f32[1536]{0:T(1024)S(1)}, bf16[576,1536]{1,0:T(8,128)(2,1)}) fusion(f32[576,1536]{1,0:T(8,128)} %get-tuple-element.53, bf16[576,768]{1,0:T(8,128)(2,1)} %reshape.372, bf16[1,1536,768]{2,1,0:T(8,128)(2,1)} %param.34), kind=kOutput, calls=%fused_computation.16 | convolution fusion | flops 1378417152 | bytes 8558592 | tf_op jit(solution)/shard_map/rd,fd->rf/dot_general | solution.py:170
  128.3 4.8 fusion.8
  133.1 9.7 %all-reduce.20 = bf16[16,36,768]{2,1,0:T(8,128)(2,1)} all-reduce(f32[16,36,768]{2,1,0:T(8,128)} %fusion.8), channel_id=1, replica_groups=mesh['dp'=16,'tensor'=2] {'tensor'}, use_global_device_ids=true, to_apply=%region_14.15 | all-reduce | flops 442368 | bytes 2654208 | tf_op jit(solution)/shard_map/psum | solution.py:46
  142.8 6.1 %all-to-all-start.3 = ((bf16[16,36,768]{2,1,0:T(8,128)(2,1)}), bf16[16,36,768]{2,1,0:T(8,128)(2,1)S(1)}, u32[]{:S(2)}, u32[]{:S(2)}) async-start(bf16[16,36,768]{2,1,0:T(8,128)(2,1)} %all-reduce.20), calls=%async_computation.3 | async-start | bytes 1966080 | tf_op jit(solution)/shard_map/all_to_all | solution.py:47
  151.6 20.8 %all-to-all-done.3 = bf16[16,36,768]{2,1,0:T(8,128)(2,1)S(1)} async-done(((bf16[16,36,768]{2,1,0:T(8,128)(2,1)}), bf16[16,36,768]{2,1,0:T(8,128)(2,1)S(1)}, u32[]{:S(2)}, u32[]{:S(2)}) %all-to-all-start.3) | async-done | bytes 884768 | tf_op jit(solution)/shard_map/all_to_all | solution.py:47
  172.4 6.3 %all-to-all-start.1 = ((bf16[16,36,768]{2,1,0:T(8,128)(2,1)}), bf16[16,36,768]{2,1,0:T(8,128)(2,1)S(1)}, u32[]{:S(2)}, u32[]{:S(2)}) async-start(bf16[16,36,768]{2,1,0:T(8,128)(2,1)} %add_convert_fusion), calls=%async_computation.1 | async-start | bytes 1966080 | tf_op jit(solution)/shard_map/all_to_all | solution.py:47
  190.7 10.3 %all-to-all-done.1 = bf16[16,36,768]{2,1,0:T(8,128)(2,1)S(1)} async-done(((bf16[16,36,768]{2,1,0:T(8,128)(2,1)}), bf16[16,36,768]{2,1,0:T(8,128)(2,1)S(1)}, u32[]{:S(2)}, u32[]{:S(2)}) %all-to-all-start.1) | async-done | bytes 884768 | tf_op jit(solution)/shard_map/all_to_all | solution.py:47
  208.0 4.5 multiply_reduce_fusion.1
  229.1 14.9 %all-reduce.15.cloned.1.call-done = bf16[197,768]{1,0:T(8,128)(2,1)} async-done(((bf16[197,768]{1,0:T(8,128)(2,1)}), bf16[197,768]{1,0:T(8,128)(2,1)}) %all-reduce.15.cloned.1.call-update) | async-done | bytes 302608 | tf_op jit(solution)/shard_map/psum | solution.py:246
  246.2 3.9 stack.55
  254.1 5.8 %convolution_bitcast_fusion.1 = f32[1,768,1536]{2,1,0:T(8,128)} fusion(bf16[576,768]{1,0:T(8,128)(2,1)S(1)} %copy-done.15, bf16[576,1536]{1,0:T(8,128)(2,1)} %get-tuple-element.58), kind=kOutput, calls=%fused_computation.8 | convolution fusion | flops 1358954496 | bytes 7372800 | tf_op jit(solution)/shard_map/rd,rf->df/dot_general | solution.py:176
  260.0 4.2 convolution_bitcast_fusion
  265.3 93.3 %all-reduce.17.cloned.1.call-done = (f32[768]{0:T(1024)}, f32[768]{0:T(1024)}, f32[2,384]{1,0:T(2,128)}, f32[768]{0:T(1024)}, f32[768]{0:T(1024)}, /*index=5*/f32[768]{0:T(1024)}, f32[768,16]{0,1:T(8,128)}, f32[5]{0:T(128)}) async-done(((f32[768]{0:T(1024)}, f32[768]{0:T(1024)}, f32[2,384]{1,0:T(2,128)}, f32[768]{0:T(1024)}, f32[768]{0:T(1024)}, /*index=5*/f32[768]{0:T(1024)}, f32[768,16]{0,1:T(8,128)}, ...) | async-done | bytes 67620 | tf_op jit(solution)/shard_map/psum | solution.py:261
  361.7 183.2 %all-reduce.19.cloned.1.call-done = (f32[768,3,384]{2,0,1:T(8,128)}, f32[384,768]{1,0:T(8,128)}) async-done(((f32[768,3,384]{2,0,1:T(8,128)}, f32[384,768]{1,0:T(8,128)}), (f32[768,3,384]{2,0,1:T(8,128)}, f32[384,768]{1,0:T(8,128)})) %all-reduce.19.cloned.1.call-update) | async-done | bytes 4718608 | tf_op jit(solution)/shard_map/psum | solution.py:261
  547.5 4.2 copy.107
  (181 shorter events, 100.2 us)
Async XLA Ops:
  7.2 87.7 %copy-start = (bf16[1,768,1536]{2,1,0:T(8,128)(2,1)S(1)}, bf16[1,768,1536]{2,1,0:T(8,128)(2,1)}, u32[]{:S(2)}) copy-start(bf16[1,768,1536]{2,1,0:T(8,128)(2,1)} %param.32) | copy-start | bytes 7077892
  7.2 34.6 %all-reduce.11.cloned.1.call-start = ((), (), s32[]{:S(2)}) async-start(), calls=%async_computation.4 | async-start | bytes 1228800 | tf_op jit(solution)/shard_map/psum | solution.py:107
  18.2 23.6 %copy-start.2 = (bf16[197,768]{1,0:T(8,128)(2,1)S(1)}, bf16[197,768]{1,0:T(8,128)(2,1)}, u32[]{:S(2)}) copy-start(bf16[197,768]{1,0:T(8,128)(2,1)} %param.18) | copy-start | bytes 907780
  18.2 23.6 %copy-start.24 = (f32[768]{0:T(1024)S(1)}, f32[768]{0:T(1024)}, u32[]{:S(2)}) copy-start(f32[768]{0:T(1024)} %param.28) | copy-start | bytes 9220
  18.9 24.4 %copy-start.21 = (f32[768]{0:T(1024)S(1)}, f32[768]{0:T(1024)}, u32[]{:S(2)}) copy-start(f32[768]{0:T(1024)} %param.29) | copy-start | bytes 9220
  18.9 24.4 %copy-start.26 = (f32[768]{0:T(1024)S(1)}, f32[768]{0:T(1024)}, u32[]{:S(2)}) copy-start(f32[768]{0:T(1024)} %param.30) | copy-start | bytes 9220
  55.9 30.4 %all-to-all-start = ((bf16[16,36,768]{2,1,0:T(8,128)(2,1)}), bf16[16,36,768]{2,1,0:T(8,128)(2,1)}, u32[]{:S(2)}, u32[]{:S(2)}) async-start(bf16[16,36,768]{2,1,0:T(8,128)(2,1)} %reshape.368), calls=%async_computation | async-start | bytes 1966080 | tf_op jit(solution)/shard_map/all_to_all | solution.py:41
  62.7 5.3 copy-start.19
  75.7 17.0 %copy-start.25 = (f32[1,1536]{1,0:T(1,128)S(1)}, f32[1,1536]{1,0:T(1,128)}, u32[]{:S(2)}) copy-start(f32[1,1536]{1,0:T(1,128)} %param.33) | copy-start | bytes 18436
  86.3 28.4 %all-to-all-start.2 = ((bf16[16,36,768]{2,1,0:T(8,128)(2,1)}), bf16[16,36,768]{2,1,0:T(8,128)(2,1)}, u32[]{:S(2)}, u32[]{:S(2)}) async-start(bf16[16,36,768]{2,1,0:T(8,128)(2,1)} %reshape.371), calls=%async_computation.2 | async-start | bytes 1966080 | tf_op jit(solution)/shard_map/all_to_all | solution.py:41
  92.5 56.5 %all-reduce.13.cloned.1.call-start = ((), (), s32[]{:S(2)}) async-start(), calls=%async_computation.5 | async-start | bytes 3932160 | tf_op jit(solution)/shard_map/psum | solution.py:46
  133.1 15.8 %copy-start.32 = (f32[1,768]{1,0:T(1,128)S(1)}, f32[1,768]{1,0:T(1,128)}, u32[]{:S(2)}) copy-start(f32[1,768]{1,0:T(1,128)} %param.35) | copy-start | bytes 9220
  142.8 29.6 %all-to-all-start.3 = ((bf16[16,36,768]{2,1,0:T(8,128)(2,1)}), bf16[16,36,768]{2,1,0:T(8,128)(2,1)S(1)}, u32[]{:S(2)}, u32[]{:S(2)}) async-start(bf16[16,36,768]{2,1,0:T(8,128)(2,1)} %all-reduce.20), calls=%async_computation.3 | async-start | bytes 1966080 | tf_op jit(solution)/shard_map/all_to_all | solution.py:47
  172.4 28.6 %all-to-all-start.1 = ((bf16[16,36,768]{2,1,0:T(8,128)(2,1)}), bf16[16,36,768]{2,1,0:T(8,128)(2,1)S(1)}, u32[]{:S(2)}, u32[]{:S(2)}) async-start(bf16[16,36,768]{2,1,0:T(8,128)(2,1)} %add_convert_fusion), calls=%async_computation.1 | async-start | bytes 1966080 | tf_op jit(solution)/shard_map/all_to_all | solution.py:47
  178.7 65.3 %all-reduce.15.cloned.1.call-start = ((), (), s32[]{:S(2)}) async-start(), calls=%async_computation.6 | async-start | bytes 614400 | tf_op jit(solution)/shard_map/psum | solution.py:246
  206.0 6.6 %copy-start.6 = (f32[197,768]{1,0:T(8,128)S(1)}, f32[197,768]{1,0:T(8,128)}, u32[]{:S(2)}) copy-start(f32[197,768]{1,0:T(8,128)} %reduce_sum.287) | copy-start | bytes 1815556
  212.6 4.5 copy-start.8
  225.5 133.1 %all-reduce.17.cloned.1.call-start = ((), (), s32[]{:S(2)}) async-start(), calls=%async_computation.7 | async-start | bytes 146432 | tf_op jit(solution)/shard_map/psum | solution.py:261
  226.4 23.7 %copy-start.18 = (bf16[6,64,197]{2,1,0:T(8,128)(2,1)S(1)}, bf16[6,64,197]{2,1,0:T(8,128)(2,1)}, u32[]{:S(2)}) copy-start(bf16[6,64,197]{2,1,0:T(8,128)(2,1)} %copy-done.17) | copy-start | bytes 453892
  250.1 294.8 %all-reduce.19.cloned.1.call-start = ((), (), s32[]{:S(2)}) async-start(), calls=%async_computation.8 | async-start | bytes 9437184 | tf_op jit(solution)/shard_map/psum | solution.py:261
  254.1 5.9 %copy-start.9 = (bf16[576,1536]{1,0:T(8,128)(2,1)S(1)}, bf16[576,1536]{1,0:T(8,128)(2,1)}, u32[]{:S(2)}) copy-start(bf16[576,1536]{1,0:T(8,128)(2,1)} %get-tuple-element.52) | copy-start | bytes 5308420
  254.1 5.9 %copy-start.16 = (bf16[576,768]{1,0:T(8,128)(2,1)S(1)}, bf16[576,768]{1,0:T(8,128)(2,1)}, u32[]{:S(2)}) copy-start(bf16[576,768]{1,0:T(8,128)(2,1)} %reshape.372) | copy-start | bytes 2654212
  547.4 4.8 copy-start.14
  547.4 8.2 %copy-start.1 = (bf16[1,768,1536]{2,1,0:T(8,128)(2,1)S(1)}, bf16[1,768,1536]{2,1,0:T(8,128)(2,1)}, u32[]{:S(2)}) copy-start(bf16[1,768,1536]{2,1,0:T(8,128)(2,1)} %param.32) | copy-start | bytes 7077892
  (20 other events, 52.6 us)
Sparse Core Ops, SparseCore 0:
  20.2 21.5 all-reduce.10
  109.4 22.2 all-reduce.12
  225.6 18.3 all-reduce.14
  251.5 107.0 all-reduce.16
  364.8 180.0 all-reduce.18
where the time goes:
time: 572 us; the launch traced here: 563 us
  waiting for transfers between devices  358 us (63%)
  local copies, waits for them, and re-layouts  68.4 us (12%)
  matrix products  56.9 us (10%)
  other arithmetic  28 us (5%)
  starting transfers between devices  26.2 us (5%)
  between operations  15.4 us (3%)
  blocking collectives  9.69 us (2%)
    psum x2, waiting for transfers between devices, per_device(): lax.psum((grad_ln1_gain, grad_ln1_bias, grad_w_qkv, grad_bias_qv, grad_w_...  277 us
    all_to_all x2, waiting for transfers between devices, from_experts(): lax.all_to_all((summed + shift_vec).astype(jnp.bfloat16), 'dp', split_axi...  31.2 us
    psum x1, waiting for transfers between devices, per_device(): attention = lax.psum(attn_part, 'tensor') + b_attn_out  21.4 us
    psum x1, waiting for transfers between devices, per_device(): lax.psum(head_part.astype(jnp.bfloat16), 'tensor').astype(jnp.float32)  14.9 us
    all_to_all x2, waiting for transfers between devices, to_experts(): lax.all_to_all(buffer, 'dp', split_axis=0, concat_axis=0, tiled=True)  13.9 us
    all_to_all x2, starting transfers between devices, to_experts(): lax.all_to_all(buffer, 'dp', split_axis=0, concat_axis=0, tiled=True)  13 us
    unnamed x79, local copies, waits for them, and re-layouts  12.4 us
    all_to_all x2, starting transfers between devices, from_experts(): lax.all_to_all((summed + shift_vec).astype(jnp.bfloat16), 'dp', split_axi...  12.4 us
  transfers between devices with their start and end apart: 9, of which 8 were waited for; matrix products, arithmetic and copies ran while one was open for 15% of the time, Pallas kernels for 0%

commit v1 on v0

v1 whole, which is shorter than its diff:
```python
import functools
import math

import jax
import jax.numpy as jnp
from jax import lax
from jax.experimental import pallas as pl
from jax.experimental.pallas import tpu as pltpu
from jax.sharding import PartitionSpec as P

HEAD = 64
SEQ = 197
LANE = 128
EPS = 1e-06
ROOT = math.sqrt(2.0 / math.pi)
CUBE = 0.044715
BUNCH = 16
MESH = pl.DeviceIdType.MESH
F32 = jnp.float32
BF16 = jnp.bfloat16
DMA = pltpu.SemaphoreType.DMA


def up_to(value, step):
    return -(-value // step) * step


def dot(a, b):
    return lax.dot_general(a, b, (((1,), (0,)), ((), ())), preferred_element_type=F32)


def dot_bt(a, b):
    return lax.dot_general(a, b, (((1,), (1,)), ((), ())), preferred_element_type=F32)


def dot_at(a, b):
    return lax.dot_general(a, b, (((0,), (0,)), ((), ())), preferred_element_type=F32)


def iota(shape, dim):
    return lax.broadcasted_iota(jnp.int32, shape, dim)


def one(cond, kind=BF16):
    return jnp.where(cond, 1.0, 0.0).astype(kind)


def split(value):
    high = value.astype(BF16)
    return high, (value - high.astype(F32)).astype(BF16)


def norm_parts(values):
    scale = 1.0 / values.shape[-1]
    center = values - jnp.sum(values, axis=-1, keepdims=True) * scale
    inverse = lax.rsqrt(jnp.sum(center * center, axis=-1, keepdims=True) * scale + EPS)
    return center * inverse, inverse


def norm_backward(incoming, normal, inverse, gain_vec):
    scale = 1.0 / incoming.shape[-1]
    scaled = incoming * gain_vec
    return inverse * (
        scaled
        - jnp.sum(scaled, axis=-1, keepdims=True) * scale
        - normal * (jnp.sum(scaled * normal, axis=-1, keepdims=True) * scale)
    )


def remote(src, dst, send_sem, recv_sem, device):
    return pltpu.make_async_remote_copy(
        src_ref=src,
        dst_ref=dst,
        send_sem=send_sem,
        recv_sem=recv_sem,
        device_id=device,
        device_id_type=MESH,
    )


class Sizes:
    def __init__(self, n, tok, width, heads_width, ff, experts):
        self.n = n
        self.tok = tok
        self.tp = up_to(tok, 16)
        self.tk = up_to(tok, LANE)
        self.width = width
        self.hw = heads_width
        self.pairs = heads_width // LANE
        self.ff = ff
        self.experts = experts
        self.cap = 2 * (3 * tok // (2 * n))
        self.main = self.cap // 16 * 16
        self.tail = self.cap - self.main
        self.half = width // 2
        self.blocks = self.half // LANE
        self.msg = self.main * self.blocks + 16
        self.nm = n * self.main
        self.slots = n * self.cap
        self.bt = BUNCH * self.tail
        self.bits = [1 << i for i in range(n.bit_length() - 1)]
        self.chunk = up_to(up_to(heads_width * width // LANE, n) // n, 16)
        self.small_rows = up_to(experts + 7, 16)
        self.small = up_to(up_to(self.small_rows * width // LANE, n) // n, 16)
        fits = 0 < self.tail * self.blocks <= 14 and n % BUNCH == 0
        if not fits or experts != n or (1 << len(self.bits)) != n:
            raise ValueError("unsupported sizes")


def chain_orders(bits):
    k = len(bits)
    if k < 4:
        return [bits] * 4
    a = list(bits)
    return [a, a[1:3] + a[:1] + a[3:], a[2:3] + a[:2] + a[3:], a]


def mega_kernel(
    z,
    tokens_ref,
    grad_out_ref,
    valid_ref,
    routes_ref,
    slots_ref,
    ln1g_ref,
    ln1b_ref,
    wqkv_hbm,
    bqv_ref,
    wo_hbm,
    bo_ref,
    ln2g_ref,
    ln2b_ref,
    router_ref,
    win_hbm,
    bin_ref,
    wout_hbm,
    bout_ref,
    o_tok,
    o_gtok,
    o_x,
    o_sg,
    o_hid,
    o_gp,
    o_red,
    o_small,
    o_bei,
    o_beo,
    o_rms,
    wqkv,
    wo,
    win,
    wout,
    xf,
    normal1,
    n1,
    n1t,
    upk,
    q_s,
    k_s,
    v_s,
    probs,
    mix,
    part,
    part_in,
    mid,
    normal2,
    n2,
    onehot,
    rows8,
    cols8,
    u_s,
    x_s,
    y_s,
    gh,
    pre,
    hid,
    gp,
    sg,
    gcol_s,
    ggv,
    half_out,
    half_in,
    gm,
    ag,
    dm,
    gpr,
    gn_out,
    gn_in,
    smallf,
    stat,
    s_msg,
    r_msg,
    f_msg,
    chain_g,
    chain_small,
    *rest,
):
    nbits = len(z.bits)
    chain_r = rest[:nbits]
    small_r = rest[nbits : 2 * nbits]
    chain_a, small_a, wsem, osem, hs, hr, ss, rs, fs, fr, cs, cr, as_, ar, sts, str_ = rest[
        2 * nbits :
    ]
    n = z.n
    me, core = lax.axis_index("dp"), lax.axis_index("tensor")
    sib = (me, 1 - core)
    tok, tp, tk, width, hw, half = z.tok, z.tp, z.tk, z.width, z.hw, z.half
    mine = pl.multiple_of(core * half, LANE)
    other = pl.multiple_of((1 - core) * half, LANE)

    barrier = pltpu.get_barrier_semaphore()

    def greet(j, carry):
        pl.semaphore_signal(
            barrier, inc=1, device_id=(lax.rem(me + j, n), core), device_id_type=MESH
        )
        return carry

    lax.fori_loop(1, n, greet, 0)
    pl.semaphore_signal(barrier, inc=1, device_id=sib, device_id_type=MESH)

    weights = [
        pltpu.make_async_copy(a, b, wsem.at[i])
        for i, (a, b) in enumerate(
            ((wqkv_hbm, wqkv), (wo_hbm, wo), (wout_hbm, wout), (win_hbm, win))
        )
    ]
    for copy in weights:
        copy.start()

    def a2a_send(i):
        r_msg[i, me] = s_msg[i, me]

        def go(j, carry):
            p = lax.rem(me + j, n)
            remote(
                s_msg.at[i, p], r_msg.at[i, me], ss.at[i, p], rs.at[i, me], (p, core)
            ).start()
            return carry

        lax.fori_loop(1, n, go, 0)
        remote(r_msg.at[i, me], f_msg.at[i, me], fs.at[i, me], fr.at[i, me], sib).start()

    def a2a_forward(i):
        def go(j, carry):
            p = lax.rem(me + n - j, n)
            remote(
                s_msg.at[i, p], r_msg.at[i, p], ss.at[i, p], rs.at[i, p], (p, core)
            ).wait_recv()
            remote(r_msg.at[i, p], f_msg.at[i, p], fs.at[i, p], fr.at[i, p], sib).start()
            return carry

        lax.fori_loop(1, n, go, 0)

    def a2a_finish(i):
        def go(j, carry):
            remote(r_msg.at[i, j], f_msg.at[i, j], fs.at[i, j], fr.at[i, j], sib).wait()
            return carry

        lax.fori_loop(0, n, go, 0)

    def a2a_sent(i):
        def go(j, carry):
            p = lax.rem(me + j, n)
            remote(
                s_msg.at[i, p], r_msg.at[i, me], ss.at[i, p], rs.at[i, me], (p, core)
            ).wait_send()
            return carry

        lax.fori_loop(1, n, go, 0)

    def assemble(i, out):
        tails = []
        for src, at in ((r_msg, mine), (f_msg, other)):
            for b in range(z.blocks):
                lanes = pl.ds(pl.multiple_of(at + b * LANE, LANE), LANE)
                if z.main:
                    rows = src[i, :, b * z.main : (b + 1) * z.main, :]
                    out[0 : z.nm, lanes] = rows.reshape(z.nm, LANE)
            for g in range(n // BUNCH):
                tail = tail_of(i, src, g)
                q, r = iota((z.bt, BUNCH * 16), 0), iota((z.bt, BUNCH * 16), 1)
                base = q // z.tail * 16 + q % z.tail
                for b in range(z.blocks):
                    lanes = pl.ds(pl.multiple_of(at + b * LANE, LANE), LANE)
                    pick = one(r == base + b * z.tail)
                    out[z.nm + g * z.bt : z.nm + (g + 1) * z.bt, lanes] = dot(pick, tail).astype(
                        BF16
                    )

    def tail_of(i, src, g):
        rows = src[i, g * BUNCH : (g + 1) * BUNCH, z.msg - 16 : z.msg, :]
        return rows.reshape(BUNCH * 16, LANE)

    def pack(i, value, extra):
        if z.main:
            for b in range(z.blocks):
                s_msg[i, :, b * z.main : (b + 1) * z.main, :] = value[
                    0 : z.nm, b * LANE : (b + 1) * LANE
                ].reshape(n, z.main, LANE)
        q, r = iota((BUNCH * 16, z.bt), 1), iota((BUNCH * 16, z.bt), 0)
        base = q // z.tail * 16 + q % z.tail
        for g in range(n // BUNCH):
            tail = None if extra is None else extra[g]
            for b in range(z.blocks):
                put = one(r == base + b * z.tail)
                rows = value[z.nm + g * z.bt : z.nm + (g + 1) * z.bt, b * LANE : (b + 1) * LANE]
                piece = dot(put, rows)
                tail = piece if tail is None else tail + piece
            s_msg[i, g * BUNCH : (g + 1) * BUNCH, z.msg - 16 : z.msg, :] = tail.astype(
                BF16
            ).reshape(BUNCH, 16, LANE)

    gate_row = 14

    rows8[...] = jnp.full(rows8.shape, -1.0, F32)
    rows8[0:2, 0:tok] = routes_ref[...].astype(F32)
    rows8[2:4, 0:tok] = slots_ref[...].astype(F32)
    rows8[4:5, 0:tok] = valid_ref[...].astype(F32)
    table = rows8[...]
    r_row = [table[k : k + 1, :].astype(jnp.int32) for k in range(2)]
    j_row = [table[2 + k : 3 + k, :].astype(jnp.int32) for k in range(2)]
    keep_row = table[4:5, :] > 0.5

    def targets(r, j):
        sent = (r >= 0) & (j < z.cap)
        flat = jnp.where(j < z.main, r * z.main + j, z.nm + r * z.tail + (j - z.main))
        return sent, jnp.where(sent, flat, -1)

    sent_row, flat_row = zip(*[targets(r, j) for r, j in zip(r_row, j_row)])
    cols8[...] = jnp.transpose(table)
    r_col = [cols8[0:tp, k : k + 1].astype(jnp.int32) for k in range(2)]
    j_col = [cols8[0:tp, 2 + k : 3 + k].astype(jnp.int32) for k in range(2)]
    keep_col = jnp.where(cols8[0:tp, 4:5] > 0.5, 1.0, 0.0)
    sent_col, flat_col = zip(*[targets(r, j) for r, j in zip(r_col, j_col)])

    slot_id = iota((z.slots, tk), 0)
    onehot[...] = one((slot_id == flat_row[0]) | (slot_id == flat_row[1]))
    tail_id = iota((BUNCH * 16, tk), 0)
    tail_row = [
        jnp.where(s & (j >= z.main), r * 16 + (j - z.main), -1000)
        for s, r, j in zip(sent_row, r_row, j_row)
    ]

    def place(src, i, extra):
        if z.main:
            for b in range(z.blocks):
                lanes = pl.ds(pl.multiple_of(mine + b * LANE, LANE), LANE)
                rows = dot(onehot[0 : z.nm, :], src[:, lanes]).astype(BF16)
                s_msg[i, :, b * z.main : (b + 1) * z.main, :] = rows.reshape(n, z.main, LANE)
        for g in range(n // BUNCH):
            tail = None if extra is None else extra[g]
            for b in range(z.blocks):
                lanes = pl.ds(pl.multiple_of(mine + b * LANE, LANE), LANE)
                at = b * z.tail - g * BUNCH * 16
                put = one((tail_id == tail_row[0] + at) | (tail_id == tail_row[1] + at))
                piece = dot(put, src[:, lanes])
                tail = piece if tail is None else tail + piece
            s_msg[i, g * BUNCH : (g + 1) * BUNCH, z.msg - 16 : z.msg, :] = tail.astype(
                BF16
            ).reshape(BUNCH, 16, LANE)

    upk[tok // 16 * 16 :, :] = jnp.zeros((tk - tok // 16 * 16, width), BF16)
    upk[0:tok, :] = grad_out_ref[...]
    place(upk, 0, None)

    xf[tok // 8 * 8 :, :] = jnp.zeros((tp - tok // 8 * 8, width), F32)
    xf[0:tok, :] = tokens_ref[...].astype(F32)
    normal, inverse1 = norm_parts(xf[...])
    normal1[...] = normal
    n1[tp:, :] = jnp.zeros((tk - tp, width), BF16)
    n1[0:tp, :] = (normal * ln1g_ref[...] + ln1b_ref[...]).astype(BF16)

    pl.semaphore_wait(barrier, n)
    a2a_send(0)

    weights[0].wait()
    for c, (dst, bias) in enumerate(((q_s, bqv_ref[0:1, :]), (k_s, None), (v_s, bqv_ref[1:2, :]))):
        value = dot(n1[0:tp, :], wqkv[c])
        if bias is not None:
            value = value + bias
        dst[tp:, :] = jnp.zeros((tk - tp, hw), BF16)
        dst[0:tp, :] = value.astype(BF16)

    score_scale = 1.0 / math.sqrt(HEAD)
    low_lane = iota((1, LANE), 1) < HEAD
    head_mask = [one(low_lane), one(jnp.logical_not(low_lane))]
    for p in range(z.pairs):
        lanes = slice(p * LANE, (p + 1) * LANE)
        qp, kp, vp = q_s[0:tp, lanes], k_s[:, lanes], v_s[:, lanes]
        outs = []
        for h in range(2):
            scores = dot_bt(qp * head_mask[h], kp) * score_scale
            scores = jnp.where(keep_row, scores, -1000000000.0)
            weights_h = jnp.exp(scores - jnp.max(scores, axis=-1, keepdims=True))
            prob = weights_h / jnp.sum(weights_h, axis=-1, keepdims=True)
            probs[2 * p + h] = prob
            outs.append(dot(prob.astype(BF16), vp))
        mix[0:tp, lanes] = jnp.where(low_lane, outs[0], outs[1]).astype(BF16)
    mix[tp:, :] = jnp.zeros((tk - tp, hw), BF16)
    weights[1].wait()
    part[...] = dot(mix[0:tp, :], wo[...])
    swap = remote(part, part_in, hs.at[0], hr.at[0], sib)
    swap.start()
    n1t[...] = jnp.transpose(n1[...])
    swap.wait()

    attention = part[...] + part_in[...] + bo_ref[...]
    stat_attn = jnp.sum(keep_col * attention * attention)
    middle = xf[...] + attention
    mid[...] = middle
    normal, inverse2 = norm_parts(middle)
    normal2[...] = normal
    n2[tp:, :] = jnp.zeros((tk - tp, width), BF16)
    n2[0:tp, :] = (normal * ln2g_ref[...] + ln2b_ref[...]).astype(BF16)
    logits = dot_bt(router_ref[...], n2[...])
    expert_id = iota((z.experts, tk), 0)
    chosen = [
        jnp.sum(jnp.where(expert_id == r, logits, 0.0), axis=0, keepdims=True) for r in r_row
    ]
    top = jnp.maximum(chosen[0], chosen[1])
    raw = [jnp.exp(c - top) for c in chosen]
    total = raw[0] + raw[1]
    gate_rows = [r / total for r in raw]
    cols8[0:tk, :] = jnp.transpose(
        jnp.concatenate(gate_rows + [jnp.zeros((6, tk), F32)], axis=0)
    )
    gate = [cols8[0:tp, k : k + 1] for k in range(2)]

    slot_lane = iota((tk, LANE), 1)
    numbers = []
    pad_col = [
        jnp.concatenate([j, jnp.full((tk - tp, 1), -1, jnp.int32)], axis=0) for j in j_col
    ]
    for g in range(n // BUNCH):
        number = None
        for k in range(2):
            high, low = split(gate_rows[k])
            at = r_row[k] * 16 + (gate_row - g * BUNCH * 16)
            lift = jnp.where(
                sent_row[k] & (tail_id == at), high.astype(F32), 0.0
            ) + jnp.where(sent_row[k] & (tail_id == at + 1), low.astype(F32), 0.0)
            piece = dot(lift.astype(BF16), one(slot_lane == pad_col[k]))
            number = piece if number is None else number + piece
        numbers.append(number)
    place(n2, 1, numbers)
    a2a_send(1)

    a2a_forward(0)
    a2a_finish(0)
    assemble(0, u_s)
    weights[2].wait()
    gh[...] = dot_bt(u_s[...], wout[...])

    weights[3].wait()
    a2a_forward(1)
    a2a_finish(1)
    assemble(1, x_s)

    def numbered(rows, per, first):
        q, r = iota((rows, BUNCH * 16), 0), iota((rows, BUNCH * 16), 1)
        pick = r == q // per * 16 + gate_row
        lane = iota((rows, LANE), 1) == iota((rows, LANE), 0) % per + first
        return pick, r == q // per * 16 + gate_row + 1, lane

    parts = [(0, BUNCH * z.main, z.main, 0)] if z.main else []
    parts += [(z.nm, z.bt, z.tail, z.main)]
    for g in range(n // BUNCH):
        tail = tail_of(1, r_msg, g)
        for at, rows, per, first in parts:
            high, low, lane = numbered(rows, per, first)
            picked = dot(one(high | low), tail)
            gcol_s[at + g * rows : at + (g + 1) * rows, :] = jnp.sum(
                jnp.where(lane, picked, 0.0), axis=-1, keepdims=True
            )
    pre[...] = dot(x_s[...], win[...])
    step = 16

    def activate(i, carry):
        rows = pl.ds(pl.multiple_of(i * step, step), step)
        v = pre[rows, :] + bin_ref[...]
        v2 = v * v
        t = jnp.tanh(ROOT * v * (1.0 + CUBE * v2))
        half_sum = 0.5 + 0.5 * t
        act = v * half_sum
        back = half_sum + (0.5 * ROOT) * v * (1.0 - t * t) * (1.0 + (3.0 * CUBE) * v2)
        g = gh[rows, :]
        hid[rows, :] = act.astype(BF16)
        gp[rows, :] = (gcol_s[rows, :] * g * back).astype(BF16)
        ggv[rows, :] = jnp.sum(g * act, axis=-1, keepdims=True)
        return carry

    lax.fori_loop(0, z.slots // step, activate, 0)

    half_out[0] = dot_bt(gp[...], win[pl.ds(other, half), :])
    swap = remote(half_out.at[0], half_in.at[0], hs.at[1], hr.at[1], sib)
    swap.start()
    own = dot_bt(gp[...], win[pl.ds(mine, half), :])
    bias_half = bout_ref[:, pl.ds(mine, half)]
    gg = ggv[...] + jnp.sum(
        u_s[:, pl.ds(mine, half)].astype(F32) * bias_half, axis=-1, keepdims=True
    )
    numbers = []
    for g in range(n // BUNCH):
        number = None
        for at, rows, per, first in parts:
            q, r = iota((BUNCH * 16, rows), 1), iota((BUNCH * 16, rows), 0)
            lane = iota((rows, LANE), 1) == iota((rows, LANE), 0) % per + first
            high, low = split(jnp.where(lane, gg[at + g * rows : at + (g + 1) * rows, :], 0.0))
            piece = dot(one(r == q // per * 16 + gate_row), high) + dot(
                one(r == q // per * 16 + gate_row + 1), low
            )
            number = piece if number is None else number + piece
        numbers.append(number)
    swap.wait()
    pack(2, (own + half_in[0]).astype(BF16), numbers)
    a2a_send(2)

    half_out[1] = dot(hid[...], wout[:, pl.ds(other, half)])
    swap = remote(half_out.at[1], half_in.at[1], hs.at[2], hr.at[2], sib)
    swap.start()
    own = dot(hid[...], wout[:, pl.ds(mine, half)]) + bias_half
    swap.wait()
    pack(3, (own + half_in[1]).astype(BF16), None)
    a2a_send(3)

    sg[...] = (gcol_s[...] * u_s[...].astype(F32)).astype(BF16)
    o_beo[...] = jnp.sum(sg[...].astype(F32), axis=0, keepdims=True)
    o_bei[...] = jnp.sum(gp[...].astype(F32), axis=0, keepdims=True)
    stores = [
        pltpu.make_async_copy(a, b, osem.at[i])
        for i, (a, b) in enumerate(((x_s, o_x), (sg, o_sg), (hid, o_hid), (gp, o_gp)))
    ]
    for copy in stores:
        copy.start()
    mix_t = jnp.transpose(mix[...])

    flat_id = iota((tp, z.slots), 1)
    back_one = [one(flat_id == f) for f in flat_col]
    a2a_forward(2)
    a2a_finish(2)
    assemble(2, y_s)
    tail_lane = iota((tp, BUNCH * 16), 1)
    grad_gate = []
    for k in range(2):
        row = None
        for g in range(n // BUNCH):
            at = r_col[k] * 16 + (gate_row - g * BUNCH * 16)
            pick = one(sent_col[k] & ((tail_lane == at) | (tail_lane == at + 1)))
            piece = dot(pick, tail_of(2, r_msg, g)) + dot(pick, tail_of(2, f_msg, g))
            row = piece if row is None else row + piece
        row = jnp.where(iota((tp, LANE), 1) == j_col[k], row, 0.0)
        grad_gate.append(jnp.sum(row, axis=-1, keepdims=True))
    mean_gate = gate[0] * grad_gate[0] + gate[1] * grad_gate[1]
    e_pad = up_to(z.experts, LANE)
    e_lane = iota((tp, e_pad), 1)
    grad_logits = jnp.where(
        e_lane == r_col[0], gate[0] * (grad_gate[0] - mean_gate), 0.0
    ) + jnp.where(e_lane == r_col[1], gate[1] * (grad_gate[1] - mean_gate), 0.0)
    gl_high, gl_low = split(grad_logits)
    router_pad = router_ref[...]
    if e_pad > z.experts:
        router_pad = jnp.concatenate(
            [router_pad, jnp.zeros((e_pad - z.experts, width), BF16)], axis=0
        )
    grad_n2 = (
        dot(back_one[0] + back_one[1], y_s[...])
        + dot(gl_high, router_pad)
        + dot(gl_low, router_pad)
    )
    grad_router = dot_at(gl_high, n2[0:tp, :]) + dot_at(gl_low, n2[0:tp, :])
    smallf[...] = jnp.zeros(smallf.shape, F32)
    ne = z.experts
    smallf[0:ne, :] = grad_router[0:ne, :]
    normal = normal2[...]
    smallf[ne + 2 : ne + 3, :] = jnp.sum(grad_n2 * normal, axis=0, keepdims=True)
    smallf[ne + 3 : ne + 4, :] = jnp.sum(grad_n2, axis=0, keepdims=True)
    gm[...] = upk[0:tp, :].astype(F32) + norm_backward(grad_n2, normal, inverse2, ln2g_ref[...])
    ag[tp:, :] = jnp.zeros((tk - tp, width), BF16)
    ag[0:tp, :] = gm[...].astype(BF16)
    smallf[ne + 4 : ne + 5, :] = jnp.sum(ag[...].astype(F32), axis=0, keepdims=True)

    groups = []
    for order in chain_orders(z.bits) + [z.bits]:
        start, size, steps = 0, n, []
        for b in order:
            bit = lax.rem(me // b, 2)
            peer = me + b * (1 - 2 * bit)
            size = size // 2
            steps.append((peer, start + (1 - bit) * size, start + bit * size, size))
            start = start + bit * size
        groups.append((steps, start))
    n_main = len(groups) - 1

    def chain_of(g):
        if g < n_main:
            return chain_g.at[g], [r.at[g] for r in chain_r], chain_a.at[g], z.chunk
        return chain_small, list(small_r), small_a, z.small

    def region(ref, at, count, rows):
        return ref.at[pl.ds(pl.multiple_of(at * rows, 16), count * rows)]

    def rs_copy(g, s):
        src, bufs, _, rows = chain_of(g)
        peer, give, _, size = groups[g][0][s]
        return remote(
            region(src, give, size, rows), bufs[s], cs.at[g, s], cr.at[g, s], (peer, core)
        )

    def rs_add(g, s, at, count, dst):
        src, bufs, _, rows = chain_of(g)
        keep = groups[g][0][s][2]

        def go(i, carry):
            here = pl.ds(pl.multiple_of((at + i) * rows, 16), rows)
            there = pl.ds(pl.multiple_of((at + i - keep) * rows, 16), rows)
            dst[here, :] = (src[here, :].astype(F32) + bufs[s][there, :].astype(F32)).astype(BF16)
            return carry

        lax.fori_loop(0, count, go, 0)

    def rs_step(g, s):
        src, _, out, _ = chain_of(g)
        rs_copy(g, s).wait()
        if s + 1 < nbits:
            _, give, keep, size = groups[g][0][s + 1]
            rs_add(g, s, give, size, src)
            rs_copy(g, s + 1).start()
            rs_add(g, s, keep, size, src)
        else:
            rs_add(g, s, groups[g][1], 1, out)
            ag_copy(g, s).start()

    def ag_copy(g, s):
        _, _, out, rows = chain_of(g)
        peer, _, keep, size = groups[g][0][s]
        piece = region(out, keep, size, rows)
        return remote(piece, piece, as_.at[g, s], ar.at[g, s], (peer, core))

    def ag_step(g, s):
        _, _, out, rows = chain_of(g)
        peer, give, _, size = groups[g][0][s]
        ag_copy(g, s).wait_send()
        piece = region(out, give, size, rows)
        remote(piece, piece, as_.at[g, s], ar.at[g, s], (peer, core)).wait_recv()
        if s > 0:
            ag_copy(g, s - 1).start()

    def fill(g, value, row):
        for b in range(value.shape[1] // LANE):
            chain_g[g, row : row + value.shape[0], :] = value[
                :, b * LANE : (b + 1) * LANE
            ].astype(BF16)
            row += value.shape[0]
        return row

    pad_from = hw * width // LANE
    if pad_from < n * z.chunk:
        for g in range(n_main):
            chain_g[g, pad_from:, :] = jnp.zeros((n * z.chunk - pad_from, LANE), BF16)
    fill(0, dot(mix_t, ag[...]), 0)
    rs_copy(0, 0).start()

    dm[...] = dot_bt(ag[0:tp, :], wo[...]).astype(BF16)
    for p in range(z.pairs):
        lanes = slice(p * LANE, (p + 1) * LANE)
        qp, kp, vp, dp = q_s[0:tp, lanes], k_s[:, lanes], v_s[:, lanes], dm[:, lanes]
        dq, dk, dv = [], [], []
        for h in range(2):
            prob = probs[2 * p + h]
            gprob = dot_bt(dp * head_mask[h], vp)
            inner = jnp.sum(prob * gprob, axis=-1, keepdims=True)
            gs = (prob * (gprob - inner)).astype(BF16)
            dq.append(dot(gs, kp))
            dk.append(dot_at(gs, qp))
            dv.append(dot_at(prob.astype(BF16), dp))
        for c, (pair, scale) in enumerate(((dq, score_scale), (dk, score_scale), (dv, 1.0))):
            value = (jnp.where(low_lane, pair[0], pair[1]) * scale).astype(BF16)
            at = slice(c * hw + p * LANE, c * hw + (p + 1) * LANE)
            if c == 0:
                gpr[0:tp, at] = value
                gpr[tp:, at] = jnp.zeros((tk - tp, LANE), BF16)
            else:
                gpr[:, at] = value
        joined = jnp.concatenate(
            [gpr[:, c * hw + p * LANE : c * hw + (p + 1) * LANE] for c in range(3)], axis=1
        )
        fill(1 + p, dot(n1t[...], joined), 0)
        rs_copy(1 + p, 0).start()

    head_part = None
    for c in range(3):
        piece = dot_bt(gpr[0:tp, c * hw : (c + 1) * hw], wqkv[c])
        head_part = piece if head_part is None else head_part + piece
    gn_out[...] = head_part.astype(BF16)
    swap = remote(gn_out, gn_in, hs.at[3], hr.at[3], sib)
    swap.start()
    smallf[ne + 5 : ne + 6, 0:hw] = jnp.sum(gpr[:, 0:hw].astype(F32), axis=0, keepdims=True)
    smallf[ne + 6 : ne + 7, 0:hw] = jnp.sum(
        gpr[:, 2 * hw : 3 * hw].astype(F32), axis=0, keepdims=True
    )
    swap.wait()
    grad_n1 = gn_out[...].astype(F32) + gn_in[...].astype(F32)
    normal = normal1[...]
    smallf[ne : ne + 1, :] = jnp.sum(grad_n1 * normal, axis=0, keepdims=True)
    smallf[ne + 1 : ne + 2, :] = jnp.sum(grad_n1, axis=0, keepdims=True)
    back = gm[...] + norm_backward(grad_n1, normal, inverse1, ln1g_ref[...])
    o_gtok[...] = back[0:tok, :]
    used = z.small_rows * (width // LANE)
    for b in range(width // LANE):
        chain_small[b * z.small_rows : (b + 1) * z.small_rows, :] = smallf[
            :, b * LANE : (b + 1) * LANE
        ].astype(BF16)
    if used < n * z.small:
        chain_small[used:, :] = jnp.zeros((n * z.small - used, LANE), BF16)
    rs_copy(n_main, 0).start()

    a2a_forward(3)
    a2a_finish(3)
    assemble(3, y_s)
    branch = gate[0] * dot(back_one[0], y_s[...]) + gate[1] * dot(back_one[1], y_s[...])
    output = mid[...] + branch
    o_tok[...] = output[0:tok, :].astype(BF16)
    lane_id = iota((1, LANE), 1)
    x_all = xf[...]
    line = jnp.zeros((1, LANE), F32)
    for i, number in enumerate(
        (
            jnp.sum(keep_col * x_all * x_all),
            stat_attn,
            jnp.sum(keep_col * branch * branch),
            jnp.sum(keep_col * output * output),
            jnp.sum(keep_col),
        )
    ):
        line = jnp.where(lane_id == i, number, line)
    stat[me] = jnp.broadcast_to(line, (8, LANE))

    def stat_go(j, carry):
        p = lax.rem(me + j, n)
        remote(stat.at[me], stat.at[me], sts.at[p], str_.at[me], (p, core)).start()
        return carry

    lax.fori_loop(1, n, stat_go, 0)

    for s in range(nbits):
        for g in range(n_main + 1):
            rs_step(g, s)

    def stat_wait(j, carry):
        p = lax.rem(me + j, n)
        remote(stat.at[me], stat.at[me], sts.at[p], str_.at[me], (p, core)).wait_send()
        remote(stat.at[p], stat.at[p], sts.at[p], str_.at[p], (p, core)).wait_recv()
        return carry

    lax.fori_loop(1, n, stat_wait, 0)
    totals = jnp.sum(stat[...], axis=0)
    count = jnp.sum(jnp.where(iota((8, LANE), 1) == 4, totals, 0.0), axis=-1, keepdims=True)
    o_rms[...] = jnp.sqrt(totals / (count * width))

    for s in range(nbits - 1, -1, -1):
        for g in range(n_main + 1):
            ag_step(g, s)
    for g in range(n_main):
        copy = pltpu.make_async_copy(chain_a.at[g], o_red.at[g], osem.at[4 + g])
        copy.start()
        stores.append(copy)
    for b in range(width // LANE):
        o_small[:, b * LANE : (b + 1) * LANE] = small_a[
            b * z.small_rows : (b + 1) * z.small_rows, :
        ].astype(F32)
    for i in range(4):
        a2a_sent(i)
    for copy in stores:
        copy.wait()


def per_device(
    tokens,
    grad_out,
    valid_mask,
    routes,
    slot_index,
    ln1_gain,
    ln1_bias,
    w_qkv,
    bias_qv,
    w_attn_out,
    b_attn_out,
    ln2_gain,
    ln2_bias,
    router,
    w_expert_in,
    b_expert_in,
    w_expert_out,
    b_expert_out,
):
    tok, width = tokens.shape
    hw = w_qkv.shape[2]
    ff = w_expert_in.shape[2]
    z = Sizes(lax.axis_size("dp"), tok, width, hw, ff, router.shape[1])
    n, tp, tk = z.n, z.tp, z.tk
    nbits = len(z.bits)
    vmem = pl.BlockSpec(memory_space=pltpu.VMEM)
    any_ = pl.BlockSpec(memory_space=pl.ANY)
    shape = jax.ShapeDtypeStruct
    groups = 1 + z.pairs
    V = pltpu.VMEM
    scratch = [
        V((3, width, hw), BF16),
        V((hw, width), BF16),
        V((width, ff), BF16),
        V((ff, width), BF16),
        V((tp, width), F32),
        V((tp, width), F32),
        V((tk, width), BF16),
        V((width, tk), BF16),
        V((tk, width), BF16),
        V((tk, hw), BF16),
        V((tk, hw), BF16),
        V((tk, hw), BF16),
        V((2 * z.pairs, tp, tk), F32),
        V((tk, hw), BF16),
        V((tp, width), F32),
        V((tp, width), F32),
        V((tp, width), F32),
        V((tp, width), F32),
        V((tk, width), BF16),
        V((z.slots, tk), BF16),
        V((8, tk), F32),
        V((tk, 8), F32),
        V((z.slots, width), BF16),
        V((z.slots, width), BF16),
        V((z.slots, width), BF16),
        V((z.slots, ff), F32),
        V((z.slots, ff), F32),
        V((z.slots, ff), BF16),
        V((z.slots, ff), BF16),
        V((z.slots, width), BF16),
        V((z.slots, 1), F32),
        V((z.slots, 1), F32),
        V((2, z.slots, z.half), F32),
        V((2, z.slots, z.half), F32),
        V((tp, width), F32),
        V((tk, width), BF16),
        V((tp, hw), BF16),
        V((tk, 3 * hw), BF16),
        V((tp, width), BF16),
        V((tp, width), BF16),
        V((z.small_rows, width), F32),
        V((n, 8, LANE), F32),
        V((4, n, z.msg, LANE), BF16),
        V((4, n, z.msg, LANE), BF16),
        V((4, n, z.msg, LANE), BF16),
        V((groups, n * z.chunk, LANE), BF16),
        V((n * z.small, LANE), BF16),
    ]
    scratch += [V((groups, (n >> (s + 1)) * z.chunk, LANE), BF16) for s in range(nbits)]
    scratch += [V(((n >> (s + 1)) * z.small, LANE), BF16) for s in range(nbits)]
    scratch += [
        V((groups, n * z.chunk, LANE), BF16),
        V((n * z.small, LANE), BF16),
        DMA((4,)),
        DMA((4 + groups,)),
        DMA((4,)),
        DMA((4,)),
        DMA((4, n)),
        DMA((4, n)),
        DMA((4, n)),
        DMA((4, n)),
        DMA((groups + 1, nbits)),
        DMA((groups + 1, nbits)),
        DMA((groups + 1, nbits)),
        DMA((groups + 1, nbits)),
        DMA((n,)),
        DMA((n,)),
    ]
    row = lambda v: v.reshape(1, -1)
    outs = pl.pallas_call(
        functools.partial(mega_kernel, z),
        out_shape=(
            shape((tok, width), BF16),
            shape((tok, width), F32),
            shape((z.slots, width), BF16),
            shape((z.slots, width), BF16),
            shape((z.slots, ff), BF16),
            shape((z.slots, ff), BF16),
            shape((groups, n * z.chunk, LANE), BF16),
            shape((z.small_rows, width), F32),
            shape((1, ff), F32),
            shape((1, width), F32),
            shape((8, LANE), F32),
        ),
        in_specs=[vmem] * 7
        + [any_, vmem, any_, vmem, vmem, vmem, vmem, any_, vmem, any_, vmem],
        out_specs=(vmem, vmem, any_, any_, any_, any_, any_, vmem, vmem, vmem, vmem),
        scratch_shapes=scratch,
        compiler_params=pltpu.CompilerParams(
            collective_id=0, has_side_effects=True, vmem_limit_bytes=60 * 2**20
        ),
    )(
        tokens,
        grad_out,
        row(valid_mask),
        routes.T,
        slot_index.T,
        row(ln1_gain),
        row(ln1_bias),
        jnp.transpose(w_qkv, (1, 0, 2)),
        bias_qv,
        w_attn_out,
        row(b_attn_out),
        row(ln2_gain),
        row(ln2_bias),
        router.T,
        w_expert_in[0],
        b_expert_in,
        w_expert_out[0],
        b_expert_out,
    )
    o_tok, o_gtok, o_x, o_sg, o_hid, o_gp, o_red, o_small, o_bei, o_beo, o_rms = outs
    gwin = lax.dot_general(
        o_x, o_gp, (((0,), (0,)), ((), ())), preferred_element_type=F32
    )
    gwout = lax.dot_general(
        o_hid, o_sg, (((0,), (0,)), ((), ())), preferred_element_type=F32
    )
    used = hw * width // LANE
    red = o_red[:, :used].astype(F32)
    gwo = jnp.transpose(red[0].reshape(width // LANE, hw, LANE), (1, 0, 2)).reshape(hw, width)
    gq = red[1:].reshape(z.pairs, 3, width, LANE)
    gwqkv = jnp.transpose(gq, (2, 1, 0, 3)).reshape(width, 3, hw)
    ne = z.experts
    return (
        o_tok,
        o_gtok,
        o_small[ne],
        o_small[ne + 1],
        gwqkv,
        o_small[ne + 5 : ne + 7, :hw],
        gwo,
        o_small[ne + 4],
        o_small[ne + 2],
        o_small[ne + 3],
        o_small[:ne].T,
        gwin[None],
        o_bei,
        gwout[None],
        o_beo,
        o_rms[0, :4],
    )


def solution(mesh):
    return jax.shard_map(
        per_device,
        mesh=mesh,
        in_specs=(
            P("dp", None),
            P("dp", None),
            P("dp"),
            P("dp", None),
            P("dp", None),
            P(),
            P(),
            P(None, None, "tensor"),
            P(None, "tensor"),
            P("tensor", None),
            P(),
            P(),
            P(),
            P(),
            P("dp", None, "tensor"),
            P("dp", "tensor"),
            P("dp", "tensor", None),
            P("dp", None),
        ),
        out_specs=(
            P("dp", None),
            P("dp", None),
            P(),
            P(),
            P(None, None, "tensor"),
            P(None, "tensor"),
            P("tensor", None),
            P(),
            P(),
            P(),
            P(),
            P("dp", None, "tensor"),
            P("dp", "tensor"),
            P("dp", "tensor", None),
            P("dp", None),
            P(),
        ),
        check_vma=False,
    )
```

time: 572 us -> 161 us (0.28); the launches traced: 563 us -> 161 us
  waiting for transfers between devices: 358 us -> 0 us
  Pallas kernels: 0 us -> 124 us
  matrix products: 56.9 us -> 8.44 us
  local copies, waits for them, and re-layouts: 68.4 us -> 27.5 us
  other arithmetic: 28 us -> 0 us
  starting transfers between devices: 26.2 us -> 0 us
  between operations: 15.4 us -> 0.7 us
  blocking collectives: 9.69 us -> 0 us
    psum x5 -> x0, waiting for transfers between devices: 313 us -> none  [the longest x2 277 us: per_device(): lax.psum((grad_ln1_gain, grad_ln1_bias, grad_w_qkv, grad_bias_qv, grad_w_...]
    pallas_call x0 -> x1, Pallas kernels: none -> 124 us  [per_device(): pl.pallas_call(functools.partial(mega_kernel, z), out_shape=(shape((tok,...]
    dot_general x20 -> x2, matrix products: 55.3 us -> 8.44 us  [the longest x1 4.23 us: per_device(): lax.dot_general(o_hid, o_sg, (((0,), (0,)), ((), ())), preferred_element_...]
    all_to_all x4 -> x0, waiting for transfers between devices: 45 us -> none  [the longest x2 31.2 us: from_experts(): lax.all_to_all((summed + shift_vec).astype(jnp.bfloat16), 'dp', split_axi...]
    all_to_all x4 -> x0, starting transfers between devices: 25.4 us -> none  [the longest x2 13 us: to_experts(): lax.all_to_all(buffer, 'dp', split_axis=0, concat_axis=0, tiled=True)]
    reduce_sum x16 -> x0, other arithmetic: 16.1 us -> none  [the longest x1 4.5 us: per_device(): grad_gates = jnp.sum(upstream[:, None, :] * arrived_rows, axis=-1)]
    psum x1 -> x0, blocking collectives: 9.69 us -> none  [from_experts(): summed = lax.psum(partial_rows, 'tensor')]
    dot_general x2 -> x0, local copies, waits for them, and re-layouts: 6.95 us -> none  [the longest x1 3.49 us: per_device(): jnp.einsum('rf,df->rd', grad_pre_low, w_expert_in[0], preferred_element_t...]
  transfers between devices with their start and end apart: 9 -> 0, of which waited for: 8 -> 0; matrix products, arithmetic and copies ran while one was open for 15% -> 0% of each run, Pallas kernels for 0% -> 0%
where the time goes in v1:
time: 161 us
  Pallas kernels  124 us (77%)
  local copies, waits for them, and re-layouts  27.5 us (17%)
  matrix products  8.44 us (5%)
    pallas_call x1, Pallas kernels, per_device(): pl.pallas_call(functools.partial(mega_kernel, z), out_shape=(shape((tok,...  124 us
    unnamed x22, local copies, waits for them, and re-layouts  9.43 us
    reshape x5, local copies, waits for them, and re-layouts, per_device(): row = lambda v: v.reshape(1, -1)  6.33 us
    dot_general x1, matrix products, per_device(): lax.dot_general(o_hid, o_sg, (((0,), (0,)), ((), ())), preferred_element_...  4.23 us
    dot_general x1, matrix products, per_device(): lax.dot_general(o_x, o_gp, (((0,), (0,)), ((), ())), preferred_element_ty...  4.22 us

profile of v1, /device:TPU:0, one launch (start us, length us, event | category | flops | bytes accessed | tf_op | source)
XLA Modules:
  0.0 160.7 jit_solution(9591307950981111506)
XLA Ops:
  0.6 1.3 reshape.60.ln1g_ref
  1.9 1.3 reshape.61.ln1b_ref
  3.2 1.3 reshape.62.bo_ref
  4.4 1.3 reshape.63.ln2g_ref
  5.7 1.3 reshape.64.ln2b_ref
  7.0 124.1 %shard_map.297 = (bf16[197,768]{1,0:T(8,128)(2,1)}, f32[197,768]{1,0:T(8,128)}, bf16[576,768]{1,0:T(8,128)(2,1)}, bf16[576,768]{1,0:T(8,128)(2,1)}, bf16[576,153...) custom-call(bf16[197,768]{1,0:T(8,128)(2,1)} %tokens_ref.1, ...), custom_call_target="tpu_custom_call" | custom-call | tf_op jit(solution)/shard_map/pallas_call | solution.py:879
  131.1 1.2 slice_bitcast_fusion.1
  132.3 1.3 slice.33
  133.6 1.6 %slice_reduce_fusion = (f32[768]{0:T(1024)}, f32[768]{0:T(1024)}, f32[768]{0:T(1024)}, f32[768]{0:T(1024)}, f32[768]{0:T(1024)}) fusion(f32[32,768]{1,0:T(8,128)} %get-tuple-element.29), kind=kLoop, calls=%fused_computation.3 | loop fusion | bytes 30720 | tf_op jit(solution)/shard_map/slice | solution.py:944
  135.2 1.4 slice_bitcast_fusion
  136.7 1.1 slice.41
  137.8 0.4 copy.37
  138.2 1.4 copy.39
  139.6 1.7 %slice.40 = f32[3,2304,128]{2,1,0:T(8,128)S(1)} slice(bf16[4,2304,128]{2,1,0:T(8,128)(2,1)} %get-tuple-element.30), slice={[1:4], [0:2304], [0:128]} | slice | bytes 7077888 | tf_op jit(solution)/shard_map/slice | solution.py:931
  141.3 2.9 %copy.36 = f32[3,3,768,128]{2,3,0,1:T(8,128)} copy(f32[3,3,768,128]{3,2,1,0:T(8,128)S(1)} %bitcast.27) | data formatting | bytes 7077888 | tf_op jit(solution)/shard_map/reshape | solution.py:931
  144.2 5.3 %copy.38 = f32[768,3,384]{2,0,1:T(8,128)} copy(f32[768,3,384]{0,2,1:T(8,128)} %bitcast.28) | data formatting | bytes 7077888
  149.5 0.0 copy-done.5
  149.5 4.2 %convolution_bitcast_fusion.1 = f32[1,768,1536]{2,1,0:T(8,128)} fusion(bf16[576,768]{1,0:T(8,128)(2,1)S(1)} %copy-done.7, bf16[576,1536]{1,0:T(8,128)(2,1)S(1)} %copy-done.5), kind=kOutput, calls=%fused_computation.1 | convolution fusion | flops 1358954496 | bytes 7372800 | tf_op jit(solution)/shard_map/dot_general | solution.py:922
  153.8 0.0 copy-done.6
  153.8 4.2 %convolution_bitcast_fusion = f32[1,1536,768]{2,1,0:T(8,128)} fusion(bf16[576,1536]{1,0:T(8,128)(2,1)S(1)} %copy-done.4, bf16[576,768]{1,0:T(8,128)(2,1)S(1)} %copy-done.6), kind=kOutput, calls=%fused_computation | convolution fusion | flops 1358954496 | bytes 7372800 | tf_op jit(solution)/shard_map/dot_general | solution.py:925
  158.0 0.7 copy.44
  158.7 0.8 copy.45
  159.6 0.6 copy.46
  160.2 0.6 copy.47
  (14 shorter events, 0.0 us)
Async XLA Ops:
  144.2 5.3 %copy-start.5 = (bf16[576,1536]{1,0:T(8,128)(2,1)S(1)}, bf16[576,1536]{1,0:T(8,128)(2,1)}, u32[]{:S(2)}) copy-start(bf16[576,1536]{1,0:T(8,128)(2,1)} %get-tuple-element.32) | copy-start | bytes 5308420
  144.2 5.3 %copy-start.7 = (bf16[576,768]{1,0:T(8,128)(2,1)S(1)}, bf16[576,768]{1,0:T(8,128)(2,1)}, u32[]{:S(2)}) copy-start(bf16[576,768]{1,0:T(8,128)(2,1)} %get-tuple-element.31) | copy-start | bytes 2654212
  149.5 4.2 %copy-start.4 = (bf16[576,1536]{1,0:T(8,128)(2,1)S(1)}, bf16[576,1536]{1,0:T(8,128)(2,1)}, u32[]{:S(2)}) copy-start(bf16[576,1536]{1,0:T(8,128)(2,1)} %get-tuple-element.34) | copy-start | bytes 5308420
  149.5 4.2 %copy-start.6 = (bf16[576,768]{1,0:T(8,128)(2,1)S(1)}, bf16[576,768]{1,0:T(8,128)(2,1)}, u32[]{:S(2)}) copy-start(bf16[576,768]{1,0:T(8,128)(2,1)} %get-tuple-element.35) | copy-start | bytes 2654212
  153.8 4.2 %copy-start.1 = (bf16[197,768]{1,0:T(8,128)(2,1)S(1)}, bf16[197,768]{1,0:T(8,128)(2,1)}, u32[]{:S(2)}) copy-start(bf16[197,768]{1,0:T(8,128)(2,1)} %get-tuple-element.75) | copy-start | bytes 907780
  153.8 5.0 %copy-start = (f32[197,768]{1,0:T(8,128)S(1)}, f32[197,768]{1,0:T(8,128)}, u32[]{:S(2)}) copy-start(f32[197,768]{1,0:T(8,128)} %get-tuple-element.76) | copy-start | bytes 1815556
  158.0 1.6 copy-start.2
  158.0 2.1 %copy-start.3 = (f32[1,768]{1,0:T(1,128)S(1)}, f32[1,768]{1,0:T(1,128)}, u32[]{:S(2)}) copy-start(f32[1,768]{1,0:T(1,128)} %get-tuple-element.89) | copy-start | bytes 9220

commit v2 on v1

--- a/solution.py
+++ b/solution.py
@@ -15,6 +15,7 @@
 ROOT = math.sqrt(2.0 / math.pi)
 CUBE = 0.044715
 BUNCH = 16
+TILE = 256
 MESH = pl.DeviceIdType.MESH
 F32 = jnp.float32
 BF16 = jnp.bfloat16
@@ -35,6 +36,10 @@
 
 def dot_at(a, b):
     return lax.dot_general(a, b, (((0,), (0,)), ((), ())), preferred_element_type=F32)
+
+
+def row_of(ref):
+    return ref[...].reshape(1, ref.shape[0])
 
 
 def iota(shape, dim):
@@ -99,20 +104,24 @@
         self.slots = n * self.cap
         self.bt = BUNCH * self.tail
         self.bits = [1 << i for i in range(n.bit_length() - 1)]
-        self.chunk = up_to(up_to(heads_width * width // LANE, n) // n, 16)
+        self.pack_rows = 4 * heads_width * width // LANE
+        self.chains = 6
+        self.chain_rows = self.pack_rows // self.chains
+        self.chunk = up_to(up_to(self.chain_rows, n) // n, 16)
         self.small_rows = up_to(experts + 7, 16)
         self.small = up_to(up_to(self.small_rows * width // LANE, n) // n, 16)
         fits = 0 < self.tail * self.blocks <= 14 and n % BUNCH == 0
+        fits = fits and self.chain_rows % heads_width == 0 and self.chain_rows % width == 0
         if not fits or experts != n or (1 << len(self.bits)) != n:
             raise ValueError("unsupported sizes")
 
 
 def chain_orders(bits):
     k = len(bits)
-    if k < 4:
-        return [bits] * 4
-    a = list(bits)
-    return [a, a[1:3] + a[:1] + a[3:], a[2:3] + a[:2] + a[3:], a]
+    if k < 3:
+        return [bits] * 6
+    order = ((0, 1, 2), (1, 2, 0), (2, 0, 1), (0, 2, 1), (1, 0, 2), (2, 1, 0))
+    return [[bits[i] for i in head] + bits[3:] for head in order]
 
 
 def mega_kernel(
@@ -176,6 +185,8 @@
     hid,
     gp,
     sg,
+    x_t,
+    hid_t,
     gcol_s,
     ggv,
     half_out,
@@ -369,7 +380,7 @@
     normal, inverse1 = norm_parts(xf[...])
     normal1[...] = normal
     n1[tp:, :] = jnp.zeros((tk - tp, width), BF16)
-    n1[0:tp, :] = (normal * ln1g_ref[...] + ln1b_ref[...]).astype(BF16)
+    n1[0:tp, :] = (normal * row_of(ln1g_ref) + row_of(ln1b_ref)).astype(BF16)
 
     pl.semaphore_wait(barrier, n)
     a2a_send(0)
@@ -405,14 +416,14 @@
     n1t[...] = jnp.transpose(n1[...])
     swap.wait()
 
-    attention = part[...] + part_in[...] + bo_ref[...]
+    attention = part[...] + part_in[...] + row_of(bo_ref)
     stat_attn = jnp.sum(keep_col * attention * attention)
     middle = xf[...] + attention
     mid[...] = middle
     normal, inverse2 = norm_parts(middle)
     normal2[...] = normal
     n2[tp:, :] = jnp.zeros((tk - tp, width), BF16)
-    n2[0:tp, :] = (normal * ln2g_ref[...] + ln2b_ref[...]).astype(BF16)
+    n2[0:tp, :] = (normal * row_of(ln2g_ref) + row_of(ln2b_ref)).astype(BF16)
     logits = dot_bt(router_ref[...], n2[...])
     expert_id = iota((z.experts, tk), 0)
     chosen = [
@@ -522,14 +533,15 @@
     own = dot(hid[...], wout[:, pl.ds(mine, half)]) + bias_half
     swap.wait()
     pack(3, (own + half_in[1]).astype(BF16), None)
-    a2a_send(3)
 
     sg[...] = (gcol_s[...] * u_s[...].astype(F32)).astype(BF16)
+    x_t[...] = jnp.transpose(x_s[...])
+    hid_t[...] = jnp.transpose(hid[...])
     o_beo[...] = jnp.sum(sg[...].astype(F32), axis=0, keepdims=True)
     o_bei[...] = jnp.sum(gp[...].astype(F32), axis=0, keepdims=True)
     stores = [
         pltpu.make_async_copy(a, b, osem.at[i])
-        for i, (a, b) in enumerate(((x_s, o_x), (sg, o_sg), (hid, o_hid), (gp, o_gp)))
+        for i, (a, b) in enumerate(((x_t, o_x), (sg, o_sg), (hid_t, o_hid), (gp, o_gp)))
     ]
     for copy in stores:
         copy.start()
@@ -538,6 +550,7 @@
     flat_id = iota((tp, z.slots), 1)
     back_one = [one(flat_id == f) for f in flat_col]
     a2a_forward(2)
+    a2a_send(3)
     a2a_finish(2)
     assemble(2, y_s)
     tail_lane = iota((tp, BUNCH * 16), 1)
@@ -575,7 +588,7 @@
     normal = normal2[...]
     smallf[ne + 2 : ne + 3, :] = jnp.sum(grad_n2 * normal, axis=0, keepdims=True)
     smallf[ne + 3 : ne + 4, :] = jnp.sum(grad_n2, axis=0, keepdims=True)
-    gm[...] = upk[0:tp, :].astype(F32) + norm_backward(grad_n2, normal, inverse2, ln2g_ref[...])
+    gm[...] = upk[0:tp, :].astype(F32) + norm_backward(grad_n2, normal, inverse2, row_of(ln2g_ref))
     ag[tp:, :] = jnp.zeros((tk - tp, width), BF16)
     ag[0:tp, :] = gm[...].astype(BF16)
     smallf[ne + 4 : ne + 5, :] = jnp.sum(ag[...].astype(F32), axis=0, keepdims=True)
@@ -646,20 +659,22 @@
         if s > 0:
             ag_copy(g, s - 1).start()
 
-    def fill(g, value, row):
+    filled = 0
+
+    def fill(value):
+        nonlocal filled
+        rows = value.shape[0]
         for b in range(value.shape[1] // LANE):
-            chain_g[g, row : row + value.shape[0], :] = value[
-                :, b * LANE : (b + 1) * LANE
-            ].astype(BF16)
-            row += value.shape[0]
-        return row
-
-    pad_from = hw * width // LANE
-    if pad_from < n * z.chunk:
+            g, at = divmod(filled, z.chain_rows)
+            chain_g[g, at : at + rows, :] = value[:, b * LANE : (b + 1) * LANE].astype(BF16)
+            filled += rows
+            if filled == (g + 1) * z.chain_rows:
+                rs_copy(g, 0).start()
+
+    if z.chain_rows < n * z.chunk:
         for g in range(n_main):
-            chain_g[g, pad_from:, :] = jnp.zeros((n * z.chunk - pad_from, LANE), BF16)
-    fill(0, dot(mix_t, ag[...]), 0)
-    rs_copy(0, 0).start()
+            chain_g[g, z.chain_rows :, :] = jnp.zeros((n * z.chunk - z.chain_rows, LANE), BF16)
+    fill(dot(mix_t, ag[...]))
 
     dm[...] = dot_bt(ag[0:tp, :], wo[...]).astype(BF16)
     for p in range(z.pairs):
@@ -685,8 +700,7 @@
         joined = jnp.concatenate(
             [gpr[:, c * hw + p * LANE : c * hw + (p + 1) * LANE] for c in range(3)], axis=1
         )
-        fill(1 + p, dot(n1t[...], joined), 0)
-        rs_copy(1 + p, 0).start()
+        fill(dot(n1t[...], joined))
 
     head_part = None
     for c in range(3):
@@ -704,7 +718,7 @@
     normal = normal1[...]
     smallf[ne : ne + 1, :] = jnp.sum(grad_n1 * normal, axis=0, keepdims=True)
     smallf[ne + 1 : ne + 2, :] = jnp.sum(grad_n1, axis=0, keepdims=True)
-    back = gm[...] + norm_backward(grad_n1, normal, inverse1, ln1g_ref[...])
+    back = gm[...] + norm_backward(grad_n1, normal, inverse1, row_of(ln1g_ref))
     o_gtok[...] = back[0:tok, :]
     used = z.small_rows * (width // LANE)
     for b in range(width // LANE):
@@ -771,6 +785,121 @@
         ].astype(F32)
     for i in range(4):
         a2a_sent(i)
+    for copy in stores:
+        copy.wait()
+
+
+def last_kernel(
+    z,
+    i_tok,
+    i_gtok,
+    i_x,
+    i_sg,
+    i_hid,
+    i_gp,
+    i_red,
+    i_small,
+    i_bei,
+    i_beo,
+    i_rms,
+    o_tok,
+    o_gtok,
+    o_ln1g,
+    o_ln1b,
+    o_wqkv,
+    o_bqv,
+    o_wo,
+    o_bo,
+    o_ln2g,
+    o_ln2b,
+    o_router,
+    o_win,
+    o_bin,
+    o_wout,
+    o_bout,
+    o_rms,
+    x_t,
+    sg,
+    hid_t,
+    gp,
+    red,
+    wqkv,
+    wo,
+    win,
+    wout,
+    tok_s,
+    gtok_s,
+    isem,
+    osem,
+):
+    ne, width, hw = z.experts, z.width, z.hw
+    loads = [
+        pltpu.make_async_copy(i_red.at[g], red.at[g], isem.at[6 + g]) for g in range(z.chains)
+    ]
+    loads += [
+        pltpu.make_async_copy(a, b, isem.at[i])
+        for i, (a, b) in enumerate(
+            (
+                (i_x, x_t),
+                (i_gp, gp),
+                (i_hid, hid_t),
+                (i_sg, sg),
+                (i_tok, tok_s),
+                (i_gtok, gtok_s),
+            )
+        )
+    ]
+    for copy in loads:
+        copy.start()
+    stores = []
+
+    def store(src, dst, i):
+        copy = pltpu.make_async_copy(src, dst, osem.at[i])
+        copy.start()
+        stores.append(copy)
+
+    for ref, i in ((o_ln1g, 0), (o_ln1b, 1), (o_ln2g, 2), (o_ln2b, 3), (o_bo, 4)):
+        ref[...] = i_small[ne + i : ne + i + 1, :].reshape(width)
+    o_router[...] = i_small[0:ne, :]
+    o_bqv[...] = i_small[ne + 5 : ne + 7, 0:hw]
+    o_bin[...] = i_bei[...]
+    o_bout[...] = i_beo[...]
+    o_rms[...] = i_rms[0:1, 0:4].reshape(4)
+
+    at, ready = 0, 0
+
+    def take(rows):
+        nonlocal at, ready
+        g, row = divmod(at, z.chain_rows)
+        if g == ready:
+            loads[g].wait()
+            ready += 1
+        at += rows
+        return red[g, row : row + rows, :].astype(F32)
+
+    for b in range(width // LANE):
+        wo[:, b * LANE : (b + 1) * LANE] = take(hw)
+    store(wo, o_wo, 2)
+    for p in range(z.pairs):
+        for c in range(3):
+            wqkv[c, :, p * LANE : (p + 1) * LANE] = take(width)
+    store(wqkv, o_wqkv, 3)
+    for i in range(2):
+        loads[z.chains + i].wait()
+    tiles = z.ff // TILE
+    for t in range(tiles):
+        cols = slice(t * TILE, (t + 1) * TILE)
+        win[:, cols] = dot(x_t[...], gp[:, cols])
+        store(win.at[:, cols], o_win.at[0, :, cols], 4 + t)
+    for i in range(2, 4):
+        loads[z.chains + i].wait()
+    for t in range(tiles):
+        rows = slice(t * TILE, (t + 1) * TILE)
+        wout[rows, :] = dot(hid_t[rows, :], sg[...])
+        store(wout.at[rows, :], o_wout.at[0, rows, :], 4 + tiles + t)
+    for i, (src, dst) in enumerate(((tok_s, o_tok), (gtok_s, o_gtok))):
+        loads[z.chains + 4 + i].wait()
+        store(src, dst, i)
     for copy in stores:
         copy.wait()
 
@@ -804,7 +933,7 @@
     vmem = pl.BlockSpec(memory_space=pltpu.VMEM)
     any_ = pl.BlockSpec(memory_space=pl.ANY)
     shape = jax.ShapeDtypeStruct
-    groups = 1 + z.pairs
+    groups = z.chains
     V = pltpu.VMEM
     scratch = [
         V((3, width, hw), BF16),
@@ -837,6 +966,8 @@
         V((z.slots, ff), BF16),
         V((z.slots, ff), BF16),
         V((z.slots, width), BF16),
+        V((width, z.slots), BF16),
+        V((ff, z.slots), BF16),
         V((z.slots, 1), F32),
         V((z.slots, 1), F32),
         V((2, z.slots, z.half), F32),
@@ -881,9 +1012,9 @@
         out_shape=(
             shape((tok, width), BF16),
             shape((tok, width), F32),
+            shape((width, z.slots), BF16),
             shape((z.slots, width), BF16),
-            shape((z.slots, width), BF16),
-            shape((z.slots, ff), BF16),
+            shape((ff, z.slots), BF16),
             shape((z.slots, ff), BF16),
             shape((groups, n * z.chunk, LANE), BF16),
             shape((z.small_rows, width), F32),
@@ -904,14 +1035,14 @@
         row(valid_mask),
         routes.T,
         slot_index.T,
-        row(ln1_gain),
-        row(ln1_bias),
+        ln1_gain,
+        ln1_bias,
         jnp.transpose(w_qkv, (1, 0, 2)),
         bias_qv,
         w_attn_out,
-        row(b_attn_out),
-        row(ln2_gain),
-        row(ln2_bias),
+        b_attn_out,
+        ln2_gain,
+        ln2_bias,
         router.T,
         w_expert_in[0],
         b_expert_in,
@@ -919,35 +1050,62 @@
         b_expert_out,
     )
     o_tok, o_gtok, o_x, o_sg, o_hid, o_gp, o_red, o_small, o_bei, o_beo, o_rms = outs
-    gwin = lax.dot_general(
-        o_x, o_gp, (((0,), (0,)), ((), ())), preferred_element_type=F32
-    )
-    gwout = lax.dot_general(
-        o_hid, o_sg, (((0,), (0,)), ((), ())), preferred_element_type=F32
-    )
-    used = hw * width // LANE
-    red = o_red[:, :used].astype(F32)
-    gwo = jnp.transpose(red[0].reshape(width // LANE, hw, LANE), (1, 0, 2)).reshape(hw, width)
-    gq = red[1:].reshape(z.pairs, 3, width, LANE)
-    gwqkv = jnp.transpose(gq, (2, 1, 0, 3)).reshape(width, 3, hw)
     ne = z.experts
+    vec = shape((width,), F32)
+    last = pl.pallas_call(
+        functools.partial(last_kernel, z),
+        out_shape=(
+            shape((tok, width), BF16),
+            shape((tok, width), F32),
+            vec,
+            vec,
+            shape((3, width, hw), F32),
+            shape((2, hw), F32),
+            shape((hw, width), F32),
+            vec,
+            vec,
+            vec,
+            shape((ne, width), F32),
+            shape((1, width, ff), F32),
+            shape((1, ff), F32),
+            shape((1, ff, width), F32),
+            shape((1, width), F32),
+            shape((4,), F32),
+        ),
+        in_specs=[any_] * 7 + [vmem] * 4,
+        out_specs=(
+            [any_] * 2
+            + [vmem] * 2
+            + [any_, vmem, any_]
+            + [vmem] * 4
+            + [any_, vmem, any_, vmem, vmem]
+        ),
+        scratch_shapes=[
+            V((width, z.slots), BF16),
+            V((z.slots, width), BF16),
+            V((ff, z.slots), BF16),
+            V((z.slots, ff), BF16),
+            V((groups, n * z.chunk, LANE), BF16),
+            V((3, width, hw), F32),
+            V((hw, width), F32),
+            V((width, ff), F32),
+            V((ff, width), F32),
+            V((tok, width), BF16),
+            V((tok, width), F32),
+            DMA((6 + groups,)),
+            DMA((4 + 2 * (ff // TILE),)),
+        ],
+        compiler_params=pltpu.CompilerParams(vmem_limit_bytes=60 * 2**20),
+    )(o_tok, o_gtok, o_x, o_sg, o_hid, o_gp, o_red, o_small, o_bei, o_beo, o_rms)
     return (
-        o_tok,
-        o_gtok,
-        o_small[ne],
-        o_small[ne + 1],
-        gwqkv,
-        o_small[ne + 5 : ne + 7, :hw],
-        gwo,
-        o_small[ne + 4],
-        o_small[ne + 2],
-        o_small[ne + 3],
-        o_small[:ne].T,
-        gwin[None],
-        o_bei,
-        gwout[None],
-        o_beo,
-        o_rms[0, :4],
+        last[0],
+        last[1],
+        last[2],
+        last[3],
+        jnp.transpose(last[4], (1, 0, 2)),
+        *last[5:10],
+        last[10].T,
+        *last[11:],
     )
 
 

time: 161 us -> 126 us (0.78)
  local copies, waits for them, and re-layouts: 27.5 us -> 0 us
  matrix products: 8.44 us -> 0 us
    pallas_call x0 -> x1, Pallas kernels: none -> 10.6 us  [per_device(): pl.pallas_call(functools.partial(last_kernel, z), out_shape=(shape((tok,...]
    pallas_call x1, Pallas kernels: 124 us -> 115 us  [per_device(): pl.pallas_call(functools.partial(mega_kernel, z), out_shape=(shape((tok,...]
    unnamed x22 -> x0, local copies, waits for them, and re-layouts: 9.43 us -> none
    reshape x6 -> x0, local copies, waits for them, and re-layouts: 9.28 us -> none  [the longest x5 6.33 us: per_device(): row = lambda v: v.reshape(1, -1)]
    dot_general x2 -> x0, matrix products: 8.44 us -> none  [the longest x1 4.23 us: per_device(): lax.dot_general(o_hid, o_sg, (((0,), (0,)), ((), ())), preferred_element_...]
    slice x4 -> x0, local copies, waits for them, and re-layouts: 5.78 us -> none  [the longest x1 1.7 us: per_device(): gq = red[1:].reshape(z.pairs, 3, width, LANE)]
where the time goes in v2:
time: 126 us
  Pallas kernels  125 us (99%)
    pallas_call x1, Pallas kernels, per_device(): pl.pallas_call(functools.partial(mega_kernel, z), out_shape=(shape((tok,...  115 us
    pallas_call x1, Pallas kernels, per_device(): pl.pallas_call(functools.partial(last_kernel, z), out_shape=(shape((tok,...  10.6 us

profile of v2, /device:TPU:0, one launch (start us, length us, event | category | flops | bytes accessed | tf_op | source)
XLA Modules:
  0.0 126.1 jit_solution(15128251251713449240)
XLA Ops:
  0.7 114.6 %shard_map.297 = (bf16[197,768]{1,0:T(8,128)(2,1)}, f32[197,768]{1,0:T(8,128)}, bf16[768,576]{1,0:T(8,128)(2,1)}, bf16[576,768]{1,0:T(8,128)(2,1)}, bf16[1536,57...) custom-call(bf16[197,768]{1,0:T(8,128)(2,1)} %tokens_ref.1, ...), custom_call_target="tpu_custom_call" | custom-call | tf_op jit(solution)/shard_map/pallas_call | solution.py:1010
  115.3 10.6 %shard_map.298 = (bf16[197,768]{1,0:T(8,128)(2,1)}, f32[197,768]{1,0:T(8,128)}, f32[768]{0:T(1024)}, f32[768]{0:T(1024)}, f32[3,768,384]{2,1,0:T(8,128)}, /*inde...) custom-call(bf16[197,768]{1,0:T(8,128)(2,1)} %get-tuple-element.43.i, ...), custom_call_target="tpu_custom_call" | custom-call | tf_op jit(solution)/shard_map/pallas_call | solution.py:1055

commit v3 on v2

--- a/solution.py
+++ b/solution.py
@@ -14,7 +14,8 @@
 EPS = 1e-06
 ROOT = math.sqrt(2.0 / math.pi)
 CUBE = 0.044715
-BUNCH = 16
+GROUPS = 4
+SEND_ORDER = (0, 2, 1, 3)
 TILE = 256
 MESH = pl.DeviceIdType.MESH
 F32 = jnp.float32
@@ -100,9 +101,11 @@
         self.half = width // 2
         self.blocks = self.half // LANE
         self.msg = self.main * self.blocks + 16
-        self.nm = n * self.main
+        self.per = n // GROUPS
+        self.gm = self.per * self.main
+        self.gt = self.per * self.tail
+        self.rows = self.per * self.cap
         self.slots = n * self.cap
-        self.bt = BUNCH * self.tail
         self.bits = [1 << i for i in range(n.bit_length() - 1)]
         self.pack_rows = 4 * heads_width * width // LANE
         self.chains = 6
@@ -110,7 +113,7 @@
         self.chunk = up_to(up_to(self.chain_rows, n) // n, 16)
         self.small_rows = up_to(experts + 7, 16)
         self.small = up_to(up_to(self.small_rows * width // LANE, n) // n, 16)
-        fits = 0 < self.tail * self.blocks <= 14 and n % BUNCH == 0
+        fits = 0 < self.tail * self.blocks <= 14 and self.gt % 16 == 0
         fits = fits and self.chain_rows % heads_width == 0 and self.chain_rows % width == 0
         if not fits or experts != n or (1 << len(self.bits)) != n:
             raise ValueError("unsupported sizes")
@@ -126,8 +129,8 @@
 
 def mega_kernel(
     z,
-    tokens_ref,
-    grad_out_ref,
+    tokens_hbm,
+    grad_out_hbm,
     valid_ref,
     routes_ref,
     slots_ref,
@@ -155,6 +158,10 @@
     o_bei,
     o_beo,
     o_rms,
+    tokens_ref,
+    grad_out_ref,
+    tok_out,
+    gtok_out,
     wqkv,
     wo,
     win,
@@ -191,6 +198,7 @@
     ggv,
     half_out,
     half_in,
+    half_own,
     gm,
     ag,
     dm,
@@ -209,7 +217,7 @@
     nbits = len(z.bits)
     chain_r = rest[:nbits]
     small_r = rest[nbits : 2 * nbits]
-    chain_a, small_a, wsem, osem, hs, hr, ss, rs, fs, fr, cs, cr, as_, ar, sts, str_ = rest[
+    chain_a, small_a, wsem, osem, hs, hr, ss, rs, fs, fr, cs, cr, as_, ar, st = rest[
         2 * nbits :
     ]
     n = z.n
@@ -230,6 +238,12 @@
     lax.fori_loop(1, n, greet, 0)
     pl.semaphore_signal(barrier, inc=1, device_id=sib, device_id_type=MESH)
 
+    tokens_in = [
+        pltpu.make_async_copy(a, b, wsem.at[4 + i])
+        for i, (a, b) in enumerate(((tokens_hbm, tokens_ref), (grad_out_hbm, grad_out_ref)))
+    ]
+    for copy in tokens_in[::-1]:
+        copy.start()
     weights = [
         pltpu.make_async_copy(a, b, wsem.at[i])
         for i, (a, b) in enumerate(
@@ -239,88 +253,78 @@
     for copy in weights:
         copy.start()
 
-    def a2a_send(i):
-        r_msg[i, me] = s_msg[i, me]
-
-        def go(j, carry):
-            p = lax.rem(me + j, n)
-            remote(
-                s_msg.at[i, p], r_msg.at[i, me], ss.at[i, p], rs.at[i, me], (p, core)
-            ).start()
+    per = z.per
+    own = me // per
+    own_bits = [lax.rem(own, 2), own // 2]
+
+    def group_at(k):
+        turned = [b + t * (1 - 2 * b) for b, t in zip(own_bits, (k % 2, k // 2))]
+        return turned[0] + 2 * turned[1]
+
+    def members(ref, i, g):
+        return ref.at[i, pl.ds(g * per, per)]
+
+    def rows_of(g, first=0, count=None):
+        return pl.ds(pl.multiple_of(g * z.rows + first, 16), z.rows if count is None else count)
+
+    def a2a_send(i, k):
+        g = group_at(k)
+        if k == 0:
+            pltpu.make_async_copy(s_msg.at[i, me], r_msg.at[i, me], rs.at[i, own]).start()
+
+        def go(m, carry):
+            p = g * per + lax.rem(me + m, per)
+            remote(s_msg.at[i, p], r_msg.at[i, me], ss.at[i], rs.at[i, own], (p, core)).start()
             return carry
 
-        lax.fori_loop(1, n, go, 0)
-        remote(r_msg.at[i, me], f_msg.at[i, me], fs.at[i, me], fr.at[i, me], sib).start()
-
-    def a2a_forward(i):
-        def go(j, carry):
-            p = lax.rem(me + n - j, n)
-            remote(
-                s_msg.at[i, p], r_msg.at[i, p], ss.at[i, p], rs.at[i, p], (p, core)
-            ).wait_recv()
-            remote(r_msg.at[i, p], f_msg.at[i, p], fs.at[i, p], fr.at[i, p], sib).start()
-            return carry
-
-        lax.fori_loop(1, n, go, 0)
-
-    def a2a_finish(i):
-        def go(j, carry):
-            remote(r_msg.at[i, j], f_msg.at[i, j], fs.at[i, j], fr.at[i, j], sib).wait()
-            return carry
-
-        lax.fori_loop(0, n, go, 0)
+        lax.fori_loop(1 if k == 0 else 0, per, go, 0)
+
+    def a2a_forward(i, k):
+        g = group_at(k)
+        block = members(r_msg, i, g)
+        remote(block, block, ss.at[i], rs.at[i, g], sib).wait_recv()
+        remote(block, members(f_msg, i, g), fs.at[i], fr.at[i, g], sib).start()
+
+    def a2a_take(i, k):
+        block = members(f_msg, i, group_at(k))
+        remote(block, block, fs.at[i], fr.at[i, group_at(k)], sib).wait_recv()
 
     def a2a_sent(i):
-        def go(j, carry):
-            p = lax.rem(me + j, n)
-            remote(
-                s_msg.at[i, p], r_msg.at[i, me], ss.at[i, p], rs.at[i, me], (p, core)
-            ).wait_send()
-            return carry
-
-        lax.fori_loop(1, n, go, 0)
-
-    def assemble(i, out):
-        tails = []
+        block = s_msg.at[i, pl.ds(0, n - 1)]
+        remote(block, block, ss.at[i], rs.at[i, 0], sib).wait_send()
+        remote(r_msg.at[i], f_msg.at[i], fs.at[i], fr.at[i, 0], sib).wait_send()
+
+    def tail_of(i, src, g):
+        rows = src[i, pl.ds(g * per, per), z.msg - 16 : z.msg, :]
+        return rows.reshape(per * 16, LANE)
+
+    def assemble(i, g, out):
+        q, r = iota((z.gt, per * 16), 0), iota((z.gt, per * 16), 1)
+        base = q // z.tail * 16 + q % z.tail
         for src, at in ((r_msg, mine), (f_msg, other)):
+            tail = tail_of(i, src, g)
             for b in range(z.blocks):
                 lanes = pl.ds(pl.multiple_of(at + b * LANE, LANE), LANE)
                 if z.main:
-                    rows = src[i, :, b * z.main : (b + 1) * z.main, :]
-                    out[0 : z.nm, lanes] = rows.reshape(z.nm, LANE)
-            for g in range(n // BUNCH):
-                tail = tail_of(i, src, g)
-                q, r = iota((z.bt, BUNCH * 16), 0), iota((z.bt, BUNCH * 16), 1)
-                base = q // z.tail * 16 + q % z.tail
-                for b in range(z.blocks):
-                    lanes = pl.ds(pl.multiple_of(at + b * LANE, LANE), LANE)
-                    pick = one(r == base + b * z.tail)
-                    out[z.nm + g * z.bt : z.nm + (g + 1) * z.bt, lanes] = dot(pick, tail).astype(
-                        BF16
-                    )
-
-    def tail_of(i, src, g):
-        rows = src[i, g * BUNCH : (g + 1) * BUNCH, z.msg - 16 : z.msg, :]
-        return rows.reshape(BUNCH * 16, LANE)
-
-    def pack(i, value, extra):
-        if z.main:
-            for b in range(z.blocks):
-                s_msg[i, :, b * z.main : (b + 1) * z.main, :] = value[
-                    0 : z.nm, b * LANE : (b + 1) * LANE
-                ].reshape(n, z.main, LANE)
-        q, r = iota((BUNCH * 16, z.bt), 1), iota((BUNCH * 16, z.bt), 0)
+                    rows = src[i, pl.ds(g * per, per), b * z.main : (b + 1) * z.main, :]
+                    out[rows_of(g, 0, z.gm), lanes] = rows.reshape(z.gm, LANE)
+                pick = one(r == base + b * z.tail)
+                out[rows_of(g, z.gm, z.gt), lanes] = dot(pick, tail).astype(BF16)
+
+    def pack(i, g, value, tail):
+        q, r = iota((per * 16, z.gt), 1), iota((per * 16, z.gt), 0)
         base = q // z.tail * 16 + q % z.tail
-        for g in range(n // BUNCH):
-            tail = None if extra is None else extra[g]
-            for b in range(z.blocks):
-                put = one(r == base + b * z.tail)
-                rows = value[z.nm + g * z.bt : z.nm + (g + 1) * z.bt, b * LANE : (b + 1) * LANE]
-                piece = dot(put, rows)
-                tail = piece if tail is None else tail + piece
-            s_msg[i, g * BUNCH : (g + 1) * BUNCH, z.msg - 16 : z.msg, :] = tail.astype(
-                BF16
-            ).reshape(BUNCH, 16, LANE)
+        for b in range(z.blocks):
+            lanes = slice(b * LANE, (b + 1) * LANE)
+            if z.main:
+                s_msg[i, pl.ds(g * per, per), b * z.main : (b + 1) * z.main, :] = value[
+                    0 : z.gm, lanes
+                ].reshape(per, z.main, LANE)
+            piece = dot(one(r == base + b * z.tail), value[z.gm : z.rows, lanes])
+            tail = piece if tail is None else tail + piece
+        s_msg[i, pl.ds(g * per, per), z.msg - 16 : z.msg, :] = tail.astype(BF16).reshape(
+            per, 16, LANE
+        )
 
     gate_row = 14
 
@@ -335,8 +339,10 @@
 
     def targets(r, j):
         sent = (r >= 0) & (j < z.cap)
-        flat = jnp.where(j < z.main, r * z.main + j, z.nm + r * z.tail + (j - z.main))
-        return sent, jnp.where(sent, flat, -1)
+        g = r // per
+        m = r - g * per
+        flat = jnp.where(j < z.main, m * z.main + j, z.gm + m * z.tail + (j - z.main))
+        return sent, jnp.where(sent, g * z.rows + flat, -1)
 
     sent_row, flat_row = zip(*[targets(r, j) for r, j in zip(r_row, j_row)])
     cols8[...] = jnp.transpose(table)
@@ -347,35 +353,38 @@
 
     slot_id = iota((z.slots, tk), 0)
     onehot[...] = one((slot_id == flat_row[0]) | (slot_id == flat_row[1]))
-    tail_id = iota((BUNCH * 16, tk), 0)
+    tail_id = iota((per * 16, tk), 0)
     tail_row = [
         jnp.where(s & (j >= z.main), r * 16 + (j - z.main), -1000)
         for s, r, j in zip(sent_row, r_row, j_row)
     ]
 
-    def place(src, i, extra):
-        if z.main:
-            for b in range(z.blocks):
-                lanes = pl.ds(pl.multiple_of(mine + b * LANE, LANE), LANE)
-                rows = dot(onehot[0 : z.nm, :], src[:, lanes]).astype(BF16)
-                s_msg[i, :, b * z.main : (b + 1) * z.main, :] = rows.reshape(n, z.main, LANE)
-        for g in range(n // BUNCH):
-            tail = None if extra is None else extra[g]
-            for b in range(z.blocks):
-                lanes = pl.ds(pl.multiple_of(mine + b * LANE, LANE), LANE)
-                at = b * z.tail - g * BUNCH * 16
-                put = one((tail_id == tail_row[0] + at) | (tail_id == tail_row[1] + at))
-                piece = dot(put, src[:, lanes])
-                tail = piece if tail is None else tail + piece
-            s_msg[i, g * BUNCH : (g + 1) * BUNCH, z.msg - 16 : z.msg, :] = tail.astype(
-                BF16
-            ).reshape(BUNCH, 16, LANE)
+    def place(src, i, g, tail):
+        first = g * (per * 16)
+        for b in range(z.blocks):
+            lanes = pl.ds(pl.multiple_of(mine + b * LANE, LANE), LANE)
+            rows = src[:, lanes]
+            if z.main:
+                main = dot(onehot[rows_of(g, 0, z.gm), :], rows).astype(BF16)
+                s_msg[i, pl.ds(g * per, per), b * z.main : (b + 1) * z.main, :] = main.reshape(
+                    per, z.main, LANE
+                )
+            at = b * z.tail - first
+            put = one((tail_id == tail_row[0] + at) | (tail_id == tail_row[1] + at))
+            piece = dot(put, rows)
+            tail = piece if tail is None else tail + piece
+        s_msg[i, pl.ds(g * per, per), z.msg - 16 : z.msg, :] = tail.astype(BF16).reshape(
+            per, 16, LANE
+        )
 
     upk[tok // 16 * 16 :, :] = jnp.zeros((tk - tok // 16 * 16, width), BF16)
+    tokens_in[1].wait()
     upk[0:tok, :] = grad_out_ref[...]
-    place(upk, 0, None)
+    for g in range(GROUPS):
+        place(upk, 0, g, None)
 
     xf[tok // 8 * 8 :, :] = jnp.zeros((tp - tok // 8 * 8, width), F32)
+    tokens_in[0].wait()
     xf[0:tok, :] = tokens_ref[...].astype(F32)
     normal, inverse1 = norm_parts(xf[...])
     normal1[...] = normal
@@ -383,7 +392,8 @@
     n1[0:tp, :] = (normal * row_of(ln1g_ref) + row_of(ln1b_ref)).astype(BF16)
 
     pl.semaphore_wait(barrier, n)
-    a2a_send(0)
+    for k in SEND_ORDER:
+        a2a_send(0, k)
 
     weights[0].wait()
     for c, (dst, bias) in enumerate(((q_s, bqv_ref[0:1, :]), (k_s, None), (v_s, bqv_ref[1:2, :]))):
@@ -411,7 +421,7 @@
     mix[tp:, :] = jnp.zeros((tk - tp, hw), BF16)
     weights[1].wait()
     part[...] = dot(mix[0:tp, :], wo[...])
-    swap = remote(part, part_in, hs.at[0], hr.at[0], sib)
+    swap = remote(part, part_in, hs.at[2, 0], hr.at[2, 0], sib)
     swap.start()
     n1t[...] = jnp.transpose(n1[...])
     swap.wait()
@@ -439,100 +449,115 @@
     gate = [cols8[0:tp, k : k + 1] for k in range(2)]
 
     slot_lane = iota((tk, LANE), 1)
-    numbers = []
     pad_col = [
         jnp.concatenate([j, jnp.full((tk - tp, 1), -1, jnp.int32)], axis=0) for j in j_col
     ]
-    for g in range(n // BUNCH):
+    at_slot = [one(slot_lane == j) for j in pad_col]
+    halves = [split(g) for g in gate_rows]
+    for k in SEND_ORDER:
+        g = group_at(k)
         number = None
-        for k in range(2):
-            high, low = split(gate_rows[k])
-            at = r_row[k] * 16 + (gate_row - g * BUNCH * 16)
+        for c in range(2):
+            high, low = halves[c]
+            at = r_row[c] * 16 + (gate_row - g * (per * 16))
             lift = jnp.where(
-                sent_row[k] & (tail_id == at), high.astype(F32), 0.0
-            ) + jnp.where(sent_row[k] & (tail_id == at + 1), low.astype(F32), 0.0)
-            piece = dot(lift.astype(BF16), one(slot_lane == pad_col[k]))
+                sent_row[c] & (tail_id == at), high.astype(F32), 0.0
+            ) + jnp.where(sent_row[c] & (tail_id == at + 1), low.astype(F32), 0.0)
+            piece = dot(lift.astype(BF16), at_slot[c])
             number = piece if number is None else number + piece
-        numbers.append(number)
-    place(n2, 1, numbers)
-    a2a_send(1)
-
-    a2a_forward(0)
-    a2a_finish(0)
-    assemble(0, u_s)
+        place(n2, 1, g, number)
+        a2a_send(1, k)
+
+    for k in range(GROUPS):
+        a2a_forward(0, k)
+    for k in range(GROUPS):
+        a2a_take(0, k)
+        assemble(0, group_at(k), u_s)
     weights[2].wait()
     gh[...] = dot_bt(u_s[...], wout[...])
 
     weights[3].wait()
-    a2a_forward(1)
-    a2a_finish(1)
-    assemble(1, x_s)
-
-    def numbered(rows, per, first):
-        q, r = iota((rows, BUNCH * 16), 0), iota((rows, BUNCH * 16), 1)
-        pick = r == q // per * 16 + gate_row
-        lane = iota((rows, LANE), 1) == iota((rows, LANE), 0) % per + first
-        return pick, r == q // per * 16 + gate_row + 1, lane
-
-    parts = [(0, BUNCH * z.main, z.main, 0)] if z.main else []
-    parts += [(z.nm, z.bt, z.tail, z.main)]
-    for g in range(n // BUNCH):
+    parts = [(0, z.gm, z.main, 0)] if z.main else []
+    parts += [(z.gm, z.gt, z.tail, z.main)]
+    step = 16
+
+    def activate(g):
+        def go(i, carry):
+            here = pl.ds(pl.multiple_of(i * step, step), step)
+            rows = pl.ds(pl.multiple_of(g * z.rows + i * step, step), step)
+            v = pre[here, :] + bin_ref[...]
+            v2 = v * v
+            s = 0.5 + 0.5 * jnp.tanh(v * (ROOT + (ROOT * CUBE) * v2))
+            act = v * s
+            back = s + act * (1.0 - s) * (2.0 * ROOT + (6.0 * ROOT * CUBE) * v2)
+            up = gh[rows, :]
+            hid[rows, :] = act.astype(BF16)
+            gp[rows, :] = (gcol_s[rows, :] * up * back).astype(BF16)
+            ggv[rows, :] = jnp.sum(up * act, axis=-1, keepdims=True)
+            return carry
+
+        lax.fori_loop(0, z.rows // step, go, 0)
+
+    bias_half = bout_ref[:, pl.ds(mine, half)]
+
+    def swap_of(j, k):
+        return remote(half_out.at[j, k], half_in.at[j, k], hs.at[j, k], hr.at[j, k], sib)
+
+    def slots_in(k):
+        g = group_at(k)
+        a2a_take(1, k)
+        assemble(1, g, x_s)
         tail = tail_of(1, r_msg, g)
-        for at, rows, per, first in parts:
-            high, low, lane = numbered(rows, per, first)
-            picked = dot(one(high | low), tail)
-            gcol_s[at + g * rows : at + (g + 1) * rows, :] = jnp.sum(
-                jnp.where(lane, picked, 0.0), axis=-1, keepdims=True
+        for at, rows, each, first in parts:
+            q, r = iota((rows, per * 16), 0), iota((rows, per * 16), 1)
+            number = r - q // each * 16
+            pick = one((number == gate_row) | (number == gate_row + 1))
+            lane = iota((rows, LANE), 1) == iota((rows, LANE), 0) % each + first
+            gcol_s[rows_of(g, at, rows), :] = jnp.sum(
+                jnp.where(lane, dot(pick, tail), 0.0), axis=-1, keepdims=True
             )
-    pre[...] = dot(x_s[...], win[...])
-    step = 16
-
-    def activate(i, carry):
-        rows = pl.ds(pl.multiple_of(i * step, step), step)
-        v = pre[rows, :] + bin_ref[...]
-        v2 = v * v
-        t = jnp.tanh(ROOT * v * (1.0 + CUBE * v2))
-        half_sum = 0.5 + 0.5 * t
-        act = v * half_sum
-        back = half_sum + (0.5 * ROOT) * v * (1.0 - t * t) * (1.0 + (3.0 * CUBE) * v2)
-        g = gh[rows, :]
-        hid[rows, :] = act.astype(BF16)
-        gp[rows, :] = (gcol_s[rows, :] * g * back).astype(BF16)
-        ggv[rows, :] = jnp.sum(g * act, axis=-1, keepdims=True)
-        return carry
-
-    lax.fori_loop(0, z.slots // step, activate, 0)
-
-    half_out[0] = dot_bt(gp[...], win[pl.ds(other, half), :])
-    swap = remote(half_out.at[0], half_in.at[0], hs.at[1], hr.at[1], sib)
-    swap.start()
-    own = dot_bt(gp[...], win[pl.ds(mine, half), :])
-    bias_half = bout_ref[:, pl.ds(mine, half)]
-    gg = ggv[...] + jnp.sum(
-        u_s[:, pl.ds(mine, half)].astype(F32) * bias_half, axis=-1, keepdims=True
-    )
-    numbers = []
-    for g in range(n // BUNCH):
+        pre[...] = dot(x_s[rows_of(g), :], win[...])
+        activate(g)
+        back = gp[rows_of(g), :]
+        half_out[0, k] = dot_bt(back, win[pl.ds(other, half), :]).astype(BF16)
+        swap_of(0, k).start()
+        half_own[k] = dot_bt(back, win[pl.ds(mine, half), :])
+
+    def slots_back(k):
+        g = group_at(k)
+        gg = ggv[rows_of(g), :] + jnp.sum(
+            u_s[rows_of(g), pl.ds(mine, half)].astype(F32) * bias_half, axis=-1, keepdims=True
+        )
         number = None
-        for at, rows, per, first in parts:
-            q, r = iota((BUNCH * 16, rows), 1), iota((BUNCH * 16, rows), 0)
-            lane = iota((rows, LANE), 1) == iota((rows, LANE), 0) % per + first
-            high, low = split(jnp.where(lane, gg[at + g * rows : at + (g + 1) * rows, :], 0.0))
-            piece = dot(one(r == q // per * 16 + gate_row), high) + dot(
-                one(r == q // per * 16 + gate_row + 1), low
-            )
+        for at, rows, each, first in parts:
+            q, r = iota((per * 16, rows), 1), iota((per * 16, rows), 0)
+            lane = iota((rows, LANE), 1) == iota((rows, LANE), 0) % each + first
+            high, low = split(jnp.where(lane, gg[at : at + rows, :], 0.0))
+            line = r - q // each * 16
+            piece = dot(one(line == gate_row), high) + dot(one(line == gate_row + 1), low)
             number = piece if number is None else number + piece
-        numbers.append(number)
-    swap.wait()
-    pack(2, (own + half_in[0]).astype(BF16), numbers)
-    a2a_send(2)
-
-    half_out[1] = dot(hid[...], wout[:, pl.ds(other, half)])
-    swap = remote(half_out.at[1], half_in.at[1], hs.at[2], hr.at[2], sib)
-    swap.start()
-    own = dot(hid[...], wout[:, pl.ds(mine, half)]) + bias_half
-    swap.wait()
-    pack(3, (own + half_in[1]).astype(BF16), None)
+        swap_of(0, k).wait()
+        pack(2, g, (half_own[k] + half_in[0, k].astype(F32)).astype(BF16), number)
+        a2a_send(2, k)
+
+    a2a_forward(1, 0)
+    a2a_forward(1, 1)
+    for k in range(GROUPS):
+        slots_in(k)
+        if k + 2 < GROUPS:
+            a2a_forward(1, k + 2)
+        if k > 0:
+            slots_back(k - 1)
+    slots_back(GROUPS - 1)
+
+    for k in range(GROUPS):
+        act = hid[rows_of(group_at(k)), :]
+        half_out[1, k] = dot(act, wout[:, pl.ds(other, half)]).astype(BF16)
+        swap_of(1, k).start()
+        half_own[k] = dot(act, wout[:, pl.ds(mine, half)]) + bias_half
+    for k in range(GROUPS):
+        swap_of(1, k).wait()
+        pack(3, group_at(k), (half_own[k] + half_in[1, k].astype(F32)).astype(BF16), None)
 
     sg[...] = (gcol_s[...] * u_s[...].astype(F32)).astype(BF16)
     x_t[...] = jnp.transpose(x_s[...])
@@ -549,21 +574,28 @@
 
     flat_id = iota((tp, z.slots), 1)
     back_one = [one(flat_id == f) for f in flat_col]
-    a2a_forward(2)
-    a2a_send(3)
-    a2a_finish(2)
-    assemble(2, y_s)
-    tail_lane = iota((tp, BUNCH * 16), 1)
-    grad_gate = []
-    for k in range(2):
-        row = None
-        for g in range(n // BUNCH):
-            at = r_col[k] * 16 + (gate_row - g * BUNCH * 16)
-            pick = one(sent_col[k] & ((tail_lane == at) | (tail_lane == at + 1)))
-            piece = dot(pick, tail_of(2, r_msg, g)) + dot(pick, tail_of(2, f_msg, g))
-            row = piece if row is None else row + piece
-        row = jnp.where(iota((tp, LANE), 1) == j_col[k], row, 0.0)
-        grad_gate.append(jnp.sum(row, axis=-1, keepdims=True))
+    for k in range(GROUPS):
+        a2a_forward(2, k)
+    for k in SEND_ORDER:
+        a2a_send(3, k)
+    tail_lane = iota((tp, per * 16), 1)
+    number = [None, None]
+    for k in range(GROUPS):
+        g = group_at(k)
+        a2a_take(2, k)
+        assemble(2, g, y_s)
+        tails = [tail_of(2, r_msg, g), tail_of(2, f_msg, g)]
+        for c in range(2):
+            at = r_col[c] * 16 + (gate_row - g * (per * 16))
+            pick = one(sent_col[c] & ((tail_lane == at) | (tail_lane == at + 1)))
+            piece = dot(pick, tails[0]) + dot(pick, tails[1])
+            number[c] = piece if number[c] is None else number[c] + piece
+    grad_gate = [
+        jnp.sum(
+            jnp.where(iota((tp, LANE), 1) == j_col[c], number[c], 0.0), axis=-1, keepdims=True
+        )
+        for c in range(2)
+    ]
     mean_gate = gate[0] * grad_gate[0] + gate[1] * grad_gate[1]
     e_pad = up_to(z.experts, LANE)
     e_lane = iota((tp, e_pad), 1)
@@ -617,7 +649,7 @@
         src, bufs, _, rows = chain_of(g)
         peer, give, _, size = groups[g][0][s]
         return remote(
-            region(src, give, size, rows), bufs[s], cs.at[g, s], cr.at[g, s], (peer, core)
+            region(src, give, size, rows), bufs[s], cs.at[g], cr.at[g, s], (peer, core)
         )
 
     def rs_add(g, s, at, count, dst):
@@ -648,14 +680,14 @@
         _, _, out, rows = chain_of(g)
         peer, _, keep, size = groups[g][0][s]
         piece = region(out, keep, size, rows)
-        return remote(piece, piece, as_.at[g, s], ar.at[g, s], (peer, core))
+        return remote(piece, piece, as_.at[g], ar.at[g, s], (peer, core))
 
     def ag_step(g, s):
         _, _, out, rows = chain_of(g)
         peer, give, _, size = groups[g][0][s]
         ag_copy(g, s).wait_send()
         piece = region(out, give, size, rows)
-        remote(piece, piece, as_.at[g, s], ar.at[g, s], (peer, core)).wait_recv()
+        remote(piece, piece, as_.at[g], ar.at[g, s], (peer, core)).wait_recv()
         if s > 0:
             ag_copy(g, s - 1).start()
 
@@ -707,7 +739,7 @@
         piece = dot_bt(gpr[0:tp, c * hw : (c + 1) * hw], wqkv[c])
         head_part = piece if head_part is None else head_part + piece
     gn_out[...] = head_part.astype(BF16)
-    swap = remote(gn_out, gn_in, hs.at[3], hr.at[3], sib)
+    swap = remote(gn_out, gn_in, hs.at[2, 1], hr.at[2, 1], sib)
     swap.start()
     smallf[ne + 5 : ne + 6, 0:hw] = jnp.sum(gpr[:, 0:hw].astype(F32), axis=0, keepdims=True)
     smallf[ne + 6 : ne + 7, 0:hw] = jnp.sum(
@@ -719,7 +751,10 @@
     smallf[ne : ne + 1, :] = jnp.sum(grad_n1 * normal, axis=0, keepdims=True)
     smallf[ne + 1 : ne + 2, :] = jnp.sum(grad_n1, axis=0, keepdims=True)
     back = gm[...] + norm_backward(grad_n1, normal, inverse1, row_of(ln1g_ref))
-    o_gtok[...] = back[0:tok, :]
+    gtok_out[...] = back[0:tok, :]
+    copy = pltpu.make_async_copy(gtok_out, o_gtok, osem.at[4])
+    copy.start()
+    stores.append(copy)
     used = z.small_rows * (width // LANE)
     for b in range(width // LANE):
         chain_small[b * z.small_rows : (b + 1) * z.small_rows, :] = smallf[
@@ -729,12 +764,17 @@
         chain_small[used:, :] = jnp.zeros((n * z.small - used, LANE), BF16)
     rs_copy(n_main, 0).start()
 
-    a2a_forward(3)
-    a2a_finish(3)
-    assemble(3, y_s)
+    for k in range(GROUPS):
+        a2a_forward(3, k)
+    for k in range(GROUPS):
+        a2a_take(3, k)
+        assemble(3, group_at(k), y_s)
     branch = gate[0] * dot(back_one[0], y_s[...]) + gate[1] * dot(back_one[1], y_s[...])
     output = mid[...] + branch
-    o_tok[...] = output[0:tok, :].astype(BF16)
+    tok_out[...] = output[0:tok, :].astype(BF16)
+    copy = pltpu.make_async_copy(tok_out, o_tok, osem.at[5])
+    copy.start()
+    stores.append(copy)
     lane_id = iota((1, LANE), 1)
     x_all = xf[...]
     line = jnp.zeros((1, LANE), F32)
@@ -752,7 +792,7 @@
 
     def stat_go(j, carry):
         p = lax.rem(me + j, n)
-        remote(stat.at[me], stat.at[me], sts.at[p], str_.at[me], (p, core)).start()
+        remote(stat.at[me], stat.at[me], st.at[0], st.at[1], (p, core)).start()
         return carry
 
     lax.fori_loop(1, n, stat_go, 0)
@@ -761,13 +801,8 @@
         for g in range(n_main + 1):
             rs_step(g, s)
 
-    def stat_wait(j, carry):
-        p = lax.rem(me + j, n)
-        remote(stat.at[me], stat.at[me], sts.at[p], str_.at[me], (p, core)).wait_send()
-        remote(stat.at[p], stat.at[p], sts.at[p], str_.at[p], (p, core)).wait_recv()
-        return carry
-
-    lax.fori_loop(1, n, stat_wait, 0)
+    block = stat.at[pl.ds(0, n - 1)]
+    remote(block, block, st.at[0], st.at[1], sib).wait()
     totals = jnp.sum(stat[...], axis=0)
     count = jnp.sum(jnp.where(iota((8, LANE), 1) == 4, totals, 0.0), axis=-1, keepdims=True)
     o_rms[...] = jnp.sqrt(totals / (count * width))
@@ -776,7 +811,7 @@
         for g in range(n_main + 1):
             ag_step(g, s)
     for g in range(n_main):
-        copy = pltpu.make_async_copy(chain_a.at[g], o_red.at[g], osem.at[4 + g])
+        copy = pltpu.make_async_copy(chain_a.at[g], o_red.at[g], osem.at[6 + g])
         copy.start()
         stores.append(copy)
     for b in range(width // LANE):
@@ -936,6 +971,10 @@
     groups = z.chains
     V = pltpu.VMEM
     scratch = [
+        V((tok, width), BF16),
+        V((tok, width), BF16),
+        V((tok, width), BF16),
+        V((tok, width), F32),
         V((3, width, hw), BF16),
         V((hw, width), BF16),
         V((width, ff), BF16),
@@ -962,7 +1001,7 @@
         V((z.slots, width), BF16),
         V((z.slots, width), BF16),
         V((z.slots, ff), F32),
-        V((z.slots, ff), F32),
+        V((z.rows, ff), F32),
         V((z.slots, ff), BF16),
         V((z.slots, ff), BF16),
         V((z.slots, width), BF16),
@@ -970,8 +1009,9 @@
         V((ff, z.slots), BF16),
         V((z.slots, 1), F32),
         V((z.slots, 1), F32),
-        V((2, z.slots, z.half), F32),
-        V((2, z.slots, z.half), F32),
+        V((2, GROUPS, z.rows, z.half), BF16),
+        V((2, GROUPS, z.rows, z.half), BF16),
+        V((GROUPS, z.rows, z.half), F32),
         V((tp, width), F32),
         V((tk, width), BF16),
         V((tp, hw), BF16),
@@ -991,20 +1031,19 @@
     scratch += [
         V((groups, n * z.chunk, LANE), BF16),
         V((n * z.small, LANE), BF16),
+        DMA((6,)),
+        DMA((6 + groups,)),
+        DMA((3, GROUPS)),
+        DMA((3, GROUPS)),
         DMA((4,)),
-        DMA((4 + groups,)),
+        DMA((4, GROUPS)),
         DMA((4,)),
-        DMA((4,)),
-        DMA((4, n)),
-        DMA((4, n)),
-        DMA((4, n)),
-        DMA((4, n)),
+        DMA((4, GROUPS)),
+        DMA((groups + 1,)),
         DMA((groups + 1, nbits)),
+        DMA((groups + 1,)),
         DMA((groups + 1, nbits)),
-        DMA((groups + 1, nbits)),
-        DMA((groups + 1, nbits)),
-        DMA((n,)),
-        DMA((n,)),
+        DMA((2,)),
     ]
     row = lambda v: v.reshape(1, -1)
     outs = pl.pallas_call(
@@ -1022,9 +1061,10 @@
             shape((1, width), F32),
             shape((8, LANE), F32),
         ),
-        in_specs=[vmem] * 7
+        in_specs=[any_] * 2
+        + [vmem] * 5
         + [any_, vmem, any_, vmem, vmem, vmem, vmem, any_, vmem, any_, vmem],
-        out_specs=(vmem, vmem, any_, any_, any_, any_, any_, vmem, vmem, vmem, vmem),
+        out_specs=(any_,) * 7 + (vmem,) * 4,
         scratch_shapes=scratch,
         compiler_params=pltpu.CompilerParams(
             collective_id=0, has_side_effects=True, vmem_limit_bytes=60 * 2**20

time: 126 us -> 118 us (0.937)
  Pallas kernels: 125 us -> 117 us
    pallas_call x1, Pallas kernels: 115 us -> 107 us  [per_device(): pl.pallas_call(functools.partial(mega_kernel, z), out_shape=(shape((tok,...]
where the time goes in v3:
time: 118 us
  Pallas kernels  117 us (99%)
    pallas_call x1, Pallas kernels, per_device(): pl.pallas_call(functools.partial(mega_kernel, z), out_shape=(shape((tok,...  107 us
    pallas_call x1, Pallas kernels, per_device(): pl.pallas_call(functools.partial(last_kernel, z), out_shape=(shape((tok,...  10.6 us

profile of v3, /device:TPU:0, one launch (start us, length us, event | category | flops | bytes accessed | tf_op | source)
XLA Modules:
  0.0 118.1 jit_solution(14348924612024732453)
XLA Ops:
  0.7 106.6 %shard_map.297 = (bf16[197,768]{1,0:T(8,128)(2,1)}, f32[197,768]{1,0:T(8,128)}, bf16[768,576]{1,0:T(8,128)(2,1)}, bf16[576,768]{1,0:T(8,128)(2,1)}, bf16[1536,57...) custom-call(bf16[197,768]{1,0:T(8,128)(2,1)} %tokens_hbm.1, ...), custom_call_target="tpu_custom_call" | custom-call | tf_op jit(solution)/shard_map/pallas_call | solution.py:1049
  107.3 10.6 %shard_map.298 = (bf16[197,768]{1,0:T(8,128)(2,1)}, f32[197,768]{1,0:T(8,128)}, f32[768]{0:T(1024)}, f32[768]{0:T(1024)}, f32[3,768,384]{2,1,0:T(8,128)}, /*inde...) custom-call(bf16[197,768]{1,0:T(8,128)(2,1)} %get-tuple-element.43.i, ...), custom_call_target="tpu_custom_call" | custom-call | tf_op jit(solution)/shard_map/pallas_call | solution.py:1095

commit v4 on v3

--- a/solution.py
+++ b/solution.py
@@ -15,6 +15,37 @@
 ROOT = math.sqrt(2.0 / math.pi)
 CUBE = 0.044715
 GROUPS = 4
+LAST = 5
+ORDERS = (
+    (0, 1, 3, 2),
+    (1, 3, 0, 2),
+    (2, 0, 1, 3),
+    (0, 2, 1, 3),
+    (1, 0, 3, 2),
+    (2, 1, 0, 3),
+    (3, 0, 1, 2),
+    (2, 1, 0, 3),
+    (1, 0, 2, 3),
+    (1, 3, 0, 2),
+    (0, 1, 2, 3),
+    (0, 3, 1, 2),
+)
+STEPS = (
+    (5, 0, 0), (5, 1, 0), (5, 2, 0), (5, 4, 0), (5, 12, 0), (5, 3, 0), (5, 8, 0), (5, 5, 0),
+    (5, 9, 0), (5, 10, 0), (5, 11, 0), (5, 0, 1), (5, 7, 0), (5, 6, 0), (5, 12, 1), (5, 2, 1),
+    (5, 4, 1), (5, 1, 1), (5, 3, 1), (5, 8, 1), (5, 5, 1), (5, 10, 1), (5, 7, 1), (5, 9, 1),
+    (5, 12, 2), (5, 6, 1), (5, 2, 2), (5, 1, 2), (5, 0, 2), (5, 3, 2), (5, 5, 2), (5, 4, 2),
+    (5, 11, 1), (5, 8, 2), (5, 7, 2), (5, 12, 3), (5, 10, 2), (5, 9, 2), (5, 6, 2), (5, 2, 3),
+    (5, 1, 3), (5, 0, 3), (5, 3, 3), (5, 5, 3), (5, 4, 3), (5, 11, 2), (5, 12, -4), (5, 8, 3),
+    (5, 7, 3), (5, 9, 3), (5, 10, 3), (5, 6, 3), (5, 2, -4), (5, 1, -4), (5, 0, -4), (5, 3, -4),
+    (5, 12, -3), (5, 5, -4), (5, 4, -4), (5, 11, 3), (5, 8, -4), (5, 7, -4), (5, 9, -4),
+    (5, 10, -4), (5, 6, -4), (5, 2, -3), (5, 1, -3), (5, 5, -3), (5, 12, -2), (5, 3, -3),
+    (5, 11, -4), (5, 0, -3), (5, 7, -3), (5, 4, -3), (5, 6, -3), (5, 9, -3), (5, 8, -3),
+    (5, 10, -3), (5, 12, -1), (5, 2, -2), (5, 5, -2), (5, 1, -2), (5, 11, -3), (5, 3, -2),
+    (5, 0, -2), (5, 9, -2), (5, 4, -2), (5, 6, -2), (5, 7, -2), (5, 8, -2), (5, 10, -2),
+    (5, 11, -2), (5, 3, -1), (5, 1, -1), (5, 0, -1), (5, 2, -1), (5, 5, -1), (5, 10, -1),
+    (5, 9, -1), (5, 4, -1), (5, 11, -1), (5, 8, -1), (5, 6, -1), (5, 7, -1),
+)
 SEND_ORDER = (0, 2, 1, 3)
 TILE = 256
 MESH = pl.DeviceIdType.MESH
@@ -108,7 +139,7 @@
         self.slots = n * self.cap
         self.bits = [1 << i for i in range(n.bit_length() - 1)]
         self.pack_rows = 4 * heads_width * width // LANE
-        self.chains = 6
+        self.chains = 12 if n <= 16 else 6
         self.chain_rows = self.pack_rows // self.chains
         self.chunk = up_to(up_to(self.chain_rows, n) // n, 16)
         self.small_rows = up_to(experts + 7, 16)
@@ -119,34 +150,44 @@
             raise ValueError("unsupported sizes")
 
 
-def chain_orders(bits):
-    k = len(bits)
-    if k < 3:
-        return [bits] * 6
+def chain_orders(bits, chains):
+    if len(bits) == 4 and chains == len(ORDERS):
+        return [[bits[i] for i in order] for order in ORDERS]
+    if len(bits) < 3:
+        return [bits] * chains
     order = ((0, 1, 2), (1, 2, 0), (2, 0, 1), (0, 2, 1), (1, 0, 2), (2, 1, 0))
-    return [[bits[i] for i in head] + bits[3:] for head in order]
+    return [[bits[i] for i in order[c % 6]] + bits[3:] for c in range(chains)]
+
+
+def chain_steps(bits, chains):
+    if len(bits) == 4 and chains == len(ORDERS):
+        return STEPS
+    steps = [(LAST, c, s) for s in range(len(bits)) for c in range(chains + 1)]
+    return steps + [
+        (LAST, c, -1 - s) for s in range(len(bits) - 1, -1, -1) for c in range(chains + 1)
+    ]
 
 
 def mega_kernel(
     z,
     tokens_hbm,
     grad_out_hbm,
-    valid_ref,
-    routes_ref,
-    slots_ref,
-    ln1g_ref,
-    ln1b_ref,
+    valid_hbm,
+    routes_hbm,
+    slots_hbm,
+    ln1g_hbm,
+    ln1b_hbm,
     wqkv_hbm,
-    bqv_ref,
+    bqv_hbm,
     wo_hbm,
-    bo_ref,
-    ln2g_ref,
-    ln2b_ref,
-    router_ref,
+    bo_hbm,
+    ln2g_hbm,
+    ln2b_hbm,
+    router_hbm,
     win_hbm,
-    bin_ref,
+    bin_hbm,
     wout_hbm,
-    bout_ref,
+    bout_hbm,
     o_tok,
     o_gtok,
     o_x,
@@ -160,6 +201,18 @@
     o_rms,
     tokens_ref,
     grad_out_ref,
+    valid_ref,
+    routes_ref,
+    slots_ref,
+    ln1g_ref,
+    ln1b_ref,
+    bqv_ref,
+    bo_ref,
+    ln2g_ref,
+    ln2b_ref,
+    router_ref,
+    bin_ref,
+    bout_ref,
     tok_out,
     gtok_out,
     wqkv,
@@ -199,6 +252,8 @@
     half_out,
     half_in,
     half_own,
+    whole,
+    win_t,
     gm,
     ag,
     dm,
@@ -242,7 +297,26 @@
         pltpu.make_async_copy(a, b, wsem.at[4 + i])
         for i, (a, b) in enumerate(((tokens_hbm, tokens_ref), (grad_out_hbm, grad_out_ref)))
     ]
-    for copy in tokens_in[::-1]:
+    small_in = [
+        pltpu.make_async_copy(a, b, wsem.at[6 + i])
+        for i, (a, b) in enumerate(
+            (
+                (valid_hbm, valid_ref),
+                (routes_hbm, routes_ref),
+                (slots_hbm, slots_ref),
+                (ln1g_hbm, ln1g_ref),
+                (ln1b_hbm, ln1b_ref),
+                (bqv_hbm, bqv_ref),
+                (bo_hbm, bo_ref),
+                (ln2g_hbm, ln2g_ref),
+                (ln2b_hbm, ln2b_ref),
+                (router_hbm, router_ref),
+                (bin_hbm, bin_ref),
+                (bout_hbm, bout_ref),
+            )
+        )
+    ]
+    for copy in small_in + tokens_in[::-1]:
         copy.start()
     weights = [
         pltpu.make_async_copy(a, b, wsem.at[i])
@@ -328,6 +402,8 @@
 
     gate_row = 14
 
+    for copy in small_in:
+        copy.wait()
     rows8[...] = jnp.full(rows8.shape, -1.0, F32)
     rows8[0:2, 0:tok] = routes_ref[...].astype(F32)
     rows8[2:4, 0:tok] = slots_ref[...].astype(F32)
@@ -466,7 +542,8 @@
             piece = dot(lift.astype(BF16), at_slot[c])
             number = piece if number is None else number + piece
         place(n2, 1, g, number)
-        a2a_send(1, k)
+        if k < GROUPS - 1:
+            a2a_send(1, k)
 
     for k in range(GROUPS):
         a2a_forward(0, k)
@@ -476,7 +553,10 @@
     weights[2].wait()
     gh[...] = dot_bt(u_s[...], wout[...])
 
+    a2a_send(1, GROUPS - 1)
     weights[3].wait()
+    win_t[...] = jnp.transpose(win[...])
+
     parts = [(0, z.gm, z.main, 0)] if z.main else []
     parts += [(z.gm, z.gt, z.tail, z.main)]
     step = 16
@@ -485,18 +565,24 @@
         def go(i, carry):
             here = pl.ds(pl.multiple_of(i * step, step), step)
             rows = pl.ds(pl.multiple_of(g * z.rows + i * step, step), step)
-            v = pre[here, :] + bin_ref[...]
-            v2 = v * v
-            s = 0.5 + 0.5 * jnp.tanh(v * (ROOT + (ROOT * CUBE) * v2))
-            act = v * s
-            back = s + act * (1.0 - s) * (2.0 * ROOT + (6.0 * ROOT * CUBE) * v2)
-            up = gh[rows, :]
-            hid[rows, :] = act.astype(BF16)
-            gp[rows, :] = (gcol_s[rows, :] * up * back).astype(BF16)
-            ggv[rows, :] = jnp.sum(up * act, axis=-1, keepdims=True)
+            gate_of = jnp.broadcast_to(gcol_s[rows, :], (step, LANE))
+            total = jnp.zeros((step, LANE), F32)
+            for b in range(z.ff // LANE):
+                lanes = slice(b * LANE, (b + 1) * LANE)
+                v = pre[here, lanes] + bin_ref[:, lanes]
+                v2 = v * v
+                s = 0.5 + 0.5 * jnp.tanh(v * (ROOT + (ROOT * CUBE) * v2))
+                act = v * s
+                back = s + act * (1.0 - s) * (2.0 * ROOT + (6.0 * ROOT * CUBE) * v2)
+                up = gh[rows, lanes]
+                hid[rows, lanes] = act.astype(BF16)
+                gp[rows, lanes] = (gate_of * up * back).astype(BF16)
+                total = total + up * act
+            ggv[rows, :] = total
             return carry
 
-        lax.fori_loop(0, z.rows // step, go, 0)
+        count = z.rows // step
+        lax.fori_loop(0, count, go, 0, unroll=3 if count % 3 == 0 else 2)
 
     bias_half = bout_ref[:, pl.ds(mine, half)]
 
@@ -519,13 +605,14 @@
         pre[...] = dot(x_s[rows_of(g), :], win[...])
         activate(g)
         back = gp[rows_of(g), :]
-        half_out[0, k] = dot_bt(back, win[pl.ds(other, half), :]).astype(BF16)
+        whole[...] = dot(back, win_t[...])
+        half_out[0, k] = whole[:, pl.ds(other, half)].astype(BF16)
         swap_of(0, k).start()
-        half_own[k] = dot_bt(back, win[pl.ds(mine, half), :])
+        half_own[k] = whole[:, pl.ds(mine, half)]
 
     def slots_back(k):
         g = group_at(k)
-        gg = ggv[rows_of(g), :] + jnp.sum(
+        gg = jnp.sum(ggv[rows_of(g), :], axis=-1, keepdims=True) + jnp.sum(
             u_s[rows_of(g), pl.ds(mine, half)].astype(F32) * bias_half, axis=-1, keepdims=True
         )
         number = None
@@ -542,19 +629,23 @@
 
     a2a_forward(1, 0)
     a2a_forward(1, 1)
-    for k in range(GROUPS):
-        slots_in(k)
-        if k + 2 < GROUPS:
-            a2a_forward(1, k + 2)
-        if k > 0:
-            slots_back(k - 1)
-    slots_back(GROUPS - 1)
+    slots_in(0)
+    slots_in(1)
+    slots_back(0)
+    a2a_forward(1, 2)
+    slots_back(1)
+    slots_in(2)
+    a2a_forward(1, 3)
+    slots_back(2)
+    slots_in(3)
+    slots_back(3)
 
     for k in range(GROUPS):
         act = hid[rows_of(group_at(k)), :]
-        half_out[1, k] = dot(act, wout[:, pl.ds(other, half)]).astype(BF16)
+        whole[...] = dot(act, wout[...])
+        half_out[1, k] = whole[:, pl.ds(other, half)].astype(BF16)
         swap_of(1, k).start()
-        half_own[k] = dot(act, wout[:, pl.ds(mine, half)]) + bias_half
+        half_own[k] = whole[:, pl.ds(mine, half)] + bias_half
     for k in range(GROUPS):
         swap_of(1, k).wait()
         pack(3, group_at(k), (half_own[k] + half_in[1, k].astype(F32)).astype(BF16), None)
@@ -626,7 +717,7 @@
     smallf[ne + 4 : ne + 5, :] = jnp.sum(ag[...].astype(F32), axis=0, keepdims=True)
 
     groups = []
-    for order in chain_orders(z.bits) + [z.bits]:
+    for order in chain_orders(z.bits, z.chains) + [z.bits]:
         start, size, steps = 0, n, []
         for b in order:
             bit = lax.rem(me // b, 2)
@@ -662,7 +753,7 @@
             dst[here, :] = (src[here, :].astype(F32) + bufs[s][there, :].astype(F32)).astype(BF16)
             return carry
 
-        lax.fori_loop(0, count, go, 0)
+        lax.fori_loop(0, count, go, 0, unroll=2 if count % 2 == 0 else 1)
 
     def rs_step(g, s):
         src, _, out, _ = chain_of(g)
@@ -691,6 +782,16 @@
         if s > 0:
             ag_copy(g, s - 1).start()
 
+    waiting = list(chain_steps(z.bits, z.chains))
+
+    def advance(place):
+        while waiting and waiting[0][0] <= place:
+            _, g, s = waiting.pop(0)
+            if s >= 0:
+                rs_step(g, s)
+            else:
+                ag_step(g, -1 - s)
+
     filled = 0
 
     def fill(value):
@@ -707,6 +808,7 @@
         for g in range(n_main):
             chain_g[g, z.chain_rows :, :] = jnp.zeros((n * z.chunk - z.chain_rows, LANE), BF16)
     fill(dot(mix_t, ag[...]))
+    advance(0)
 
     dm[...] = dot_bt(ag[0:tp, :], wo[...]).astype(BF16)
     for p in range(z.pairs):
@@ -733,6 +835,7 @@
             [gpr[:, c * hw + p * LANE : c * hw + (p + 1) * LANE] for c in range(3)], axis=1
         )
         fill(dot(n1t[...], joined))
+        advance(1 + p)
 
     head_part = None
     for c in range(3):
@@ -763,6 +866,7 @@
     if used < n * z.small:
         chain_small[used:, :] = jnp.zeros((n * z.small - used, LANE), BF16)
     rs_copy(n_main, 0).start()
+    advance(1 + z.pairs)
 
     for k in range(GROUPS):
         a2a_forward(3, k)
@@ -797,19 +901,13 @@
 
     lax.fori_loop(1, n, stat_go, 0)
 
-    for s in range(nbits):
-        for g in range(n_main + 1):
-            rs_step(g, s)
-
+    advance(LAST)
     block = stat.at[pl.ds(0, n - 1)]
     remote(block, block, st.at[0], st.at[1], sib).wait()
     totals = jnp.sum(stat[...], axis=0)
     count = jnp.sum(jnp.where(iota((8, LANE), 1) == 4, totals, 0.0), axis=-1, keepdims=True)
     o_rms[...] = jnp.sqrt(totals / (count * width))
 
-    for s in range(nbits - 1, -1, -1):
-        for g in range(n_main + 1):
-            ag_step(g, s)
     for g in range(n_main):
         copy = pltpu.make_async_copy(chain_a.at[g], o_red.at[g], osem.at[6 + g])
         copy.start()
@@ -828,11 +926,11 @@
     z,
     i_tok,
     i_gtok,
-    i_x,
-    i_sg,
-    i_hid,
-    i_gp,
-    i_red,
+    x_t,
+    sg,
+    hid_t,
+    gp,
+    red,
     i_small,
     i_bei,
     i_beo,
@@ -853,39 +951,13 @@
     o_wout,
     o_bout,
     o_rms,
-    x_t,
-    sg,
-    hid_t,
-    gp,
-    red,
     wqkv,
     wo,
     win,
     wout,
-    tok_s,
-    gtok_s,
-    isem,
     osem,
 ):
     ne, width, hw = z.experts, z.width, z.hw
-    loads = [
-        pltpu.make_async_copy(i_red.at[g], red.at[g], isem.at[6 + g]) for g in range(z.chains)
-    ]
-    loads += [
-        pltpu.make_async_copy(a, b, isem.at[i])
-        for i, (a, b) in enumerate(
-            (
-                (i_x, x_t),
-                (i_gp, gp),
-                (i_hid, hid_t),
-                (i_sg, sg),
-                (i_tok, tok_s),
-                (i_gtok, gtok_s),
-            )
-        )
-    ]
-    for copy in loads:
-        copy.start()
     stores = []
 
     def store(src, dst, i):
@@ -893,6 +965,8 @@
         copy.start()
         stores.append(copy)
 
+    store(i_tok, o_tok, 0)
+    store(i_gtok, o_gtok, 1)
     for ref, i in ((o_ln1g, 0), (o_ln1b, 1), (o_ln2g, 2), (o_ln2b, 3), (o_bo, 4)):
         ref[...] = i_small[ne + i : ne + i + 1, :].reshape(width)
     o_router[...] = i_small[0:ne, :]
@@ -901,14 +975,11 @@
     o_bout[...] = i_beo[...]
     o_rms[...] = i_rms[0:1, 0:4].reshape(4)
 
-    at, ready = 0, 0
+    at = 0
 
     def take(rows):
-        nonlocal at, ready
+        nonlocal at
         g, row = divmod(at, z.chain_rows)
-        if g == ready:
-            loads[g].wait()
-            ready += 1
         at += rows
         return red[g, row : row + rows, :].astype(F32)
 
@@ -919,22 +990,15 @@
         for c in range(3):
             wqkv[c, :, p * LANE : (p + 1) * LANE] = take(width)
     store(wqkv, o_wqkv, 3)
-    for i in range(2):
-        loads[z.chains + i].wait()
     tiles = z.ff // TILE
     for t in range(tiles):
         cols = slice(t * TILE, (t + 1) * TILE)
         win[:, cols] = dot(x_t[...], gp[:, cols])
         store(win.at[:, cols], o_win.at[0, :, cols], 4 + t)
-    for i in range(2, 4):
-        loads[z.chains + i].wait()
     for t in range(tiles):
         rows = slice(t * TILE, (t + 1) * TILE)
         wout[rows, :] = dot(hid_t[rows, :], sg[...])
         store(wout.at[rows, :], o_wout.at[0, rows, :], 4 + tiles + t)
-    for i, (src, dst) in enumerate(((tok_s, o_tok), (gtok_s, o_gtok))):
-        loads[z.chains + 4 + i].wait()
-        store(src, dst, i)
     for copy in stores:
         copy.wait()
 
@@ -969,10 +1033,24 @@
     any_ = pl.BlockSpec(memory_space=pl.ANY)
     shape = jax.ShapeDtypeStruct
     groups = z.chains
+    kept = pltpu.VMEM if n <= 16 else shape
+    keep = lambda a: pltpu.with_memory_space_constraint(a, pltpu.VMEM) if n <= 16 else a
     V = pltpu.VMEM
     scratch = [
         V((tok, width), BF16),
         V((tok, width), BF16),
+        V((1, tok), jnp.int32),
+        V((2, tok), jnp.int32),
+        V((2, tok), jnp.int32),
+        V((width,), F32),
+        V((width,), F32),
+        V((2, hw), F32),
+        V((width,), F32),
+        V((width,), F32),
+        V((width,), F32),
+        V((z.experts, width), BF16),
+        V((1, ff), F32),
+        V((1, width), F32),
         V((tok, width), BF16),
         V((tok, width), F32),
         V((3, width, hw), BF16),
@@ -1008,10 +1086,12 @@
         V((width, z.slots), BF16),
         V((ff, z.slots), BF16),
         V((z.slots, 1), F32),
-        V((z.slots, 1), F32),
+        V((z.slots, LANE), F32),
         V((2, GROUPS, z.rows, z.half), BF16),
         V((2, GROUPS, z.rows, z.half), BF16),
         V((GROUPS, z.rows, z.half), F32),
+        V((z.rows, width), F32),
+        V((ff, width), BF16),
         V((tp, width), F32),
         V((tk, width), BF16),
         V((tp, hw), BF16),
@@ -1031,7 +1111,7 @@
     scratch += [
         V((groups, n * z.chunk, LANE), BF16),
         V((n * z.small, LANE), BF16),
-        DMA((6,)),
+        DMA((18,)),
         DMA((6 + groups,)),
         DMA((3, GROUPS)),
         DMA((3, GROUPS)),
@@ -1049,27 +1129,29 @@
     outs = pl.pallas_call(
         functools.partial(mega_kernel, z),
         out_shape=(
-            shape((tok, width), BF16),
-            shape((tok, width), F32),
-            shape((width, z.slots), BF16),
-            shape((z.slots, width), BF16),
-            shape((ff, z.slots), BF16),
-            shape((z.slots, ff), BF16),
-            shape((groups, n * z.chunk, LANE), BF16),
-            shape((z.small_rows, width), F32),
-            shape((1, ff), F32),
-            shape((1, width), F32),
-            shape((8, LANE), F32),
+            kept((tok, width), BF16),
+            kept((tok, width), F32),
+            kept((width, z.slots), BF16),
+            kept((z.slots, width), BF16),
+            kept((ff, z.slots), BF16),
+            kept((z.slots, ff), BF16),
+            kept((groups, n * z.chunk, LANE), BF16),
+            kept((z.small_rows, width), F32),
+            kept((1, ff), F32),
+            kept((1, width), F32),
+            kept((8, LANE), F32),
         ),
-        in_specs=[any_] * 2
-        + [vmem] * 5
-        + [any_, vmem, any_, vmem, vmem, vmem, vmem, any_, vmem, any_, vmem],
+        in_specs=[any_] * 18,
         out_specs=(any_,) * 7 + (vmem,) * 4,
         scratch_shapes=scratch,
         compiler_params=pltpu.CompilerParams(
-            collective_id=0, has_side_effects=True, vmem_limit_bytes=60 * 2**20
+            collective_id=0,
+            has_side_effects=True,
+            vmem_limit_bytes=(53 if n <= 16 else 61) * 2**20,
         ),
-    )(
+    )(*(
+        pltpu.with_memory_space_constraint(a, pltpu.HBM)
+        for a in (
         tokens,
         grad_out,
         row(valid_mask),
@@ -1088,8 +1170,8 @@
         b_expert_in,
         w_expert_out[0],
         b_expert_out,
-    )
-    o_tok, o_gtok, o_x, o_sg, o_hid, o_gp, o_red, o_small, o_bei, o_beo, o_rms = outs
+        )
+    ))
     ne = z.experts
     vec = shape((width,), F32)
     last = pl.pallas_call(
@@ -1112,7 +1194,7 @@
             shape((1, width), F32),
             shape((4,), F32),
         ),
-        in_specs=[any_] * 7 + [vmem] * 4,
+        in_specs=[any_] * 2 + [vmem] * 9,
         out_specs=(
             [any_] * 2
             + [vmem] * 2
@@ -1121,22 +1203,14 @@
             + [any_, vmem, any_, vmem, vmem]
         ),
         scratch_shapes=[
-            V((width, z.slots), BF16),
-            V((z.slots, width), BF16),
-            V((ff, z.slots), BF16),
-            V((z.slots, ff), BF16),
-            V((groups, n * z.chunk, LANE), BF16),
             V((3, width, hw), F32),
             V((hw, width), F32),
             V((width, ff), F32),
             V((ff, width), F32),
-            V((tok, width), BF16),
-            V((tok, width), F32),
-            DMA((6 + groups,)),
             DMA((4 + 2 * (ff // TILE),)),
         ],
-        compiler_params=pltpu.CompilerParams(vmem_limit_bytes=60 * 2**20),
-    )(o_tok, o_gtok, o_x, o_sg, o_hid, o_gp, o_red, o_small, o_bei, o_beo, o_rms)
+        compiler_params=pltpu.CompilerParams(vmem_limit_bytes=(30 if n <= 16 else 48) * 2**20),
+    )(*(keep(a) for a in outs))
     return (
         last[0],
         last[1],

time: 118 us -> 109 us (0.924)
  Pallas kernels: 117 us -> 108 us
    pallas_call x1, Pallas kernels: 107 us -> 101 us  [per_device(): pl.pallas_call(functools.partial(mega_kernel, z), out_shape=(kept((tok, w...]
    pallas_call x1, Pallas kernels: 10.6 us -> 6.65 us  [per_device(): pl.pallas_call(functools.partial(last_kernel, z), out_shape=(shape((tok,...]
where the time goes in v4:
time: 109 us; the launch traced here: 108 us
  Pallas kernels  108 us (99%)
    pallas_call x1, Pallas kernels, per_device(): pl.pallas_call(functools.partial(mega_kernel, z), out_shape=(kept((tok, w...  101 us
    pallas_call x1, Pallas kernels, per_device(): pl.pallas_call(functools.partial(last_kernel, z), out_shape=(shape((tok,...  6.65 us

profile of v4, /device:TPU:0, one launch (start us, length us, event | category | flops | bytes accessed | tf_op | source)
XLA Modules:
  0.0 108.5 jit_solution(8042536161550434069)
XLA Ops:
  0.7 101.0 %shard_map.297 = (bf16[197,768]{1,0:T(8,128)(2,1)S(1)}, f32[197,768]{1,0:T(8,128)S(1)}, bf16[768,576]{1,0:T(8,128)(2,1)S(1)}, bf16[576,768]{1,0:T(8,128)(2,1)S(1...) custom-call(bf16[197,768]{1,0:T(8,128)(2,1)} %tokens_hbm.1, ...), custom_call_target="tpu_custom_call" | custom-call | tf_op jit(solution)/shard_map/pallas_call | solution.py:1129
  101.6 6.6 %shard_map.298 = (bf16[197,768]{1,0:T(8,128)(2,1)}, f32[197,768]{1,0:T(8,128)}, f32[768]{0:T(1024)}, f32[768]{0:T(1024)}, f32[3,768,384]{2,1,0:T(8,128)}, /*inde...) custom-call(bf16[197,768]{1,0:T(8,128)(2,1)S(1)} %get-tuple-element., ...), custom_call_target="tpu_custom_call" | custom-call | tf_op jit(solution)/shard_map/pallas_call | solution.py:1177

commit v5 on v4

--- a/solution.py
+++ b/solution.py
@@ -190,11 +190,11 @@
     bout_hbm,
     o_tok,
     o_gtok,
-    o_x,
-    o_sg,
-    o_hid,
-    o_gp,
-    o_red,
+    x_t,
+    sg,
+    hid_t,
+    gp,
+    chain_a,
     o_small,
     o_bei,
     o_beo,
@@ -243,10 +243,6 @@
     gh,
     pre,
     hid,
-    gp,
-    sg,
-    x_t,
-    hid_t,
     gcol_s,
     ggv,
     half_out,
@@ -254,6 +250,7 @@
     half_own,
     whole,
     win_t,
+    wout_t,
     gm,
     ag,
     dm,
@@ -272,7 +269,7 @@
     nbits = len(z.bits)
     chain_r = rest[:nbits]
     small_r = rest[nbits : 2 * nbits]
-    chain_a, small_a, wsem, osem, hs, hr, ss, rs, fs, fr, cs, cr, as_, ar, st = rest[
+    small_a, wsem, osem, hs, hr, ss, rs, fs, fr, cs, cr, as_, ar, st = rest[
         2 * nbits :
     ]
     n = z.n
@@ -545,17 +542,26 @@
         if k < GROUPS - 1:
             a2a_send(1, k)
 
-    for k in range(GROUPS):
-        a2a_forward(0, k)
-    for k in range(GROUPS):
+    def upstream(k):
+        g = group_at(k)
         a2a_take(0, k)
-        assemble(0, group_at(k), u_s)
+        assemble(0, g, u_s)
+        gh[rows_of(g), :] = dot(u_s[rows_of(g), :], wout_t[...])
+
     weights[2].wait()
-    gh[...] = dot_bt(u_s[...], wout[...])
-
-    a2a_send(1, GROUPS - 1)
+    wout_t[...] = jnp.transpose(wout[...])
+    a2a_forward(0, 0)
+    a2a_forward(0, 1)
     weights[3].wait()
     win_t[...] = jnp.transpose(win[...])
+    upstream(0)
+    upstream(1)
+    a2a_forward(0, 2)
+    a2a_forward(0, 3)
+    a2a_send(1, 3)
+    a2a_forward(1, 0)
+    upstream(2)
+    upstream(3)
 
     parts = [(0, z.gm, z.main, 0)] if z.main else []
     parts += [(z.gm, z.gt, z.tail, z.main)]
@@ -627,7 +633,6 @@
         pack(2, g, (half_own[k] + half_in[0, k].astype(F32)).astype(BF16), number)
         a2a_send(2, k)
 
-    a2a_forward(1, 0)
     a2a_forward(1, 1)
     slots_in(0)
     slots_in(1)
@@ -655,12 +660,7 @@
     hid_t[...] = jnp.transpose(hid[...])
     o_beo[...] = jnp.sum(sg[...].astype(F32), axis=0, keepdims=True)
     o_bei[...] = jnp.sum(gp[...].astype(F32), axis=0, keepdims=True)
-    stores = [
-        pltpu.make_async_copy(a, b, osem.at[i])
-        for i, (a, b) in enumerate(((x_t, o_x), (sg, o_sg), (hid_t, o_hid), (gp, o_gp)))
-    ]
-    for copy in stores:
-        copy.start()
+    stores = []
     mix_t = jnp.transpose(mix[...])
 
     flat_id = iota((tp, z.slots), 1)
@@ -855,7 +855,7 @@
     smallf[ne + 1 : ne + 2, :] = jnp.sum(grad_n1, axis=0, keepdims=True)
     back = gm[...] + norm_backward(grad_n1, normal, inverse1, row_of(ln1g_ref))
     gtok_out[...] = back[0:tok, :]
-    copy = pltpu.make_async_copy(gtok_out, o_gtok, osem.at[4])
+    copy = pltpu.make_async_copy(gtok_out, o_gtok, osem.at[0])
     copy.start()
     stores.append(copy)
     used = z.small_rows * (width // LANE)
@@ -876,7 +876,7 @@
     branch = gate[0] * dot(back_one[0], y_s[...]) + gate[1] * dot(back_one[1], y_s[...])
     output = mid[...] + branch
     tok_out[...] = output[0:tok, :].astype(BF16)
-    copy = pltpu.make_async_copy(tok_out, o_tok, osem.at[5])
+    copy = pltpu.make_async_copy(tok_out, o_tok, osem.at[1])
     copy.start()
     stores.append(copy)
     lane_id = iota((1, LANE), 1)
@@ -908,10 +908,6 @@
     count = jnp.sum(jnp.where(iota((8, LANE), 1) == 4, totals, 0.0), axis=-1, keepdims=True)
     o_rms[...] = jnp.sqrt(totals / (count * width))
 
-    for g in range(n_main):
-        copy = pltpu.make_async_copy(chain_a.at[g], o_red.at[g], osem.at[6 + g])
-        copy.start()
-        stores.append(copy)
     for b in range(width // LANE):
         o_small[:, b * LANE : (b + 1) * LANE] = small_a[
             b * z.small_rows : (b + 1) * z.small_rows, :
@@ -1081,10 +1077,6 @@
         V((z.slots, ff), F32),
         V((z.rows, ff), F32),
         V((z.slots, ff), BF16),
-        V((z.slots, ff), BF16),
-        V((z.slots, width), BF16),
-        V((width, z.slots), BF16),
-        V((ff, z.slots), BF16),
         V((z.slots, 1), F32),
         V((z.slots, LANE), F32),
         V((2, GROUPS, z.rows, z.half), BF16),
@@ -1092,6 +1084,7 @@
         V((GROUPS, z.rows, z.half), F32),
         V((z.rows, width), F32),
         V((ff, width), BF16),
+        V((width, ff), BF16),
         V((tp, width), F32),
         V((tk, width), BF16),
         V((tp, hw), BF16),
@@ -1109,10 +1102,9 @@
     scratch += [V((groups, (n >> (s + 1)) * z.chunk, LANE), BF16) for s in range(nbits)]
     scratch += [V(((n >> (s + 1)) * z.small, LANE), BF16) for s in range(nbits)]
     scratch += [
-        V((groups, n * z.chunk, LANE), BF16),
         V((n * z.small, LANE), BF16),
         DMA((18,)),
-        DMA((6 + groups,)),
+        DMA((2,)),
         DMA((3, GROUPS)),
         DMA((3, GROUPS)),
         DMA((4,)),
@@ -1142,12 +1134,12 @@
             kept((8, LANE), F32),
         ),
         in_specs=[any_] * 18,
-        out_specs=(any_,) * 7 + (vmem,) * 4,
+        out_specs=(any_,) * 2 + (vmem,) * 9,
         scratch_shapes=scratch,
         compiler_params=pltpu.CompilerParams(
             collective_id=0,
             has_side_effects=True,
-            vmem_limit_bytes=(53 if n <= 16 else 61) * 2**20,
+            vmem_limit_bytes=(54 if n <= 16 else 61) * 2**20,
         ),
     )(*(
         pltpu.with_memory_space_constraint(a, pltpu.HBM)

time: 109 us -> 105 us (0.963)
  Pallas kernels: 108 us -> 104 us
    pallas_call x1, Pallas kernels: 101 us -> 97.7 us  [per_device(): pl.pallas_call(functools.partial(mega_kernel, z), out_shape=(kept((tok, w...]
where the time goes in v5:
time: 105 us
  Pallas kernels  104 us (99%)
    pallas_call x1, Pallas kernels, per_device(): pl.pallas_call(functools.partial(mega_kernel, z), out_shape=(kept((tok, w...  97.7 us
    pallas_call x1, Pallas kernels, per_device(): pl.pallas_call(functools.partial(last_kernel, z), out_shape=(shape((tok,...  6.65 us

profile of v5, /device:TPU:0, one launch (start us, length us, event | category | flops | bytes accessed | tf_op | source)
XLA Modules:
  0.0 105.2 jit_solution(9872092144675758824)
XLA Ops:
  0.7 97.7 %shard_map.297 = (bf16[197,768]{1,0:T(8,128)(2,1)S(1)}, f32[197,768]{1,0:T(8,128)S(1)}, bf16[768,576]{1,0:T(8,128)(2,1)S(1)}, bf16[576,768]{1,0:T(8,128)(2,1)S(1...) custom-call(bf16[197,768]{1,0:T(8,128)(2,1)} %tokens_hbm.1, ...), custom_call_target="tpu_custom_call" | custom-call | tf_op jit(solution)/shard_map/pallas_call | solution.py:1121
  98.3 6.7 %shard_map.298 = (bf16[197,768]{1,0:T(8,128)(2,1)}, f32[197,768]{1,0:T(8,128)}, f32[768]{0:T(1024)}, f32[768]{0:T(1024)}, f32[3,768,384]{2,1,0:T(8,128)}, /*inde...) custom-call(bf16[197,768]{1,0:T(8,128)(2,1)S(1)} %get-tuple-element., ...), custom_call_target="tpu_custom_call" | custom-call | tf_op jit(solution)/shard_map/pallas_call | solution.py:1169

commit v6 on v5

--- a/solution.py
+++ b/solution.py
@@ -15,36 +15,41 @@
 ROOT = math.sqrt(2.0 / math.pi)
 CUBE = 0.044715
 GROUPS = 4
+QUAD = 4
 LAST = 5
-ORDERS = (
+CHAINS = (
+    (2, 0, 1, 3),
+    (2, 0, 1, 3),
+    (3, 1, 0, 2),
+)
+UNITS = (
+    (3, 2),
+    (2, 3),
+    (3, 2),
+)
+PIECES = (
+    (0, 1, 2, 3),
+    (1, 2, 0, 3),
+    (2, 0, 3, 1),
+    (1, 2, 0, 3),
     (0, 1, 3, 2),
     (1, 3, 0, 2),
-    (2, 0, 1, 3),
-    (0, 2, 1, 3),
-    (1, 0, 3, 2),
-    (2, 1, 0, 3),
-    (3, 0, 1, 2),
-    (2, 1, 0, 3),
-    (1, 0, 2, 3),
+    (0, 1, 2, 3),
     (1, 3, 0, 2),
-    (0, 1, 2, 3),
-    (0, 3, 1, 2),
+    (0, 2, 3, 1),
 )
 STEPS = (
-    (5, 0, 0), (5, 1, 0), (5, 2, 0), (5, 4, 0), (5, 12, 0), (5, 3, 0), (5, 8, 0), (5, 5, 0),
-    (5, 9, 0), (5, 10, 0), (5, 11, 0), (5, 0, 1), (5, 7, 0), (5, 6, 0), (5, 12, 1), (5, 2, 1),
-    (5, 4, 1), (5, 1, 1), (5, 3, 1), (5, 8, 1), (5, 5, 1), (5, 10, 1), (5, 7, 1), (5, 9, 1),
-    (5, 12, 2), (5, 6, 1), (5, 2, 2), (5, 1, 2), (5, 0, 2), (5, 3, 2), (5, 5, 2), (5, 4, 2),
-    (5, 11, 1), (5, 8, 2), (5, 7, 2), (5, 12, 3), (5, 10, 2), (5, 9, 2), (5, 6, 2), (5, 2, 3),
-    (5, 1, 3), (5, 0, 3), (5, 3, 3), (5, 5, 3), (5, 4, 3), (5, 11, 2), (5, 12, -4), (5, 8, 3),
-    (5, 7, 3), (5, 9, 3), (5, 10, 3), (5, 6, 3), (5, 2, -4), (5, 1, -4), (5, 0, -4), (5, 3, -4),
-    (5, 12, -3), (5, 5, -4), (5, 4, -4), (5, 11, 3), (5, 8, -4), (5, 7, -4), (5, 9, -4),
-    (5, 10, -4), (5, 6, -4), (5, 2, -3), (5, 1, -3), (5, 5, -3), (5, 12, -2), (5, 3, -3),
-    (5, 11, -4), (5, 0, -3), (5, 7, -3), (5, 4, -3), (5, 6, -3), (5, 9, -3), (5, 8, -3),
-    (5, 10, -3), (5, 12, -1), (5, 2, -2), (5, 5, -2), (5, 1, -2), (5, 11, -3), (5, 3, -2),
-    (5, 0, -2), (5, 9, -2), (5, 4, -2), (5, 6, -2), (5, 7, -2), (5, 8, -2), (5, 10, -2),
-    (5, 11, -2), (5, 3, -1), (5, 1, -1), (5, 0, -1), (5, 2, -1), (5, 5, -1), (5, 10, -1),
-    (5, 9, -1), (5, 4, -1), (5, 11, -1), (5, 8, -1), (5, 6, -1), (5, 7, -1),
+    (4, 3, 9), (5, 4, 9), (5, 5, 9), (5, 0, 0), (5, 1, 0), (5, 2, 0), (5, 6, 0), (5, 3, 0),
+    (5, 4, 0), (5, 0, 1), (5, 6, 1), (5, 1, 1), (5, 2, 1), (5, 5, 0), (5, 3, 1), (5, 6, 2),
+    (5, 0, 2), (5, 4, 1), (5, 1, 2), (5, 2, 2), (5, 5, -4), (5, 3, -4), (5, 4, -4), (5, 6, 3),
+    (5, 5, 1), (5, 0, 3), (5, 7, -4), (5, 8, -4), (5, 6, -4), (5, 1, 3), (5, 2, 3), (5, 4, -3),
+    (5, 12, -4), (5, 11, -4), (5, 10, -4), (5, 9, -4), (5, 5, -3), (5, 3, -3), (5, 0, -4),
+    (5, 8, -3), (5, 6, -3), (5, 1, -4), (5, 12, -3), (5, 2, -4), (5, 10, -3), (5, 7, -3),
+    (5, 5, -2), (5, 11, -3), (5, 0, -3), (5, 3, -2), (5, 9, -3), (5, 2, -3), (5, 12, -2),
+    (5, 1, -3), (5, 4, -2), (5, 7, -2), (5, 9, -2), (5, 8, -2), (5, 6, -2), (5, 0, -2),
+    (5, 2, -2), (5, 10, -2), (5, 11, -2), (5, 12, -1), (5, 5, -1), (5, 1, -2), (5, 4, -1),
+    (5, 3, -1), (5, 0, -1), (5, 2, -1), (5, 7, -1), (5, 8, -1), (5, 6, -1), (5, 9, -1),
+    (5, 10, -1), (5, 1, -1), (5, 11, -1),
 )
 SEND_ORDER = (0, 2, 1, 3)
 TILE = 256
@@ -138,34 +143,35 @@
         self.rows = self.per * self.cap
         self.slots = n * self.cap
         self.bits = [1 << i for i in range(n.bit_length() - 1)]
-        self.pack_rows = 4 * heads_width * width // LANE
-        self.chains = 12 if n <= 16 else 6
-        self.chain_rows = self.pack_rows // self.chains
+        self.chain_rows = heads_width * width // LANE // 3
         self.chunk = up_to(up_to(self.chain_rows, n) // n, 16)
+        self.share = 3 * LANE // QUAD
+        self.unit_rows = self.share * width // LANE
+        self.unit = up_to(up_to(self.unit_rows, n // QUAD) // (n // QUAD), 16)
+        self.cuts = 3 if self.unit % 48 == 0 else 1
+        self.cut = self.unit // self.cuts
         self.small_rows = up_to(experts + 7, 16)
         self.small = up_to(up_to(self.small_rows * width // LANE, n) // n, 16)
         fits = 0 < self.tail * self.blocks <= 14 and self.gt % 16 == 0
-        fits = fits and self.chain_rows % heads_width == 0 and self.chain_rows % width == 0
+        fits = fits and self.chain_rows % heads_width == 0 and len(self.bits) > 2
         if not fits or experts != n or (1 << len(self.bits)) != n:
             raise ValueError("unsupported sizes")
 
 
-def chain_orders(bits, chains):
-    if len(bits) == 4 and chains == len(ORDERS):
-        return [[bits[i] for i in order] for order in ORDERS]
-    if len(bits) < 3:
-        return [bits] * chains
-    order = ((0, 1, 2), (1, 2, 0), (2, 0, 1), (0, 2, 1), (1, 0, 2), (2, 1, 0))
-    return [[bits[i] for i in order[c % 6]] + bits[3:] for c in range(chains)]
-
-
-def chain_steps(bits, chains):
-    if len(bits) == 4 and chains == len(ORDERS):
-        return STEPS
-    steps = [(LAST, c, s) for s in range(len(bits)) for c in range(chains + 1)]
-    return steps + [
-        (LAST, c, -1 - s) for s in range(len(bits) - 1, -1, -1) for c in range(chains + 1)
-    ]
+def sum_plan(bits, pairs, cuts):
+    if len(bits) == 4 and pairs == 3 and cuts == 3:
+        take = lambda orders: [[bits[i] for i in order] for order in orders]
+        halve = take(CHAINS) + take(UNITS) + [bits]
+        return halve, take(CHAINS) + take(PIECES) + [bits], STEPS
+    rolled = [bits[i:3] + bits[:i] + bits[3:] for i in range(3)]
+    halve = rolled + [bits[2:]] * pairs + [bits]
+    double = rolled + [rolled[i % 3] for i in range(pairs * cuts)] + [bits]
+    steps = [(LAST, 3 + p, 9) for p in range(pairs)]
+    for s in range(len(bits)):
+        steps += [(LAST, g, s) for g, order in enumerate(halve) if s < len(order)]
+    for s in range(len(bits) - 1, -1, -1):
+        steps += [(LAST, g, -1 - s) for g in range(len(double))]
+    return halve, double, steps
 
 
 def mega_kernel(
@@ -194,7 +200,8 @@
     sg,
     hid_t,
     gp,
-    chain_a,
+    red_w,
+    red_u,
     o_small,
     o_bei,
     o_beo,
@@ -222,7 +229,12 @@
     xf,
     normal1,
     n1,
-    n1t,
+    n1q,
+    q_t,
+    k_t,
+    dm_t,
+    gpt,
+    gq,
     upk,
     q_s,
     k_s,
@@ -254,7 +266,6 @@
     gm,
     ag,
     dm,
-    gpr,
     gn_out,
     gn_in,
     smallf,
@@ -262,15 +273,17 @@
     s_msg,
     r_msg,
     f_msg,
-    chain_g,
-    chain_small,
+    sum_w,
+    sum_u,
+    sum_s,
     *rest,
 ):
     nbits = len(z.bits)
-    chain_r = rest[:nbits]
-    small_r = rest[nbits : 2 * nbits]
-    small_a, wsem, osem, hs, hr, ss, rs, fs, fr, cs, cr, as_, ar, st = rest[
-        2 * nbits :
+    from_w = rest[:nbits]
+    from_s = rest[nbits : 2 * nbits]
+    from_u = rest[2 * nbits : 3 * nbits - 2]
+    red_s, wsem, osem, hs, hr, ss, rs, fs, fr, cs, cr, as_, ar, st, qs, us, ur = rest[
+        3 * nbits - 2 :
     ]
     n = z.n
     me, core = lax.axis_index("dp"), lax.axis_index("tensor")
@@ -397,6 +410,29 @@
             per, 16, LANE
         )
 
+    quad_bits = [lax.rem(me, 2), lax.rem(me // 2, 2)]
+
+    def in_quad(q):
+        turned = [b + t * (1 - 2 * b) for b, t in zip(quad_bits, (q % 2, q // 2))]
+        return turned[0] + 2 * turned[1]
+
+    def norm_send():
+        for q in range(1, QUAD):
+            piece = n1q.at[lax.rem(me, QUAD), core, pl.ds(0, tp)]
+            peer = me - lax.rem(me, QUAD) + in_quad(q)
+            remote(piece, piece, qs.at[0], qs.at[1], (peer, core)).start()
+
+    def norm_forward():
+        block = n1q.at[pl.ds(0, QUAD - 1), 0, pl.ds(0, tp)]
+        remote(block, block, qs.at[0], qs.at[1], sib).wait()
+        for q in range(1, QUAD):
+            piece = n1q.at[in_quad(q), core, pl.ds(0, tp)]
+            remote(piece, piece, qs.at[2], qs.at[3], sib).start()
+
+    def norm_take():
+        block = n1q.at[pl.ds(0, QUAD - 1), 0, pl.ds(0, tp)]
+        remote(block, block, qs.at[2], qs.at[3], sib).wait()
+
     gate_row = 14
 
     for copy in small_in:
@@ -463,6 +499,11 @@
     normal1[...] = normal
     n1[tp:, :] = jnp.zeros((tk - tp, width), BF16)
     n1[0:tp, :] = (normal * row_of(ln1g_ref) + row_of(ln1b_ref)).astype(BF16)
+    place_in = lax.rem(me, QUAD)
+    for h in range(2):
+        n1q[place_in, h] = n1[:, h * half : (h + 1) * half]
+        for m in range(QUAD):
+            n1q[m, h, tp:, :] = jnp.zeros((tk - tp, half), BF16)
 
     pl.semaphore_wait(barrier, n)
     for k in SEND_ORDER:
@@ -496,7 +537,10 @@
     part[...] = dot(mix[0:tp, :], wo[...])
     swap = remote(part, part_in, hs.at[2, 0], hr.at[2, 0], sib)
     swap.start()
-    n1t[...] = jnp.transpose(n1[...])
+    for p in range(z.pairs):
+        lanes = slice(p * LANE, (p + 1) * LANE)
+        q_t[p] = jnp.transpose(q_s[:, lanes])
+        k_t[p] = jnp.transpose(k_s[:, lanes])
     swap.wait()
 
     attention = part[...] + part_in[...] + row_of(bo_ref)
@@ -559,6 +603,7 @@
     a2a_forward(0, 2)
     a2a_forward(0, 3)
     a2a_send(1, 3)
+    norm_send()
     a2a_forward(1, 0)
     upstream(2)
     upstream(3)
@@ -662,6 +707,7 @@
     o_bei[...] = jnp.sum(gp[...].astype(F32), axis=0, keepdims=True)
     stores = []
     mix_t = jnp.transpose(mix[...])
+    norm_forward()
 
     flat_id = iota((tp, z.slots), 1)
     back_one = [one(flat_id == f) for f in flat_col]
@@ -716,138 +762,185 @@
     ag[0:tp, :] = gm[...].astype(BF16)
     smallf[ne + 4 : ne + 5, :] = jnp.sum(ag[...].astype(F32), axis=0, keepdims=True)
 
-    groups = []
-    for order in chain_orders(z.bits, z.chains) + [z.bits]:
-        start, size, steps = 0, n, []
+    halve, double, waiting = sum_plan(z.bits, z.pairs, z.cuts)
+    waiting = list(waiting)
+    n_main, n_cut = len(halve) - 1, len(double) - 1
+
+    def walk(order):
+        start, size, steps = 0, 1 << len(order), []
         for b in order:
             bit = lax.rem(me // b, 2)
             peer = me + b * (1 - 2 * bit)
             size = size // 2
             steps.append((peer, start + (1 - bit) * size, start + bit * size, size))
             start = start + bit * size
-        groups.append((steps, start))
-    n_main = len(groups) - 1
-
-    def chain_of(g):
+        return steps, start
+
+    halving, doubling = [walk(order) for order in halve], [walk(order) for order in double]
+
+    def sum_of(g):
+        if g < 3:
+            return sum_w.at[g], [r.at[g] for r in from_w], z.chunk, [g]
         if g < n_main:
-            return chain_g.at[g], [r.at[g] for r in chain_r], chain_a.at[g], z.chunk
-        return chain_small, list(small_r), small_a, z.small
+            pieces = [3 + (g - 3) * z.cuts + i for i in range(z.cuts)]
+            return sum_u.at[g - 3], [r.at[g - 3] for r in from_u], z.unit, pieces
+        return sum_s, list(from_s), z.small, [n_cut]
+
+    def piece_of(i):
+        if i < 3:
+            return red_w.at[i], z.chunk
+        if i < n_cut:
+            return red_u.at[i - 3], z.cut
+        return red_s, z.small
 
     def region(ref, at, count, rows):
         return ref.at[pl.ds(pl.multiple_of(at * rows, 16), count * rows)]
 
     def rs_copy(g, s):
-        src, bufs, _, rows = chain_of(g)
-        peer, give, _, size = groups[g][0][s]
+        src, bufs, rows, _ = sum_of(g)
+        peer, give, _, size = halving[g][0][s]
         return remote(
             region(src, give, size, rows), bufs[s], cs.at[g], cr.at[g, s], (peer, core)
         )
 
-    def rs_add(g, s, at, count, dst):
-        src, bufs, _, rows = chain_of(g)
-        keep = groups[g][0][s][2]
+    def rs_add(g, s, at, count):
+        src, bufs, rows, _ = sum_of(g)
+        keep = halving[g][0][s][2]
 
         def go(i, carry):
             here = pl.ds(pl.multiple_of((at + i) * rows, 16), rows)
             there = pl.ds(pl.multiple_of((at + i - keep) * rows, 16), rows)
-            dst[here, :] = (src[here, :].astype(F32) + bufs[s][there, :].astype(F32)).astype(BF16)
+            src[here, :] = (src[here, :].astype(F32) + bufs[s][there, :].astype(F32)).astype(BF16)
             return carry
 
         lax.fori_loop(0, count, go, 0, unroll=2 if count % 2 == 0 else 1)
 
     def rs_step(g, s):
-        src, _, out, _ = chain_of(g)
+        src, bufs, rows, pieces = sum_of(g)
+        steps, last = halving[g]
         rs_copy(g, s).wait()
-        if s + 1 < nbits:
-            _, give, keep, size = groups[g][0][s + 1]
-            rs_add(g, s, give, size, src)
+        if s + 1 < len(steps):
+            _, give, keep, size = steps[s + 1]
+            rs_add(g, s, give, size)
             rs_copy(g, s + 1).start()
-            rs_add(g, s, keep, size, src)
-        else:
-            rs_add(g, s, groups[g][1], 1, out)
-            ag_copy(g, s).start()
+            rs_add(g, s, keep, size)
+            return
+        first = 0
+        for i in pieces:
+            out, count = piece_of(i)
+            here = pl.ds(pl.multiple_of(last * rows + first, 16), count)
+            goal = pl.ds(pl.multiple_of(doubling[i][1] * count, 16), count)
+            out[goal, :] = (
+                src[here, :].astype(F32) + bufs[s][first : first + count, :].astype(F32)
+            ).astype(BF16)
+            ag_copy(i, nbits - 1).start()
+            first += count
 
     def ag_copy(g, s):
-        _, _, out, rows = chain_of(g)
-        peer, _, keep, size = groups[g][0][s]
+        out, rows = piece_of(g)
+        peer, _, keep, size = doubling[g][0][s]
         piece = region(out, keep, size, rows)
         return remote(piece, piece, as_.at[g], ar.at[g, s], (peer, core))
 
     def ag_step(g, s):
-        _, _, out, rows = chain_of(g)
-        peer, give, _, size = groups[g][0][s]
+        out, rows = piece_of(g)
+        peer, give, _, size = doubling[g][0][s]
         ag_copy(g, s).wait_send()
         piece = region(out, give, size, rows)
         remote(piece, piece, as_.at[g], ar.at[g, s], (peer, core)).wait_recv()
         if s > 0:
             ag_copy(g, s - 1).start()
 
-    waiting = list(chain_steps(z.bits, z.chains))
+    def share_of(p, m):
+        return gpt.at[p, pl.ds(pl.multiple_of(m * z.share, 16), z.share)]
+
+    def quad_send(p):
+        here = lax.rem(me, QUAD)
+        for q in range(1, QUAD):
+            m = in_quad(q)
+            remote(
+                share_of(p, m), gq.at[p, here], us.at[p], ur.at[p], (me - here + m, core)
+            ).start()
+        gq[p, here] = gpt[p, pl.ds(pl.multiple_of(here * z.share, 16), z.share), :]
+
+    def quad_step(p):
+        block = gq.at[p, pl.ds(0, QUAD - 1)]
+        remote(block, block, us.at[p], ur.at[p], sib).wait()
+        left = jnp.concatenate([gq[p, m] for m in range(QUAD)], axis=1)
+        row = 0
+        for h in range(2):
+            value = dot(left, n1q[:, h].reshape(QUAD * tk, half)).astype(BF16)
+            for b in range(z.blocks):
+                sum_u[p, row : row + z.share, :] = value[:, b * LANE : (b + 1) * LANE]
+                row += z.share
+        if z.unit_rows < n // QUAD * z.unit:
+            sum_u[p, z.unit_rows :, :] = jnp.zeros((n // QUAD * z.unit - z.unit_rows, LANE), BF16)
+        rs_copy(3 + p, 0).start()
 
     def advance(place):
         while waiting and waiting[0][0] <= place:
             _, g, s = waiting.pop(0)
-            if s >= 0:
+            if s == 9:
+                quad_step(g - 3)
+            elif s >= 0:
                 rs_step(g, s)
             else:
                 ag_step(g, -1 - s)
 
-    filled = 0
-
-    def fill(value):
-        nonlocal filled
-        rows = value.shape[0]
-        for b in range(value.shape[1] // LANE):
-            g, at = divmod(filled, z.chain_rows)
-            chain_g[g, at : at + rows, :] = value[:, b * LANE : (b + 1) * LANE].astype(BF16)
-            filled += rows
-            if filled == (g + 1) * z.chain_rows:
-                rs_copy(g, 0).start()
-
-    if z.chain_rows < n * z.chunk:
-        for g in range(n_main):
-            chain_g[g, z.chain_rows :, :] = jnp.zeros((n * z.chunk - z.chain_rows, LANE), BF16)
-    fill(dot(mix_t, ag[...]))
+    grad_wo = dot(mix_t, ag[...])
+    each = z.chain_rows // hw
+    for g in range(3):
+        for i in range(each):
+            b = g * each + i
+            sum_w[g, i * hw : (i + 1) * hw, :] = grad_wo[:, b * LANE : (b + 1) * LANE].astype(BF16)
+        if z.chain_rows < n * z.chunk:
+            sum_w[g, z.chain_rows :, :] = jnp.zeros((n * z.chunk - z.chain_rows, LANE), BF16)
+        rs_copy(g, 0).start()
+    norm_take()
     advance(0)
 
     dm[...] = dot_bt(ag[0:tp, :], wo[...]).astype(BF16)
+    dm_t[...] = dot_bt(wo[...], ag[...]).astype(BF16)
+    ones = jnp.ones((8, tk), BF16)
     for p in range(z.pairs):
         lanes = slice(p * LANE, (p + 1) * LANE)
-        qp, kp, vp, dp = q_s[0:tp, lanes], k_s[:, lanes], v_s[:, lanes], dm[:, lanes]
+        vp, dp = v_s[:, lanes], dm[:, lanes]
         dq, dk, dv = [], [], []
         for h in range(2):
+            rows = slice(h * HEAD, (h + 1) * HEAD)
             prob = probs[2 * p + h]
             gprob = dot_bt(dp * head_mask[h], vp)
             inner = jnp.sum(prob * gprob, axis=-1, keepdims=True)
             gs = (prob * (gprob - inner)).astype(BF16)
-            dq.append(dot(gs, kp))
-            dk.append(dot_at(gs, qp))
-            dv.append(dot_at(prob.astype(BF16), dp))
+            dq.append(dot_bt(k_t[p, rows, :], gs))
+            dk.append(dot(q_t[p, rows, 0:tp], gs))
+            dv.append(
+                dot(dm_t[p * LANE + h * HEAD : p * LANE + (h + 1) * HEAD, 0:tp], prob.astype(BF16))
+            )
         for c, (pair, scale) in enumerate(((dq, score_scale), (dk, score_scale), (dv, 1.0))):
-            value = (jnp.where(low_lane, pair[0], pair[1]) * scale).astype(BF16)
-            at = slice(c * hw + p * LANE, c * hw + (p + 1) * LANE)
+            value = (jnp.concatenate(pair, axis=0) * scale).astype(BF16)
+            at = slice(c * LANE, (c + 1) * LANE)
             if c == 0:
-                gpr[0:tp, at] = value
-                gpr[tp:, at] = jnp.zeros((tk - tp, LANE), BF16)
+                gpt[p, at, LANE:] = jnp.zeros((LANE, tk - LANE), BF16)
+                gpt[p, at, 0:tp] = value
             else:
-                gpr[:, at] = value
-        joined = jnp.concatenate(
-            [gpr[:, c * hw + p * LANE : c * hw + (p + 1) * LANE] for c in range(3)], axis=1
-        )
-        fill(dot(n1t[...], joined))
+                gpt[p, at, :] = value
+        quad_send(p)
+        line = dot_bt(ones, gpt[p])
+        smallf[ne + 5 : ne + 6, lanes] = line[0:1, 0:LANE]
+        smallf[ne + 6 : ne + 7, lanes] = line[0:1, 2 * LANE : 3 * LANE]
         advance(1 + p)
 
     head_part = None
     for c in range(3):
-        piece = dot_bt(gpr[0:tp, c * hw : (c + 1) * hw], wqkv[c])
+        joined = jnp.concatenate(
+            [gpt[p, c * LANE : (c + 1) * LANE, :] for p in range(z.pairs)], axis=0
+        )
+        piece = dot(wqkv[c], joined)
         head_part = piece if head_part is None else head_part + piece
-    gn_out[...] = head_part.astype(BF16)
+    gn_out[...] = jnp.transpose(head_part.astype(BF16))[0:tp, :]
     swap = remote(gn_out, gn_in, hs.at[2, 1], hr.at[2, 1], sib)
     swap.start()
-    smallf[ne + 5 : ne + 6, 0:hw] = jnp.sum(gpr[:, 0:hw].astype(F32), axis=0, keepdims=True)
-    smallf[ne + 6 : ne + 7, 0:hw] = jnp.sum(
-        gpr[:, 2 * hw : 3 * hw].astype(F32), axis=0, keepdims=True
-    )
     swap.wait()
     grad_n1 = gn_out[...].astype(F32) + gn_in[...].astype(F32)
     normal = normal1[...]
@@ -860,11 +953,11 @@
     stores.append(copy)
     used = z.small_rows * (width // LANE)
     for b in range(width // LANE):
-        chain_small[b * z.small_rows : (b + 1) * z.small_rows, :] = smallf[
+        sum_s[b * z.small_rows : (b + 1) * z.small_rows, :] = smallf[
             :, b * LANE : (b + 1) * LANE
         ].astype(BF16)
     if used < n * z.small:
-        chain_small[used:, :] = jnp.zeros((n * z.small - used, LANE), BF16)
+        sum_s[used:, :] = jnp.zeros((n * z.small - used, LANE), BF16)
     rs_copy(n_main, 0).start()
     advance(1 + z.pairs)
 
@@ -909,7 +1002,7 @@
     o_rms[...] = jnp.sqrt(totals / (count * width))
 
     for b in range(width // LANE):
-        o_small[:, b * LANE : (b + 1) * LANE] = small_a[
+        o_small[:, b * LANE : (b + 1) * LANE] = red_s[
             b * z.small_rows : (b + 1) * z.small_rows, :
         ].astype(F32)
     for i in range(4):
@@ -926,7 +1019,8 @@
     sg,
     hid_t,
     gp,
-    red,
+    red_w,
+    red_u,
     i_small,
     i_bei,
     i_beo,
@@ -951,6 +1045,7 @@
     wo,
     win,
     wout,
+    back_t,
     osem,
 ):
     ne, width, hw = z.experts, z.width, z.hw
@@ -971,26 +1066,39 @@
     o_bout[...] = i_beo[...]
     o_rms[...] = i_rms[0:1, 0:4].reshape(4)
 
-    at = 0
-
-    def take(rows):
-        nonlocal at
-        g, row = divmod(at, z.chain_rows)
-        at += rows
-        return red[g, row : row + rows, :].astype(F32)
-
+    each = z.chain_rows // hw
     for b in range(width // LANE):
-        wo[:, b * LANE : (b + 1) * LANE] = take(hw)
+        rows = slice(b % each * hw, (b % each + 1) * hw)
+        wo[:, b * LANE : (b + 1) * LANE] = red_w[b // each, rows, :].astype(F32)
     store(wo, o_wo, 2)
-    for p in range(z.pairs):
-        for c in range(3):
-            wqkv[c, :, p * LANE : (p + 1) * LANE] = take(width)
-    store(wqkv, o_wqkv, 3)
     tiles = z.ff // TILE
     for t in range(tiles):
         cols = slice(t * TILE, (t + 1) * TILE)
         win[:, cols] = dot(x_t[...], gp[:, cols])
         store(win.at[:, cols], o_win.at[0, :, cols], 4 + t)
+    halve, double, _ = sum_plan(z.bits, z.pairs, z.cuts)
+    nbits = len(z.bits)
+    piece = math.gcd(z.cut, z.share)
+    for p in range(z.pairs):
+        for i in range(z.cuts * z.n):
+            i, c = divmod(i, z.n)
+            order = double[3 + p * z.cuts + i]
+            device = sum(b for k, b in enumerate(order) if c >> (nbits - 1 - k) & 1)
+            q = 0
+            for b in halve[3 + p]:
+                q = 2 * q + (device // b) % 2
+            for t in range(0, z.cut, piece):
+                row = q * z.unit + i * z.cut + t
+                if row < z.unit_rows:
+                    b, j = divmod(row, z.share)
+                    goal = device % QUAD * z.share + j
+                    back_t[goal : goal + piece, b * LANE : (b + 1) * LANE] = red_u[
+                        p * z.cuts + i, c * z.cut + t : c * z.cut + t + piece, :
+                    ]
+        for c in range(3):
+            value = jnp.transpose(back_t[c * LANE : (c + 1) * LANE, :])
+            wqkv[c, :, p * LANE : (p + 1) * LANE] = value.astype(F32)
+    store(wqkv, o_wqkv, 3)
     for t in range(tiles):
         rows = slice(t * TILE, (t + 1) * TILE)
         wout[rows, :] = dot(hid_t[rows, :], sg[...])
@@ -1028,7 +1136,8 @@
     vmem = pl.BlockSpec(memory_space=pltpu.VMEM)
     any_ = pl.BlockSpec(memory_space=pl.ANY)
     shape = jax.ShapeDtypeStruct
-    groups = z.chains
+    groups = 4 + z.pairs
+    pieces = 4 + z.pairs * z.cuts
     kept = pltpu.VMEM if n <= 16 else shape
     keep = lambda a: pltpu.with_memory_space_constraint(a, pltpu.VMEM) if n <= 16 else a
     V = pltpu.VMEM
@@ -1056,7 +1165,12 @@
         V((tp, width), F32),
         V((tp, width), F32),
         V((tk, width), BF16),
-        V((width, tk), BF16),
+        V((QUAD, 2, tk, z.half), BF16),
+        V((z.pairs, LANE, tk), BF16),
+        V((z.pairs, LANE, tk), BF16),
+        V((hw, tk), BF16),
+        V((z.pairs, 3 * LANE, tk), BF16),
+        V((z.pairs, QUAD, z.share, tk), BF16),
         V((tk, width), BF16),
         V((tk, hw), BF16),
         V((tk, hw), BF16),
@@ -1088,7 +1202,6 @@
         V((tp, width), F32),
         V((tk, width), BF16),
         V((tp, hw), BF16),
-        V((tk, 3 * hw), BF16),
         V((tp, width), BF16),
         V((tp, width), BF16),
         V((z.small_rows, width), F32),
@@ -1096,11 +1209,15 @@
         V((4, n, z.msg, LANE), BF16),
         V((4, n, z.msg, LANE), BF16),
         V((4, n, z.msg, LANE), BF16),
-        V((groups, n * z.chunk, LANE), BF16),
+        V((3, n * z.chunk, LANE), BF16),
+        V((z.pairs, n // QUAD * z.unit, LANE), BF16),
         V((n * z.small, LANE), BF16),
     ]
-    scratch += [V((groups, (n >> (s + 1)) * z.chunk, LANE), BF16) for s in range(nbits)]
+    scratch += [V((3, (n >> (s + 1)) * z.chunk, LANE), BF16) for s in range(nbits)]
     scratch += [V(((n >> (s + 1)) * z.small, LANE), BF16) for s in range(nbits)]
+    scratch += [
+        V((z.pairs, (n // QUAD >> (s + 1)) * z.unit, LANE), BF16) for s in range(nbits - 2)
+    ]
     scratch += [
         V((n * z.small, LANE), BF16),
         DMA((18,)),
@@ -1111,11 +1228,14 @@
         DMA((4, GROUPS)),
         DMA((4,)),
         DMA((4, GROUPS)),
-        DMA((groups + 1,)),
-        DMA((groups + 1, nbits)),
-        DMA((groups + 1,)),
-        DMA((groups + 1, nbits)),
+        DMA((groups,)),
+        DMA((groups, nbits)),
+        DMA((pieces,)),
+        DMA((pieces, nbits)),
         DMA((2,)),
+        DMA((4,)),
+        DMA((z.pairs,)),
+        DMA((z.pairs,)),
     ]
     row = lambda v: v.reshape(1, -1)
     outs = pl.pallas_call(
@@ -1127,14 +1247,15 @@
             kept((z.slots, width), BF16),
             kept((ff, z.slots), BF16),
             kept((z.slots, ff), BF16),
-            kept((groups, n * z.chunk, LANE), BF16),
+            kept((3, n * z.chunk, LANE), BF16),
+            kept((z.pairs * z.cuts, n * z.cut, LANE), BF16),
             kept((z.small_rows, width), F32),
             kept((1, ff), F32),
             kept((1, width), F32),
             kept((8, LANE), F32),
         ),
         in_specs=[any_] * 18,
-        out_specs=(any_,) * 2 + (vmem,) * 9,
+        out_specs=(any_,) * 2 + (vmem,) * 10,
         scratch_shapes=scratch,
         compiler_params=pltpu.CompilerParams(
             collective_id=0,
@@ -1186,7 +1307,7 @@
             shape((1, width), F32),
             shape((4,), F32),
         ),
-        in_specs=[any_] * 2 + [vmem] * 9,
+        in_specs=[any_] * 2 + [vmem] * 10,
         out_specs=(
             [any_] * 2
             + [vmem] * 2
@@ -1199,6 +1320,7 @@
             V((hw, width), F32),
             V((width, ff), F32),
             V((ff, width), F32),
+            V((3 * LANE, width), BF16),
             DMA((4 + 2 * (ff // TILE),)),
         ],
         compiler_params=pltpu.CompilerParams(vmem_limit_bytes=(30 if n <= 16 else 48) * 2**20),

time: 105 us -> 102 us (0.971)
  Pallas kernels: 104 us -> 101 us
    pallas_call x1, Pallas kernels: 97.7 us -> 93.9 us  [per_device(): pl.pallas_call(functools.partial(mega_kernel, z), out_shape=(kept((tok, w...]
where the time goes in v6:
time: 102 us
  Pallas kernels  101 us (99%)
    pallas_call x1, Pallas kernels, per_device(): pl.pallas_call(functools.partial(mega_kernel, z), out_shape=(kept((tok, w...  93.9 us
    pallas_call x1, Pallas kernels, per_device(): pl.pallas_call(functools.partial(last_kernel, z), out_shape=(shape((tok,...  6.86 us

profile of v6, /device:TPU:0, one launch (start us, length us, event | category | flops | bytes accessed | tf_op | source)
XLA Modules:
  0.0 101.6 jit_solution(3436420615586141728)
XLA Ops:
  0.7 93.9 %shard_map.297 = (bf16[197,768]{1,0:T(8,128)(2,1)S(1)}, f32[197,768]{1,0:T(8,128)S(1)}, bf16[768,576]{1,0:T(8,128)(2,1)S(1)}, bf16[576,768]{1,0:T(8,128)(2,1)S(1...) custom-call(bf16[197,768]{1,0:T(8,128)(2,1)} %tokens_hbm.1, ...), custom_call_target="tpu_custom_call" | custom-call | tf_op jit(solution)/shard_map/pallas_call | solution.py:1241
  94.5 6.9 %shard_map.298 = (bf16[197,768]{1,0:T(8,128)(2,1)}, f32[197,768]{1,0:T(8,128)}, f32[768]{0:T(1024)}, f32[768]{0:T(1024)}, f32[3,768,384]{2,1,0:T(8,128)}, /*inde...) custom-call(bf16[197,768]{1,0:T(8,128)(2,1)S(1)} %get-tuple-element., ...), custom_call_target="tpu_custom_call" | custom-call | tf_op jit(solution)/shard_map/pallas_call | solution.py:1290

commit v7 on v6

--- a/solution.py
+++ b/solution.py
@@ -543,14 +543,19 @@
         k_t[p] = jnp.transpose(k_s[:, lanes])
     swap.wait()
 
-    attention = part[...] + part_in[...] + row_of(bo_ref)
-    stat_attn = jnp.sum(keep_col * attention * attention)
-    middle = xf[...] + attention
-    mid[...] = middle
-    normal, inverse2 = norm_parts(middle)
-    normal2[...] = normal
+    strips = [slice(r, r + 16) for r in range(0, tp, 16)]
     n2[tp:, :] = jnp.zeros((tk - tp, width), BF16)
-    n2[0:tp, :] = (normal * row_of(ln2g_ref) + row_of(ln2b_ref)).astype(BF16)
+    inverses, squares = [], jnp.zeros((16, width), F32)
+    for strip in strips:
+        attention = part[strip, :] + part_in[strip, :] + row_of(bo_ref)
+        squares = squares + keep_col[strip, :] * attention * attention
+        middle = xf[strip, :] + attention
+        mid[strip, :] = middle
+        normal, inverse = norm_parts(middle)
+        inverses.append(inverse)
+        normal2[strip, :] = normal
+        n2[strip, :] = (normal * row_of(ln2g_ref) + row_of(ln2b_ref)).astype(BF16)
+    stat_attn = jnp.sum(squares)
     logits = dot_bt(router_ref[...], n2[...])
     expert_id = iota((z.experts, tk), 0)
     chosen = [
@@ -754,13 +759,20 @@
     smallf[...] = jnp.zeros(smallf.shape, F32)
     ne = z.experts
     smallf[0:ne, :] = grad_router[0:ne, :]
-    normal = normal2[...]
-    smallf[ne + 2 : ne + 3, :] = jnp.sum(grad_n2 * normal, axis=0, keepdims=True)
-    smallf[ne + 3 : ne + 4, :] = jnp.sum(grad_n2, axis=0, keepdims=True)
-    gm[...] = upk[0:tp, :].astype(F32) + norm_backward(grad_n2, normal, inverse2, row_of(ln2g_ref))
+    gains, shifts, lows = [jnp.zeros((16, width), F32) for _ in range(3)]
+    for strip, inverse in zip(strips, inverses):
+        part_grad, normal = grad_n2[strip, :], normal2[strip, :]
+        gains, shifts = gains + part_grad * normal, shifts + part_grad
+        value = upk[strip, :].astype(F32) + norm_backward(
+            part_grad, normal, inverse, row_of(ln2g_ref)
+        )
+        gm[strip, :] = value
+        low = value.astype(BF16)
+        ag[strip, :] = low
+        lows = lows + low.astype(F32)
+    for i, sums in ((2, gains), (3, shifts), (4, lows)):
+        smallf[ne + i : ne + i + 1, :] = jnp.sum(sums, axis=0, keepdims=True)
     ag[tp:, :] = jnp.zeros((tk - tp, width), BF16)
-    ag[0:tp, :] = gm[...].astype(BF16)
-    smallf[ne + 4 : ne + 5, :] = jnp.sum(ag[...].astype(F32), axis=0, keepdims=True)
 
     halve, double, waiting = sum_plan(z.bits, z.pairs, z.cuts)
     waiting = list(waiting)

time: 102 us -> 102 us (level)
  no operation moved by 1% of the time
where the time goes in v7:
time: 102 us
  Pallas kernels  101 us (99%)
    pallas_call x1, Pallas kernels, per_device(): pl.pallas_call(functools.partial(mega_kernel, z), out_shape=(kept((tok, w...  93.9 us
    pallas_call x1, Pallas kernels, per_device(): pl.pallas_call(functools.partial(last_kernel, z), out_shape=(shape((tok,...  6.86 us

profile of v7, /device:TPU:0, one launch (start us, length us, event | category | flops | bytes accessed | tf_op | source)
XLA Modules:
  0.0 101.6 jit_solution(13904206065657541607)
XLA Ops:
  0.7 93.9 %shard_map.297 = (bf16[197,768]{1,0:T(8,128)(2,1)S(1)}, f32[197,768]{1,0:T(8,128)S(1)}, bf16[768,576]{1,0:T(8,128)(2,1)S(1)}, bf16[576,768]{1,0:T(8,128)(2,1)S(1...) custom-call(bf16[197,768]{1,0:T(8,128)(2,1)} %tokens_hbm.1, ...), custom_call_target="tpu_custom_call" | custom-call | tf_op jit(solution)/shard_map/pallas_call | solution.py:1253
  94.5 6.9 %shard_map.298 = (bf16[197,768]{1,0:T(8,128)(2,1)}, f32[197,768]{1,0:T(8,128)}, f32[768]{0:T(1024)}, f32[768]{0:T(1024)}, f32[3,768,384]{2,1,0:T(8,128)}, /*inde...) custom-call(bf16[197,768]{1,0:T(8,128)(2,1)S(1)} %get-tuple-element., ...), custom_call_target="tpu_custom_call" | custom-call | tf_op jit(solution)/shard_map/pallas_call | solution.py:1302
